TPU v7x, 512 devices: a whole 4x4x16 slice. The times are simulated.
512 devices in a mesh: ctx: 64 (over z, y), kv: 8 (over x, core).
Axes of the slice: x: 4, y: 4, z: 16, core: 2. Of those that a mesh axis runs over, the one named last changes fastest.
Arguments:
- cache_keys: bfloat16 [32768, 1024], P('ctx', 'kv'), may hold values from -6 to 6
- cache_values: bfloat16 [32768, 1024], P('ctx', 'kv'), may hold values from -6 to 6
- importance: bfloat16 [8, 32768], P('kv', 'ctx'), may hold values from 0.099609375 to 10
- assignment: int32 [32768], P('ctx'), may hold values from 0 to 32767, as said below
- queries: bfloat16 [128, 8192], P(None, 'kv'), may hold values from -40 to 40
Outputs:
- merged_keys: bfloat16 [32768, 1024], P('ctx', 'kv')
- merged_values: bfloat16 [32768, 1024], P('ctx', 'kv')
- attended: bfloat16 [128, 8192], P(None, 'kv')
Inputs may be any that keep to these rules, and one draw needn't show every extreme that they name: `assignment`: each entry is the row itself (the row is kept) or a kept row other than itself (the row is evicted and merges into it). The first row of every aligned block of 128 rows is kept and no row merges into it; in every aligned block between a quarter and five twelfths of the rows, rounded down, are evicted. A shard is an aligned block of 512 rows; shard numbers are taken modulo the number of shards. Of the rows of one shard, at most 16 merge into rows of the shard before it and at most 16 into rows of the shard after it, and into rows of every other shard at least 0 and at most 1. The bounds 16 and 1 are reached in every draw.
All inputs are finite; a program needn't handle non-finite values.
Results may differ from a plain program's by a relative error of at most 0.0055.
Values may be sent and summed in bfloat16 or wider, within the bound.
No kernel may reach another device: no remote copies, remote signals or barrier semaphores. Data moves between devices by JAX's collectives and lax.ppermute only.
A program may use at most 192 MiB of HBM per device.

v0:
```python
import jax
import jax.numpy as jnp
from jax import lax
from jax.sharding import PartitionSpec as P

BLOCK = 128
NEAR = 16


def bucket_ranks(bucket, bucket_count):
    row_count = bucket.shape[0]
    block_count = row_count // BLOCK
    labels = jnp.arange(bucket_count, dtype=jnp.int32)
    onehot = (bucket.reshape(block_count, 1, BLOCK) == labels[None, :, None]).astype(jnp.bfloat16)
    earlier = (jnp.arange(BLOCK)[:, None] < jnp.arange(BLOCK)[None, :]).astype(jnp.bfloat16)
    within = jnp.einsum("bnr,rs->bns", onehot, earlier, preferred_element_type=jnp.float32)
    widened = onehot.astype(jnp.float32)
    totals = jnp.sum(widened, axis=2)
    offsets = jnp.cumsum(totals, axis=0) - totals
    ranked = jnp.sum(widened * (within + offsets[:, :, None]), axis=1)
    return ranked.reshape(row_count).astype(jnp.int32)


def pack_rows(payload, slot_index, capacity):
    return tuple(
        (
            jnp.zeros((capacity,) + member.shape[1:], member.dtype)
            .at[slot_index]
            .set(member, mode="drop")
            for member in payload
        )
    )


def fold_peers(members, peers):
    return tuple(
        (member.reshape((peers, member.shape[0] // peers) + member.shape[1:]) for member in members)
    )


def unfold_peers(members):
    return tuple(
        (
            member.reshape((member.shape[0] * member.shape[1],) + member.shape[2:])
            for member in members
        )
    )


def split_target(target_rows):
    high_part = (target_rows // 128).astype(jnp.bfloat16)
    low_part = (target_rows % 128).astype(jnp.bfloat16)
    return (high_part, low_part)


def add_rows(partial_sums, arrived):
    numer_keys, numer_values, denominator = partial_sums
    key_rows, value_rows, weight_rows, high_part, low_part = arrived
    target_rows = high_part.astype(jnp.int32) * 128 + low_part.astype(jnp.int32)
    scale_rows = weight_rows.astype(jnp.float32)
    numer_keys = numer_keys.at[target_rows].add(
        key_rows.astype(jnp.float32) * scale_rows[:, None], mode="drop"
    )
    numer_values = numer_values.at[target_rows].add(
        value_rows.astype(jnp.float32) * scale_rows[:, None], mode="drop"
    )
    denominator = denominator.at[target_rows].add(scale_rows, mode="drop")
    return (numer_keys, numer_values, denominator)


def per_device(cache_keys, cache_values, importance, assignment, queries):
    row_count = cache_keys.shape[0]
    row_width = cache_keys.shape[1]
    kv_local = importance.shape[0]
    head_dim = row_width // kv_local
    shards = lax.axis_size("ctx")
    shard_index = lax.axis_index("ctx")
    row_weight = lax.psum(jnp.sum(importance.astype(jnp.float32), axis=0), "kv").astype(
        jnp.bfloat16
    )
    own_rows = shard_index * row_count + jnp.arange(row_count, dtype=jnp.int32)
    kept_rows = assignment == own_rows
    owner_shard = assignment // row_count
    target = assignment % row_count
    distance = (owner_shard - shard_index) % shards
    at_home = distance == 0
    partial_sums = (
        jnp.zeros((row_count, row_width), jnp.float32),
        jnp.zeros((row_count, row_width), jnp.float32),
        jnp.zeros((row_count,), jnp.float32),
    )
    home_high, home_low = split_target(jnp.where(at_home, target, row_count))
    partial_sums = add_rows(
        partial_sums, (cache_keys, cache_values, row_weight, home_high, home_low)
    )
    bucket_rank = bucket_ranks(distance, shards)
    target_high, target_low = split_target(target)
    payload = (cache_keys, cache_values, row_weight, target_high, target_low)
    slot_index = jnp.where(at_home, shards * NEAR, owner_shard * NEAR + bucket_rank)
    outgoing = fold_peers(pack_rows(payload, slot_index, shards * NEAR), shards)
    incoming = (
        lax.all_to_all(outgoing[0], "ctx", split_axis=0, concat_axis=0, tiled=True),
        lax.all_to_all(outgoing[1], "ctx", split_axis=0, concat_axis=0, tiled=True),
        lax.all_to_all(outgoing[2], "ctx", split_axis=0, concat_axis=0, tiled=True),
        lax.all_to_all(outgoing[3], "ctx", split_axis=0, concat_axis=0, tiled=True),
        lax.all_to_all(outgoing[4], "ctx", split_axis=0, concat_axis=0, tiled=True),
    )
    partial_sums = add_rows(partial_sums, unfold_peers(incoming))
    numer_keys, numer_values, denominator = partial_sums
    safe_total = jnp.where(kept_rows, denominator, 1.0)[:, None]
    merged_keys = jnp.where(
        kept_rows[:, None], numer_keys / safe_total, cache_keys.astype(jnp.float32)
    ).astype(jnp.bfloat16)
    merged_values = jnp.where(
        kept_rows[:, None], numer_values / safe_total, cache_values.astype(jnp.float32)
    ).astype(jnp.bfloat16)
    query_rows = queries.shape[0]
    group_size = queries.shape[1] // row_width
    query_heads = (
        queries.reshape(query_rows, kv_local, group_size, head_dim)
        .transpose(1, 0, 2, 3)
        .reshape(kv_local, query_rows * group_size, head_dim)
    )
    block_span = min(512, row_count)
    span_count = row_count // block_span
    score_scale = head_dim ** (-0.5)

    def advance(block_index, running):
        peak_score, weight_sum, accumulated = running
        key_piece = merged_keys.reshape(block_span, kv_local, head_dim)
        value_piece = merged_values.reshape(block_span, kv_local, head_dim)
        scores = (
            jnp.einsum("hqd,khd->hqk", query_heads, key_piece, preferred_element_type=jnp.float32)
            * score_scale
        )
        scores = jnp.where(kept_rows[None, None, :], scores, -jnp.inf)
        new_peak = jnp.maximum(peak_score, jnp.max(scores, axis=2))
        weights = jnp.exp(scores - new_peak[:, :, None])
        rescale = jnp.exp(peak_score - new_peak)
        weight_sum = weight_sum * rescale + jnp.sum(weights, axis=2)
        accumulated = accumulated * rescale[:, :, None] + jnp.einsum(
            "hqk,khd->hqd",
            weights.astype(jnp.bfloat16),
            value_piece,
            preferred_element_type=jnp.float32,
        )
        return (new_peak, weight_sum, accumulated)

    pair_rows = query_rows * group_size
    start_state = (
        jnp.full((kv_local, pair_rows), -jnp.inf, jnp.float32),
        jnp.zeros((kv_local, pair_rows), jnp.float32),
        jnp.zeros((kv_local, pair_rows, head_dim), jnp.float32),
    )
    peak_score, weight_sum, accumulated = lax.fori_loop(0, span_count, advance, start_state)
    global_peak = lax.pmax(peak_score, "ctx")
    rescale = jnp.exp(peak_score - global_peak)
    weight_sum, accumulated = lax.psum(
        (weight_sum * rescale, accumulated * rescale[:, :, None]), "ctx"
    )
    finished = accumulated / weight_sum[:, :, None]
    attended = (
        finished.reshape(kv_local, query_rows, group_size, head_dim)
        .transpose(1, 0, 2, 3)
        .reshape(query_rows, kv_local * group_size * head_dim)
        .astype(jnp.bfloat16)
    )
    return (merged_keys, merged_values, attended)


def solution(mesh):
    placed = (P("ctx", "kv"), P("ctx", "kv"), P("kv", "ctx"), P("ctx"), P(None, "kv"))
    return jax.shard_map(
        per_device,
        mesh=mesh,
        in_specs=placed,
        out_specs=(P("ctx", "kv"), P("ctx", "kv"), P(None, "kv")),
        check_vma=False,
    )
```

profile of v0, /device:TPU:2, one launch (start us, length us, event | category | flops | bytes accessed | tf_op | source)
XLA Modules:
  0.0 578.6 jit_solution(12934312169116344525)
XLA Ops:
  7.2 0.8 fusion.51
  8.3 0.7 fusion.35
  9.0 3.8 scatter_custom_fusion.2
  12.8 0.7 all_to_all.33
  13.5 18.7 %all-to-all-start.1 = ((bf16[64,1,16]{2,1,0:T(2,128)(2,1)}), bf16[64,1,16]{2,1,0:T(2,128)(2,1)S(1)}, u32[]{:S(2)}, u32[]{:S(2)}) async-start(bf16[64,1,16]{2,1,0:T(2,128)(2,1)} %all_to_all.33), calls=%async_computation.1 | async-start | bytes 65536 | tf_op jit(solution)/shard_map/all_to_all | solution.py:106
  32.2 0.7 reduce_sum.44
  32.9 11.7 %psum.21 = bf16[512]{0:T(512)(128)(2,1)S(1)} all-reduce(f32[512]{0:T(512)S(1)} %bitcast.42), channel_id=1, replica_groups=mesh['ctx'=64,'kv'=8] {'kv'}, use_global_device_ids=true, to_apply=%region_0.0 | all-reduce | flops 512 | bytes 3072 | tf_op jit(solution)/shard_map/psum | solution.py:78
  44.6 3.8 scatter_custom_fusion.4
  48.4 0.7 all_to_all.34
  49.1 14.7 %all-to-all-start.3 = ((bf16[64,1,16]{2,1,0:T(2,128)(2,1)}), bf16[64,1,16]{2,1,0:T(2,128)(2,1)S(1)}, u32[]{:S(2)}, u32[]{:S(2)}) async-start(bf16[64,1,16]{2,1,0:T(2,128)(2,1)} %all_to_all.34), calls=%async_computation.3 | async-start | bytes 65536 | tf_op jit(solution)/shard_map/all_to_all | solution.py:104
  63.8 3.8 scatter_custom_fusion.1
  67.6 0.7 all_to_all.32
  68.3 9.9 %all-to-all-done.3 = bf16[64,1,16]{2,1,0:T(2,128)(2,1)S(1)} async-done(((bf16[64,1,16]{2,1,0:T(2,128)(2,1)}), bf16[64,1,16]{2,1,0:T(2,128)(2,1)S(1)}, u32[]{:S(2)}, u32[]{:S(2)}) %all-to-all-start.3) | async-done | bytes 2080 | tf_op jit(solution)/shard_map/all_to_all | solution.py:104
  78.2 5.0 all-to-all-start
  83.2 2.8 scatter_custom_fusion.3
  86.0 11.8 %all-to-all-done = bf16[64,1,16]{2,1,0:T(2,128)(2,1)S(1)} async-done(((bf16[64,1,16]{2,1,0:T(2,128)(2,1)}), bf16[64,1,16]{2,1,0:T(2,128)(2,1)S(1)}, u32[]{:S(2)}, u32[]{:S(2)}) %all-to-all-start) | async-done | bytes 2080 | tf_op jit(solution)/shard_map/all_to_all | solution.py:105
  97.7 4.6 all-to-all-start.2
  102.4 2.8 scatter_custom_fusion.9
  105.2 17.3 %all-to-all-done.2 = bf16[64,16,128]{2,1,0:T(8,128)(2,1)S(1)} async-done(((bf16[64,16,128]{2,1,0:T(8,128)(2,1)}), bf16[64,16,128]{2,1,0:T(8,128)(2,1)S(1)}, u32[]{:S(2)}, u32[]{:S(2)}) %all-to-all-start.2) | async-done | bytes 262176 | tf_op jit(solution)/shard_map/all_to_all | solution.py:102
  122.4 4.6 all-to-all-start.4
  127.2 4.3 scatter_custom_fusion.6
  131.5 2.4 scatter_custom_fusion
  134.0 2.4 scatter_custom_fusion.8
  137.0 7.6 %scatter_fusion = f32[512]{0:T(512)S(1)} fusion(f32[512]{0:T(512)S(1)} %scatter_custom_fusion.6, s32[1024]{0:T(1024)S(1)} %bitcast.37, f32[1024]{0:T(1024)S(1)} %reshape.242), kind=kCustom, calls=%fused_computation.7 | custom fusion | flops 1024 | bytes 16384 | tf_op jit(solution)/shard_map/scatter-add | solution.py:67
  144.6 8.0 %scatter_custom_fusion.5 = f32[512,128]{1,0:T(8,128)S(1)} fusion(f32[512,128]{1,0:T(8,128)S(1)} %scatter_custom_fusion, s32[1024]{0:T(1024)S(1)} %bitcast.38, bf16[1024,128]{1,0:T(8,128)(2,1)S(1)} %bitcast.33, f32[1024]{0:T(1024)S(1)} %reshape.242), kind=kCustom, calls=%fused_computation.29 | custom fusion | flops 393216 | bytes 528384 | tf_op jit(solution)/shard_map/scatter-add | solution.py:61
  152.6 8.0 %scatter_custom_fusion.10 = f32[512,128]{1,0:T(8,128)S(1)} fusion(f32[512,128]{1,0:T(8,128)S(1)} %scatter_custom_fusion.8, s32[1024]{0:T(1024)S(1)} %bitcast.39, bf16[1024,128]{1,0:T(8,128)(2,1)S(1)} %bitcast.34, f32[1024]{0:T(1024)S(1)} %reshape.242), kind=kCustom, calls=%fused_computation.27 | custom fusion | flops 393216 | bytes 528384 | tf_op jit(solution)/shard_map/scatter-add | solution.py:64
  161.4 143.2 %pmax.7 = f32[1,1024]{1,0:T(1,128)S(1)} all-reduce(f32[1,1024]{1,0:T(1,128)S(1)} %bitcast.35), channel_id=1, replica_groups=mesh['ctx'=64,'kv'=8] {'ctx'}, use_global_device_ids=true, to_apply=%region_16.17 | all-reduce | flops 1024 | bytes 8192 | tf_op jit(solution)/shard_map/pmax | solution.py:156
  305.1 1.7 fusion.4
  306.8 138.0 %psum.23 = f32[1024]{0:T(1024)S(1)} all-reduce(f32[1024]{0:T(1024)S(1)} %bitcast.41), channel_id=1, replica_groups=mesh['ctx'=64,'kv'=8] {'ctx'}, use_global_device_ids=true, to_apply=%region_19.20 | all-reduce | flops 1024 | bytes 8192 | tf_op jit(solution)/shard_map/psum | solution.py:158
  444.8 124.9 %all-reduce.2.cloned.1.call-done = f32[1,1024,128]{2,1,0:T(8,128)} async-done(((f32[1,1024,128]{2,1,0:T(8,128)}), f32[1,1024,128]{2,1,0:T(8,128)}) %all-reduce.2.cloned.1.call-update) | async-done | bytes 524304 | tf_op jit(solution)/shard_map/psum | solution.py:158
  569.7 1.2 divide_convert_fusion
  571.0 0.8 convert_element_type.130
  (34 shorter events, 2.2 us)
Async XLA Ops:
  7.2 120.0 %copy-start.5 = (s32[512]{0:T(512)S(1)}, s32[512]{0:T(512)}, u32[]{:S(2)}) copy-start(s32[512]{0:T(512)} %param.8) | copy-start | bytes 6148
  7.2 124.3 %copy-start.2 = (bf16[512,128]{1,0:T(8,128)(2,1)S(1)}, bf16[512,128]{1,0:T(8,128)(2,1)}, u32[]{:S(2)}) copy-start(bf16[512,128]{1,0:T(8,128)(2,1)} %param.5) | copy-start | bytes 393220
  7.2 126.8 %copy-start.1 = (bf16[512,128]{1,0:T(8,128)(2,1)S(1)}, bf16[512,128]{1,0:T(8,128)(2,1)}, u32[]{:S(2)}) copy-start(bf16[512,128]{1,0:T(8,128)(2,1)} %param.6) | copy-start | bytes 393220
  7.2 129.2 %copy-start.3 = (bf16[128,1024]{1,0:T(8,128)(2,1)S(1)}, bf16[128,1024]{1,0:T(8,128)(2,1)}, u32[]{:S(2)}) copy-start(bf16[128,1024]{1,0:T(8,128)(2,1)} %param.9) | copy-start | bytes 786436
  13.5 35.6 %all-to-all-start.1 = ((bf16[64,1,16]{2,1,0:T(2,128)(2,1)}), bf16[64,1,16]{2,1,0:T(2,128)(2,1)S(1)}, u32[]{:S(2)}, u32[]{:S(2)}) async-start(bf16[64,1,16]{2,1,0:T(2,128)(2,1)} %all_to_all.33), calls=%async_computation.1 | async-start | bytes 65536 | tf_op jit(solution)/shard_map/all_to_all | solution.py:106
  49.1 29.1 %all-to-all-start.3 = ((bf16[64,1,16]{2,1,0:T(2,128)(2,1)}), bf16[64,1,16]{2,1,0:T(2,128)(2,1)S(1)}, u32[]{:S(2)}, u32[]{:S(2)}) async-start(bf16[64,1,16]{2,1,0:T(2,128)(2,1)} %all_to_all.34), calls=%async_computation.3 | async-start | bytes 65536 | tf_op jit(solution)/shard_map/all_to_all | solution.py:104
  78.2 19.6 %all-to-all-start = ((bf16[64,1,16]{2,1,0:T(2,128)(2,1)}), bf16[64,1,16]{2,1,0:T(2,128)(2,1)S(1)}, u32[]{:S(2)}, u32[]{:S(2)}) async-start(bf16[64,1,16]{2,1,0:T(2,128)(2,1)} %all_to_all.32), calls=%async_computation | async-start | bytes 65536 | tf_op jit(solution)/shard_map/all_to_all | solution.py:105
  97.7 24.7 %all-to-all-start.2 = ((bf16[64,16,128]{2,1,0:T(8,128)(2,1)}), bf16[64,16,128]{2,1,0:T(8,128)(2,1)S(1)}, u32[]{:S(2)}, u32[]{:S(2)}) async-start(bf16[64,16,128]{2,1,0:T(8,128)(2,1)} %bitcast.5), calls=%async_computation.2 | async-start | bytes 524288 | tf_op jit(solution)/shard_map/all_to_all | solution.py:102
  122.4 30.2 %all-to-all-start.4 = ((bf16[64,16,128]{2,1,0:T(8,128)(2,1)}), bf16[64,16,128]{2,1,0:T(8,128)(2,1)S(1)}, u32[]{:S(2)}, u32[]{:S(2)}) async-start(bf16[64,16,128]{2,1,0:T(8,128)(2,1)} %bitcast.7), calls=%async_computation.4 | async-start | bytes 524288 | tf_op jit(solution)/shard_map/all_to_all | solution.py:103
  127.1 442.6 %all-reduce.2.cloned.1.call-start = ((), (), s32[]{:S(2)}) async-start(), calls=%async_computation.5 | async-start | bytes 1048576 | tf_op jit(solution)/shard_map/psum | solution.py:158
  160.9 144.2 %copy-start = (bf16[512,128]{1,0:T(8,128)(2,1)}, bf16[512,128]{1,0:T(8,128)(2,1)S(1)}, u32[]{:S(2)}) copy-start(bf16[512,128]{1,0:T(8,128)(2,1)S(1)} %get-tuple-element.34) | copy-start | bytes 393220
  160.9 144.2 %copy-start.4 = (bf16[512,128]{1,0:T(8,128)(2,1)}, bf16[512,128]{1,0:T(8,128)(2,1)S(1)}, u32[]{:S(2)}) copy-start(bf16[512,128]{1,0:T(8,128)(2,1)S(1)} %get-tuple-element.33) | copy-start | bytes 393220
Sparse Core Ops, SparseCore 0:
  306.9 262.7 all-reduce.1
where the time goes:
time: 579 us
  blocking collectives  293 us (51%)
  waiting for transfers between devices  164 us (28%)
  starting transfers between devices  47.7 us (8%)
  other arithmetic  37.4 us (6%)
  local copies, waits for them, and re-layouts  20.1 us (3%)
  between operations  14.3 us (2%)
    pmax x1, blocking collectives, per_device(): global_peak = lax.pmax(peak_score, 'ctx')  143 us
    psum x1, blocking collectives, per_device(): lax.psum((weight_sum * rescale, accumulated * rescale[:, :, None]), 'ctx')  138 us
    psum x1, waiting for transfers between devices, per_device(): lax.psum((weight_sum * rescale, accumulated * rescale[:, :, None]), 'ctx')  125 us
    all_to_all x1, starting transfers between devices, per_device(): lax.all_to_all(outgoing[4], 'ctx', split_axis=0, concat_axis=0, tiled=True)  18.7 us
    all_to_all x1, waiting for transfers between devices, per_device(): lax.all_to_all(outgoing[0], 'ctx', split_axis=0, concat_axis=0, tiled=True)  17.3 us
    scatter x5, local copies, waits for them, and re-layouts, pack_rows(): return tuple((jnp.zeros((capacity,) + member.shape[1:], member.dtype).at[...  16.8 us
    all_to_all x1, starting transfers between devices, per_device(): lax.all_to_all(outgoing[2], 'ctx', split_axis=0, concat_axis=0, tiled=True)  14.7 us
    scatter-add x2, other arithmetic, add_rows(): denominator = denominator.at[target_rows].add(scale_rows, mode='drop')  11.9 us
  transfers between devices with their start and end apart: 6, of which 4 were waited for; matrix products, arithmetic and copies ran while one was open for 7% of the time, Pallas kernels for 0%

commit v1 on v0

v1 whole, which is shorter than its diff:
```python
import functools

import jax
import jax.numpy as jnp
from jax import lax
from jax.experimental import pallas as pl
from jax.experimental.pallas import tpu as pltpu
from jax.sharding import PartitionSpec as P

NEAR = 16
LANES = 128
PIECES = 4
STATS = 8
F32 = jnp.float32
BF16 = jnp.bfloat16


def summed_weight(importance):
    return jnp.sum(importance.astype(F32), axis=0, keepdims=True).astype(BF16).astype(F32)


def pack_kernel(shards, shard_ref, assignment_ref, importance_ref, keys_ref, values_ref, far_ref, ahead_ref, back_ref):
    row_count = keys_ref.shape[0]
    shard = shard_ref[0]
    assignment = assignment_ref[...]
    owner = assignment // row_count
    target = assignment % row_count
    distance = owner - shard
    distance = jnp.where(distance < 0, distance + shards, distance)
    is_ahead = distance == 1
    is_back = distance == shards - 1
    side = lax.broadcasted_iota(jnp.int32, (8, row_count), 0)
    flags = jnp.where(side == 0, is_ahead.astype(F32), jnp.where(side == 1, is_back.astype(F32), 0.0))
    earlier = lax.broadcasted_iota(jnp.int32, (row_count, row_count), 0) < lax.broadcasted_iota(
        jnp.int32, (row_count, row_count), 1
    )
    ranks = jnp.dot(flags.astype(BF16), earlier.astype(F32).astype(BF16), preferred_element_type=F32)
    ranks = ranks.astype(jnp.int32)
    slot = jnp.where(distance == 0, -1, owner)
    slot = jnp.where(is_ahead, shards + ranks[0:1, :], slot)
    slot = jnp.where(is_back, shards + NEAR + ranks[1:2, :], slot)
    slots = shards + 2 * NEAR
    weight = summed_weight(importance_ref[...])
    part = lax.broadcasted_iota(jnp.int32, (LANES, row_count), 0)
    high = (target // LANES).astype(F32)
    low = (target % LANES).astype(F32)
    notes = jnp.where(part == 0, weight, jnp.where(part == 1, high, jnp.where(part == 2, low, 0.0))).astype(BF16)
    line = lax.broadcasted_iota(jnp.int32, (PIECES * slots, row_count), 0)
    chosen = (line // PIECES == slot).astype(F32).astype(BF16)
    rows = jnp.concatenate([keys_ref[...], values_ref[...]], axis=1)
    picked = jnp.dot(chosen, rows, preferred_element_type=F32)
    noted = lax.dot_general(chosen, notes, (((1,), (1,)), ((), ())), preferred_element_type=F32)
    piece = lax.broadcasted_iota(jnp.int32, (PIECES * slots, LANES), 0) % PIECES
    packed = jnp.where(
        piece == 0,
        picked[:, :LANES],
        jnp.where(piece == 1, picked[:, LANES:], jnp.where(piece == 2, noted, 0.0)),
    ).astype(BF16)
    far = PIECES * shards
    near = PIECES * NEAR
    far_ref[...] = packed[:far]
    ahead_ref[...] = packed[far : far + near]
    back_ref[...] = packed[far + near :]


def split_parts(value, count):
    parts = []
    for _ in range(count):
        rounded = value.astype(BF16).astype(F32)
        parts.append(rounded)
        value = value - rounded
    return parts


def attend_kernel(
    shards,
    shard_ref,
    assignment_ref,
    importance_ref,
    keys_ref,
    values_ref,
    far_ref,
    ahead_ref,
    back_ref,
    queries_ref,
    merged_keys_ref,
    merged_values_ref,
    partial_ref,
):
    row_count, head_dim = keys_ref.shape
    shard = shard_ref[0]
    assignment = assignment_ref[...]
    own = shard * row_count + lax.broadcasted_iota(jnp.int32, (1, row_count), 1)
    kept = assignment == own
    weight = summed_weight(importance_ref[...])
    at_home = assignment // row_count == shard
    target = jnp.where(at_home, assignment % row_count, -1)
    line = lax.broadcasted_iota(jnp.int32, (row_count, row_count), 0)
    home_mix = jnp.where(target == line, weight, 0.0).astype(BF16)
    own_rows = jnp.concatenate([keys_ref[...], values_ref[...]], axis=1)
    ones = jnp.ones((row_count, LANES), BF16)
    sums = jnp.dot(home_mix, own_rows, preferred_element_type=F32)
    total = jnp.dot(home_mix, ones, preferred_element_type=F32)

    arrived = jnp.concatenate([far_ref[...], ahead_ref[...], back_ref[...]], axis=0)
    count = arrived.shape[0]
    notes = arrived.astype(F32).T
    far_weight = notes[0:1, :]
    far_target = notes[1:2, :] * LANES + notes[2:3, :]
    piece = lax.broadcasted_iota(jnp.int32, (1, count), 1) % PIECES
    far_target = jnp.where(piece == 2, far_target, -1.0).astype(jnp.int32)
    line = lax.broadcasted_iota(jnp.int32, (row_count, count), 0)
    mix = jnp.where(far_target == line, far_weight, 0.0)
    value_mix = pltpu.roll(mix, count - 1, 1).astype(BF16)
    key_mix = pltpu.roll(mix, count - 2, 1).astype(BF16)
    total = total + jnp.dot(key_mix, jnp.ones((count, LANES), BF16), preferred_element_type=F32)
    key_sums = sums[:, :head_dim] + jnp.dot(key_mix, arrived, preferred_element_type=F32)
    value_sums = sums[:, head_dim:] + jnp.dot(value_mix, arrived, preferred_element_type=F32)
    has_total = total > 0.0
    safe_total = jnp.where(has_total, total, 1.0)
    merged_keys = jnp.where(has_total, key_sums / safe_total, keys_ref[...].astype(F32)).astype(BF16)
    merged_values = jnp.where(has_total, value_sums / safe_total, values_ref[...].astype(F32)).astype(BF16)
    merged_keys_ref[...] = merged_keys
    merged_values_ref[...] = merged_values

    query_rows = queries_ref.shape[0]
    heads = queries_ref.shape[1] // head_dim
    per_peer = query_rows * heads // shards
    peers_of_head = query_rows // per_peer
    scale = head_dim ** (-0.5)
    lane = lax.broadcasted_iota(jnp.int32, (query_rows, LANES), 1)
    peaks = jnp.zeros((query_rows, LANES), F32)
    sizes = jnp.zeros((query_rows, LANES), F32)
    for head in range(heads):
        query = queries_ref[:, head * head_dim : (head + 1) * head_dim]
        scores = lax.dot_general(query, merged_keys, (((1,), (1,)), ((), ())), preferred_element_type=F32)
        scores = jnp.where(kept, scores * scale, -jnp.inf)
        peak = jnp.max(scores, axis=1, keepdims=True)
        prob = jnp.exp(scores - peak)
        size = jnp.sum(prob, axis=1, keepdims=True)
        sums = jnp.dot(prob.astype(BF16), merged_values, preferred_element_type=F32).astype(BF16)
        peaks = jnp.where(lane == head, peak, peaks)
        sizes = jnp.where(lane == head, size, sizes)
        for part in range(peers_of_head):
            partial_ref[head * peers_of_head + part, 0:per_peer, :] = sums[part * per_peer : (part + 1) * per_peer]
    peak_parts = split_parts(peaks.T, 3)
    size_parts = split_parts(sizes.T, 2)
    stat = lax.broadcasted_iota(jnp.int32, (STATS, query_rows), 0)
    for head in range(heads):
        block = jnp.zeros((STATS, query_rows), F32)
        for at, member in enumerate(peak_parts + size_parts):
            block = jnp.where(stat == at, member[head : head + 1, :], block)
        for part in range(peers_of_head):
            partial_ref[head * peers_of_head + part, per_peer : per_peer + STATS, :] = block.astype(BF16)


def combine_kernel(shards, shard_ref, partial_ref, finished_ref, factor_ref):
    per_peer = partial_ref.shape[1] - STATS
    query_rows = partial_ref.shape[2]
    stats = partial_ref[:, per_peer:, :].astype(F32)
    peak = stats[:, 0, :] + stats[:, 1, :] + stats[:, 2, :]
    size = stats[:, 3, :] + stats[:, 4, :]
    rescale = jnp.exp(peak - jnp.max(peak, axis=0, keepdims=True))
    factor = rescale / jnp.sum(rescale * size, axis=0, keepdims=True)
    if shards < LANES:
        factor = jnp.concatenate([factor, jnp.zeros((LANES - shards, query_rows), F32)], axis=0)
    factor_ref[...] = factor.T
    start = pl.multiple_of((shard_ref[0] % (query_rows // per_peer)) * per_peer, per_peer)
    factor = factor_ref[pl.ds(start, per_peer), :]
    total = jnp.zeros((per_peer, LANES), F32)
    for peer in range(shards):
        total = total + factor[:, peer : peer + 1] * partial_ref[peer, 0:per_peer, :].astype(F32)
    finished = total.astype(BF16)
    for peer in range(shards):
        finished_ref[peer] = finished


def in_vmem(count):
    return [pl.BlockSpec(memory_space=pltpu.SMEM)] + [pl.BlockSpec(memory_space=pltpu.VMEM)] * count


def run_kernel(body, shards, shapes, operands, scratch=()):
    return pl.pallas_call(
        functools.partial(body, shards),
        out_shape=[jax.ShapeDtypeStruct(shape, BF16) for shape in shapes],
        in_specs=in_vmem(len(operands) - 1),
        out_specs=[pl.BlockSpec(memory_space=pltpu.VMEM)] * len(shapes),
        scratch_shapes=list(scratch),
        compiler_params=pltpu.CompilerParams(vmem_limit_bytes=32 * 1024 * 1024),
    )(*operands)


def per_device(cache_keys, cache_values, importance, assignment, queries):
    row_count, head_dim = cache_keys.shape
    query_rows = queries.shape[0]
    heads = queries.shape[1] // head_dim
    shards = lax.axis_size("ctx")
    per_peer = query_rows * heads // shards
    shard = lax.axis_index("ctx").astype(jnp.int32).reshape(1)
    assignment = assignment.reshape(1, row_count)
    importance = lax.all_gather(importance, "kv", axis=0, tiled=True)

    far, ahead, back = run_kernel(
        pack_kernel,
        shards,
        [(PIECES * shards, LANES), (PIECES * NEAR, LANES), (PIECES * NEAR, LANES)],
        (shard, assignment, importance, cache_keys, cache_values),
    )
    from_back = lax.ppermute(ahead, "ctx", [(i, (i + 1) % shards) for i in range(shards)])
    from_ahead = lax.ppermute(back, "ctx", [(i, (i - 1) % shards) for i in range(shards)])
    far = lax.all_to_all(far.reshape(shards, PIECES, LANES), "ctx", 0, 0, tiled=True)
    far = far.reshape(shards * PIECES, LANES)

    merged_keys, merged_values, partial = run_kernel(
        attend_kernel,
        shards,
        [cache_keys.shape, cache_values.shape, (shards, per_peer + STATS, LANES)],
        (shard, assignment, importance, cache_keys, cache_values, far, from_back, from_ahead, queries),
    )
    partial = lax.all_to_all(partial, "ctx", 0, 0, tiled=True)
    (finished,) = run_kernel(
        combine_kernel,
        shards,
        [(shards, per_peer, LANES)],
        (shard, partial),
        [pltpu.VMEM((query_rows, LANES), F32)],
    )
    finished = lax.all_to_all(finished, "ctx", 0, 0, tiled=True)
    attended = finished.reshape(heads, query_rows, head_dim).transpose(1, 0, 2).reshape(query_rows, heads * head_dim)
    return (merged_keys, merged_values, attended)


def solution(mesh):
    placed = (P("ctx", "kv"), P("ctx", "kv"), P("kv", "ctx"), P("ctx"), P(None, "kv"))
    return jax.shard_map(
        per_device,
        mesh=mesh,
        in_specs=placed,
        out_specs=(P("ctx", "kv"), P("ctx", "kv"), P(None, "kv")),
        check_vma=False,
    )
```

time: 579 us -> 120 us (0.21)
  blocking collectives: 293 us -> 77.9 us
  waiting for transfers between devices: 164 us -> 6.3 us
  other arithmetic: 37.4 us -> 0 us
  starting transfers between devices: 47.7 us -> 24.9 us
  local copies, waits for them, and re-layouts: 20.1 us -> 4.9 us
  between operations: 14.3 us -> 0.7 us
    psum x2 -> x0, blocking collectives: 150 us -> none  [the longest x1 138 us: per_device(): lax.psum((weight_sum * rescale, accumulated * rescale[:, :, None]), 'ctx')]
    pmax x1 -> x0, blocking collectives: 143 us -> none  [per_device(): global_peak = lax.pmax(peak_score, 'ctx')]
    psum x1 -> x0, waiting for transfers between devices: 125 us -> none  [per_device(): lax.psum((weight_sum * rescale, accumulated * rescale[:, :, None]), 'ctx')]
    all_to_all x0 -> x2, blocking collectives: none -> 63.1 us  [the longest x1 36.8 us: per_device(): partial = lax.all_to_all(partial, 'ctx', 0, 0, tiled=True)]
    all_to_all x5 -> x1, waiting for transfers between devices: 39 us -> 4.89 us  [per_device(): lax.all_to_all(far.reshape(shards, PIECES, LANES), 'ctx', 0, 0, tiled=True)]
    scatter-add x6 -> x0, other arithmetic: 32.8 us -> none  [the longest x2 11.9 us: add_rows(): denominator = denominator.at[target_rows].add(scale_rows, mode='drop')]
    all_to_all x5 -> x1, starting transfers between devices: 47.7 us -> 15.7 us  [per_device(): lax.all_to_all(far.reshape(shards, PIECES, LANES), 'ctx', 0, 0, tiled=True)]
    scatter x5 -> x0, local copies, waits for them, and re-layouts: 16.8 us -> none  [pack_rows(): return tuple((jnp.zeros((capacity,) + member.shape[1:], member.dtype).at[...]
  transfers between devices with their start and end apart: 6 -> 3, of which waited for: 4 -> 2; matrix products, arithmetic and copies ran while one was open for 7% -> 0% of each run, Pallas kernels for 0% -> 0%
where the time goes in v1:
time: 120 us; the launch traced here: 119 us
  blocking collectives  77.9 us (65%)
  starting transfers between devices  24.9 us (21%)
  waiting for transfers between devices  6.3 us (5%)
  local copies, waits for them, and re-layouts  4.9 us (4%)
  Pallas kernels  4.73 us (4%)
    all_to_all x1, blocking collectives, per_device(): partial = lax.all_to_all(partial, 'ctx', 0, 0, tiled=True)  36.8 us
    all_to_all x1, blocking collectives, per_device(): finished = lax.all_to_all(finished, 'ctx', 0, 0, tiled=True)  26.3 us
    all_to_all x1, starting transfers between devices, per_device(): lax.all_to_all(far.reshape(shards, PIECES, LANES), 'ctx', 0, 0, tiled=True)  15.7 us
    all_gather x1, blocking collectives, per_device(): importance = lax.all_gather(importance, 'kv', axis=0, tiled=True)  14.8 us
    ppermute x1, starting transfers between devices, per_device(): lax.ppermute(back, 'ctx', [(i, (i - 1) % shards) for i in range(shards)])  5.68 us
    all_to_all x1, waiting for transfers between devices, per_device(): lax.all_to_all(far.reshape(shards, PIECES, LANES), 'ctx', 0, 0, tiled=True)  4.89 us
    pallas_call x3, Pallas kernels, run_kernel(): pl.pallas_call(functools.partial(body, shards), out_shape=[jax.ShapeDtype...  4.73 us
    unnamed x15, local copies, waits for them, and re-layouts  4.12 us
  transfers between devices with their start and end apart: 3, of which 2 were waited for; matrix products, arithmetic and copies ran while one was open for 0% of the time, Pallas kernels for 0%

profile of v1, /device:TPU:2, one launch (start us, length us, event | category | flops | bytes accessed | tf_op | source)
XLA Modules:
  0.0 119.4 jit_solution(7108919974980540522)
XLA Ops:
  0.6 0.0 copy-start.6
  0.6 0.7 copy-done.6
  1.3 14.8 %all-gather = bf16[8,1,512]{2,1,0:T(2,128)(2,1)S(1)} all-gather(bf16[1,1,512]{2,1,0:T(2,128)(2,1)S(1)} %bitcast.22), channel_id=1, replica_groups=mesh['ctx'=64,'kv'=8] {'kv'}, dimensions={0}, use_global_device_ids=true | all-gather | bytes 9216 | tf_op jit(solution)/shard_map/all_gather | solution.py:201
  16.1 0.0 copy-start.5
  16.1 0.7 copy-done.5
  16.8 0.0 copy-start
  16.8 0.9 copy-done
  17.7 0.0 copy-start.2
  17.7 0.9 copy-done.2
  18.6 0.0 copy-start.3
  18.6 1.1 shard_map.76
  19.7 0.0 copy-start.1
  19.7 15.7 %all-to-all-start = ((bf16[64,4,128]{2,1,0:T(4,128)(2,1)}), bf16[64,4,128]{2,1,0:T(4,128)(2,1)S(1)}, u32[]{:S(2)}, u32[]{:S(2)}) async-start(bf16[64,4,128]{2,1,0:T(4,128)(2,1)} %bitcast.3), calls=%async_computation | async-start | bytes 131072 | tf_op jit(solution)/shard_map/all_to_all | solution.py:211
  35.4 3.5 %collective-permute-start = (bf16[64,128]{1,0:T(8,128)(2,1)S(1)}, bf16[64,128]{1,0:T(8,128)(2,1)S(1)}, u32[]{:S(2)}, u32[]{:S(2)}) collective-permute-start(bf16[64,128]{1,0:T(8,128)(2,1)S(1)} %get-tuple-element.10), channel_id=1, source_target_pairs={{0,8},{8,16},{16,24},{24,32},{32,40},{40,48},{48,56},{56,64},{64,7... | collective-permute-start | bytes 49160 | tf_op jit(solution)/shard_map/ppermute | solution.py:209
  38.9 5.7 %collective-permute-start.1 = (bf16[64,128]{1,0:T(8,128)(2,1)S(1)}, bf16[64,128]{1,0:T(8,128)(2,1)S(1)}, u32[]{:S(2)}, u32[]{:S(2)}) collective-permute-start(bf16[64,128]{1,0:T(8,128)(2,1)S(1)} %get-tuple-element.11), channel_id=1, source_target_pairs={{0,504},{8,0},{16,8},{24,16},{32,24},{40,32},{48,40},{56,48},{64,5... | collective-permute-start | bytes 49160 | tf_op jit(solution)/shard_map/ppermute | solution.py:210
  44.6 0.0 collective-permute-done.ahead_ref
  44.6 1.4 %collective-permute-done.1.back_ref = bf16[64,128]{1,0:T(8,128)(2,1)S(1)} collective-permute-done((bf16[64,128]{1,0:T(8,128)(2,1)S(1)}, bf16[64,128]{1,0:T(8,128)(2,1)S(1)}, u32[]{:S(2)}, u32[]{:S(2)}) %collective-permute-start.1) | collective-permute-done | bytes 16416 | tf_op jit(solution)/shard_map/ppermute | solution.py:210
  46.0 4.9 %all-to-all-done = bf16[64,4,128]{2,1,0:T(4,128)(2,1)S(1)} async-done(((bf16[64,4,128]{2,1,0:T(4,128)(2,1)}), bf16[64,4,128]{2,1,0:T(4,128)(2,1)S(1)}, u32[]{:S(2)}, u32[]{:S(2)}) %all-to-all-start) | async-done | bytes 65568 | tf_op jit(solution)/shard_map/all_to_all | solution.py:211
  50.9 0.0 copy-done.3
  50.9 0.0 copy-done.1
  50.9 0.0 copy-start.4
  50.9 0.9 copy-done.4
  51.9 3.1 %shard_map.77 = (bf16[512,128]{1,0:T(8,128)(2,1)}, bf16[512,128]{1,0:T(8,128)(2,1)}, bf16[64,24,128]{2,1,0:T(8,128)(2,1)S(1)}) custom-call(s32[1]{0:T(128)} %bitcast.shard_ref, s32[1,512]{1,0:T(1,128)S(1)} %bitcast.19, bf16[8,512]{1,0:T(8,128)(2,1)S(1)} %bitcast.17, bf16[512,128]{1,0:T(8,128)(2,1)S(1)} %copy-done.1, bf16[512,128]{1,0:T(8,128)(2,1)S(1)} %copy-done.3, ...), custom_call_target="tpu_custom_call" | custom-call | tf_op jit(solution)/shard_map/pallas_call | solution.py:183
  55.0 36.8 %all_to_all.15.partial_ref = bf16[64,24,128]{2,1,0:T(8,128)(2,1)S(1)} all-to-all(bf16[64,24,128]{2,1,0:T(8,128)(2,1)S(1)} %get-tuple-element.14), channel_id=1, replica_groups=mesh['ctx'=64,'kv'=8] {'ctx'}, dimensions={0} | all-to-all | bytes 786432 | tf_op jit(solution)/shard_map/all_to_all | solution.py:220
  91.8 0.5 shard_map.78
  92.3 26.3 %all_to_all.16 = bf16[64,16,128]{2,1,0:T(8,128)(2,1)S(1)} all-to-all(bf16[64,16,128]{2,1,0:T(8,128)(2,1)S(1)} %shard_map.78), channel_id=1, replica_groups=mesh['ctx'=64,'kv'=8] {'ctx'}, dimensions={0} | all-to-all | bytes 524288 | tf_op jit(solution)/shard_map/all_to_all | solution.py:228
  118.6 0.8 copy.15
  (1 shorter events, 0.0 us)
Async XLA Ops:
  0.6 0.7 copy-start.6
  16.1 0.7 copy-start.5
  16.8 0.9 copy-start
  17.7 0.9 copy-start.2
  18.6 32.4 %copy-start.3 = (bf16[512,128]{1,0:T(8,128)(2,1)S(1)}, bf16[512,128]{1,0:T(8,128)(2,1)}, u32[]{:S(2)}) copy-start(bf16[512,128]{1,0:T(8,128)(2,1)} %values_ref.3) | copy-start | bytes 393220
  19.7 31.2 %copy-start.1 = (bf16[512,128]{1,0:T(8,128)(2,1)S(1)}, bf16[512,128]{1,0:T(8,128)(2,1)}, u32[]{:S(2)}) copy-start(bf16[512,128]{1,0:T(8,128)(2,1)} %keys_ref.3) | copy-start | bytes 393220
  19.7 31.2 %all-to-all-start = ((bf16[64,4,128]{2,1,0:T(4,128)(2,1)}), bf16[64,4,128]{2,1,0:T(4,128)(2,1)S(1)}, u32[]{:S(2)}, u32[]{:S(2)}) async-start(bf16[64,4,128]{2,1,0:T(4,128)(2,1)} %bitcast.3), calls=%async_computation | async-start | bytes 131072 | tf_op jit(solution)/shard_map/all_to_all | solution.py:211
  35.4 9.2 %collective-permute-start = (bf16[64,128]{1,0:T(8,128)(2,1)S(1)}, bf16[64,128]{1,0:T(8,128)(2,1)S(1)}, u32[]{:S(2)}, u32[]{:S(2)}) collective-permute-start(bf16[64,128]{1,0:T(8,128)(2,1)S(1)} %get-tuple-element.10), channel_id=1, source_target_pairs={{0,8},{8,16},{16,24},{24,32},{32,40},{40,48},{48,56},{56,64},{64,7... | collective-permute-start | bytes 49160 | tf_op jit(solution)/shard_map/ppermute | solution.py:209
  38.9 7.1 %collective-permute-start.1 = (bf16[64,128]{1,0:T(8,128)(2,1)S(1)}, bf16[64,128]{1,0:T(8,128)(2,1)S(1)}, u32[]{:S(2)}, u32[]{:S(2)}) collective-permute-start(bf16[64,128]{1,0:T(8,128)(2,1)S(1)} %get-tuple-element.11), channel_id=1, source_target_pairs={{0,504},{8,0},{16,8},{24,16},{32,24},{40,32},{48,40},{56,48},{64,5... | collective-permute-start | bytes 49160 | tf_op jit(solution)/shard_map/ppermute | solution.py:210
  50.9 1.0 copy-start.4

commit v2 on v1

v2 whole, which is shorter than its diff:
```python
import functools

import jax
import jax.numpy as jnp
from jax import lax
from jax.experimental import pallas as pl
from jax.experimental.pallas import tpu as pltpu
from jax.sharding import PartitionSpec as P

NEAR = 16
LANES = 128
TILE = 8
PIECES = 4
NOTES = 2
PEAK_PARTS = 3
SIZE_PARTS = 2
F32 = jnp.float32
BF16 = jnp.bfloat16


def rows_of(shape):
    return lax.broadcasted_iota(jnp.int32, shape, 0)


def lanes_of(shape):
    return lax.broadcasted_iota(jnp.int32, shape, 1)


def onehot(flags):
    return flags.astype(F32).astype(BF16)


def row_weight(importance):
    summed = jnp.sum(importance.astype(F32), axis=0).astype(BF16).astype(F32)
    return jnp.concatenate([summed[at : at + 1, :] for at in range(summed.shape[0])], axis=1)


def split_parts(value, count):
    parts = []
    for _ in range(count):
        rounded = value.astype(BF16).astype(F32)
        parts.append(rounded)
        value = value - rounded
    return parts


def peer_place(index, span):
    peer = index // span
    return peer, index - peer * span


def pull(sources, targets, semaphore):
    copies = [
        pltpu.make_async_copy(source, target, semaphore.at[at])
        for at, (source, target) in enumerate(zip(sources, targets))
    ]
    for copy in copies:
        copy.start()
    for copy in copies:
        copy.wait()


def destination(shards, shard, assignment, row_count):
    owner = assignment // row_count
    distance = owner - shard
    distance = jnp.where(distance < 0, distance + shards, distance)
    ahead = distance == 1
    back = distance == shards - 1
    side = rows_of((TILE, row_count))
    flags = jnp.where(side == 0, ahead.astype(F32), jnp.where(side == 1, back.astype(F32), 0.0)).astype(BF16)
    earlier = onehot(rows_of((row_count, row_count)) < lanes_of((row_count, row_count)))
    ranks = jnp.dot(flags, earlier, preferred_element_type=F32).astype(jnp.int32)
    rank = jnp.where(ahead, ranks[0:1, :], jnp.where(back, ranks[1:2, :], 0))
    peer = jnp.where(distance == 0, -1, owner)
    far_peer = jnp.where(ahead | back, -1, peer)
    return peer, far_peer, ahead, back, rank


def chosen_rows(shards, peer, far_peer, row_count):
    line = rows_of((PIECES * shards, row_count))
    return onehot(line // PIECES == jnp.where(line % PIECES == NOTES, peer, far_peer))


def rows_kernel(
    shards, shard_ref, assignment_hbm, keys_hbm, values_hbm, far_ref, ahead_ref, back_ref, peer_ref,
    assignment_ref, keys_ref, values_ref, semaphore,
):
    pull((assignment_hbm, keys_hbm, values_hbm), (assignment_ref, keys_ref, values_ref), semaphore)
    row_count = keys_ref.shape[0]
    assignment = assignment_ref[...]
    peer, far_peer, ahead, back, rank = destination(shards, shard_ref[0], assignment, row_count)
    rows = jnp.concatenate([keys_ref[...], values_ref[...]], axis=1)
    slot = jnp.where(ahead, rank, jnp.where(back, NEAR + rank, -1))
    near = jnp.dot(onehot(rows_of((2 * NEAR, row_count)) == slot), rows, preferred_element_type=F32).astype(BF16)
    ahead_ref[...] = jnp.concatenate([near[:NEAR, :LANES], near[:NEAR, LANES:]], axis=0)
    back_ref[...] = jnp.concatenate([near[NEAR:, :LANES], near[NEAR:, LANES:]], axis=0)
    chosen = chosen_rows(shards, peer, far_peer, row_count)
    picked = jnp.dot(chosen, rows, preferred_element_type=F32)
    target = assignment % row_count
    part = rows_of((LANES, row_count))
    place = jnp.where(
        part // NEAR == 1, (target // LANES).astype(F32), jnp.where(part // NEAR == 2, (target % LANES).astype(F32), 0.0)
    )
    notes = jnp.where(part % NEAR == rank, place, 0.0).astype(BF16)
    noted = lax.dot_general(chosen, notes, (((1,), (1,)), ((), ())), preferred_element_type=F32)
    piece = rows_of((PIECES * shards, LANES)) % PIECES
    far_ref[...] = jnp.where(
        piece == 0, picked[:, :LANES], jnp.where(piece == 1, picked[:, LANES:], jnp.where(piece == NOTES, noted, 0.0))
    ).astype(BF16)
    at = rows_of((TILE, row_count))
    peer_ref[...] = jnp.where(at == 0, peer, jnp.where(at == 1, far_peer, rank))


def weigh_kernel(shards, importance_ref, peer_ref, far_ref, out_ref):
    row_count = peer_ref.shape[1]
    weight = row_weight(importance_ref[...])
    peer, far_peer, rank = peer_ref[0:1, :], peer_ref[1:2, :], peer_ref[2:3, :]
    chosen = chosen_rows(shards, peer, far_peer, row_count)
    notes = jnp.where(rows_of((LANES, row_count)) == rank, weight, 0.0).astype(BF16)
    noted = lax.dot_general(chosen, notes, (((1,), (1,)), ((), ())), preferred_element_type=F32)
    piece = rows_of((PIECES * shards, LANES)) % PIECES
    out_ref[...] = (far_ref[...].astype(F32) + jnp.where(piece == NOTES, noted, 0.0)).astype(BF16)


def home_kernel(
    shards, shard_ref, importance_ref, assignment_hbm, keys_hbm, values_hbm, queries_hbm,
    sums_ref, total_ref, bias_ref, padded_ref, assignment_ref, keys_ref, values_ref, queries_ref, semaphore,
):
    pull(
        (assignment_hbm, keys_hbm, values_hbm, queries_hbm),
        (assignment_ref, keys_ref, values_ref, queries_ref),
        semaphore,
    )
    row_count, head_dim = keys_ref.shape
    shard = shard_ref[0]
    assignment = assignment_ref[...]
    weight = row_weight(importance_ref[...])
    target = jnp.where(assignment // row_count == shard, assignment % row_count, -1)
    index = lanes_of((1, row_count))
    kept = target == index
    line = rows_of((row_count, row_count))
    mix = jnp.where(target == line, weight, jnp.where((index == line) & jnp.logical_not(kept), 1.0, 0.0)).astype(BF16)
    rows = jnp.concatenate([keys_ref[...], values_ref[...]], axis=1)
    sums_ref[...] = jnp.dot(mix, rows, preferred_element_type=F32)
    total_ref[...] = jnp.dot(mix, jnp.ones((row_count, LANES), BF16), preferred_element_type=F32)
    bias_ref[...] = jnp.broadcast_to(jnp.where(kept, 0.0, -jnp.inf), bias_ref.shape)

    query_rows = queries_ref.shape[0]
    heads = queries_ref.shape[1] // head_dim
    per_peer = query_rows * heads // shards
    span = per_peer + 2
    group = per_peer * heads
    peers = group // per_peer
    peer, place = peer_place(rows_of((peers * span, group)), span)
    per_tile = heads * TILE // per_peer
    head = (peer % per_tile) * (per_peer // TILE) + place // TILE
    source = head * per_peer + (peer // per_tile) * TILE + place % TILE
    order = onehot((source == lanes_of((peers * span, group))) & (place < per_peer))
    for part in range(query_rows // per_peer):
        block = queries_ref[part * per_peer : (part + 1) * per_peer, :]
        block = jnp.concatenate([block[:, at * head_dim : (at + 1) * head_dim] for at in range(heads)], axis=0)
        moved = jnp.dot(order, block, preferred_element_type=F32).astype(BF16)
        padded_ref[part * peers * span : (part + 1) * peers * span, :] = moved


def attend_kernel(
    shards, shard_ref, sums_ref, total_ref, bias_ref, padded_ref, far_ref, from_back_ref, from_ahead_ref,
    merged_ref, partial_ref,
):
    row_count = sums_ref.shape[0]
    shard = shard_ref[0]
    back = jnp.where(shard == 0, shards - 1, shard - 1)
    ahead = jnp.where(shard == shards - 1, 0, shard + 1)
    far = far_ref[...]
    count = far.shape[0]
    notes = far.astype(F32).T
    lane = lanes_of((1, count))
    source = lane // PIECES
    is_far = (lane % PIECES == NOTES) & (source != back) & (source != ahead) & (source != shard)
    far_weight = notes[0:1, :]
    far_target = jnp.where(is_far, notes[NEAR : NEAR + 1, :] * LANES + notes[2 * NEAR : 2 * NEAR + 1, :], -1.0)

    line = rows_of((TILE, count))
    wanted = jnp.where(line == 0, back, ahead) * PIECES + NOTES
    picked = onehot((lanes_of((TILE, count)) == wanted) & (line < 2))
    near_notes = jnp.dot(picked, far, preferred_element_type=F32)
    near_target = (
        pltpu.roll(near_notes, LANES - NEAR, 1) * LANES + pltpu.roll(near_notes, LANES - 2 * NEAR, 1)
    )
    lane = lanes_of((1, LANES))
    second = (lane >= 2 * NEAR) & (lane < 3 * NEAR)
    shifted_notes = pltpu.roll(near_notes, 2 * NEAR, 1)
    shifted_target = pltpu.roll(near_target, 2 * NEAR, 1)
    near_weight = jnp.where(lane < NEAR, near_notes[0:1, :], shifted_notes[1:2, :])
    near_place = jnp.where(lane < NEAR, near_target[0:1, :], jnp.where(second, shifted_target[1:2, :], -1.0))

    line = rows_of((row_count, count + LANES))

    def mixing(far_shift, near_shift):
        def moved(value, shift):
            value = jnp.broadcast_to(value, (TILE, value.shape[1]))
            return pltpu.roll(value, shift, 1)[0:1, :] if shift else value[0:1, :]

        target = jnp.concatenate([moved(far_target, far_shift), moved(near_place, near_shift)], axis=1)
        weight = jnp.concatenate([moved(far_weight, far_shift), moved(near_weight, near_shift)], axis=1)
        return jnp.where(target.astype(jnp.int32) == line, weight, 0.0).astype(BF16)

    key_mix = mixing(count - NOTES, 0)
    value_mix = mixing(count - NOTES + 1, NEAR)
    arrived = jnp.concatenate(
        [far, from_back_ref[...], from_ahead_ref[...], jnp.zeros((LANES - 4 * NEAR, LANES), BF16)], axis=0
    )
    total = total_ref[...] + jnp.dot(key_mix, jnp.ones(arrived.shape, BF16), preferred_element_type=F32)
    merged_keys = (sums_ref[:, :LANES] + jnp.dot(key_mix, arrived, preferred_element_type=F32)) / total
    merged_values = (sums_ref[:, LANES:] + jnp.dot(value_mix, arrived, preferred_element_type=F32)) / total
    merged_keys = merged_keys.astype(BF16)
    merged_values = merged_values.astype(BF16)
    merged_ref[0] = merged_keys
    merged_ref[1] = merged_values

    span = padded_ref.shape[0] // shards
    per_peer = span - 2
    scale = LANES ** (-0.5)
    bias = bias_ref[0:1, :]
    group = TILE * span
    peer, place = peer_place(rows_of((group, LANES)), span)
    lane = lanes_of((group, LANES))
    part = lane // per_peer
    diagonal = place == lane % per_peer
    from_peer, from_place = peer_place(lanes_of((group, group)), span)
    to_peer, to_place = peer_place(rows_of((group, group)), span)
    gather = onehot((to_place == per_peer) & (from_peer == to_peer) & (from_place < per_peer))
    for at in range(0, padded_ref.shape[0], group):
        scores = lax.dot_general(
            padded_ref[at : at + group, :], merged_keys, (((1,), (1,)), ((), ())), preferred_element_type=F32
        )
        scores = scores * scale + bias
        peak = jnp.max(scores, axis=1, keepdims=True)
        prob = jnp.exp(scores - peak)
        size = jnp.sum(prob, axis=1, keepdims=True)
        sums = jnp.dot(prob.astype(BF16), merged_values, preferred_element_type=F32)
        stats = jnp.zeros((group, LANES), F32)
        for which, member in enumerate(split_parts(peak, PEAK_PARTS) + split_parts(size, SIZE_PARTS)):
            stats = jnp.where(part == which, member, stats)
        stats = jnp.where(diagonal, stats, 0.0).astype(BF16)
        stats = jnp.dot(gather, stats, preferred_element_type=F32)
        partial_ref[at : at + group, :] = jnp.where(place < per_peer, sums, stats).astype(BF16)


def combine_kernel(shards, partial_ref, finished_ref):
    count = partial_ref.shape[0]
    span = count // shards
    per_peer = span - 2
    partial = partial_ref[...]
    wide = (shards, count)
    picked = onehot(lanes_of(wide) == rows_of(wide) * span + per_peer)
    stats = jnp.dot(picked, partial, preferred_element_type=F32)

    def part(which):
        return pltpu.roll(stats, LANES - which * per_peer, 1) if which else stats

    valid = lanes_of((shards, LANES)) < per_peer
    peak = jnp.where(valid, (part(0) + part(1)) + part(2), 0.0)
    size = jnp.where(valid, part(3) + part(4), 1.0)
    rescale = jnp.exp(peak - jnp.max(peak, axis=0, keepdims=True))
    factor = rescale / jnp.sum(rescale * size, axis=0, keepdims=True)
    factor = jnp.concatenate([factor, jnp.zeros((LANES - shards, LANES), F32)], axis=0).T[:per_peer, :shards]
    factor = jnp.concatenate(split_parts(factor, 2), axis=0).astype(BF16)
    start = rows_of(wide) * span
    spread = onehot((lanes_of(wide) >= start) & (lanes_of(wide) < start + span))
    factor = jnp.dot(factor, spread, preferred_element_type=F32)
    unused, place = peer_place(lanes_of(factor.shape), span)
    factor = jnp.where(place == rows_of(factor.shape) % per_peer, factor, 0.0).astype(BF16)
    total = jnp.dot(factor, partial, preferred_element_type=F32)
    finished = (total[:per_peer] + total[per_peer:]).astype(BF16)
    for peer in range(shards):
        finished_ref[peer] = finished


SMEM = pl.BlockSpec(memory_space=pltpu.SMEM)
VMEM = pl.BlockSpec(memory_space=pltpu.VMEM)
ANY = pl.BlockSpec(memory_space=pl.ANY)


def run_kernel(body, shards, shapes, specs, operands, pulled=()):
    scratch = [pltpu.VMEM(member.shape, member.dtype) for member in pulled]
    if pulled:
        scratch.append(pltpu.SemaphoreType.DMA((len(pulled),)))
    return pl.pallas_call(
        functools.partial(body, shards),
        out_shape=[jax.ShapeDtypeStruct(shape, dtype) for shape, dtype in shapes],
        in_specs=specs,
        out_specs=[VMEM] * len(shapes),
        scratch_shapes=scratch,
        compiler_params=pltpu.CompilerParams(vmem_limit_bytes=24 * 1024 * 1024),
    )(*operands)


def per_device(cache_keys, cache_values, importance, assignment, queries):
    row_count, head_dim = cache_keys.shape
    query_rows = queries.shape[0]
    heads = queries.shape[1] // head_dim
    shards = lax.axis_size("ctx")
    groups = lax.axis_size("kv")
    per_peer = query_rows * heads // shards
    span = per_peer + 2
    shard = lax.axis_index("ctx").astype(jnp.int32).reshape(1)
    assignment = assignment.reshape(1, row_count)

    copies = jnp.broadcast_to(importance.reshape(1, row_count // LANES, LANES), (groups, row_count // LANES, LANES))
    importance = lax.all_to_all(copies, "kv", 0, 0, tiled=True)
    pulled = (assignment, cache_keys, cache_values)
    far, ahead, back, peer = run_kernel(
        rows_kernel,
        shards,
        [
            ((PIECES * shards, LANES), BF16),
            ((2 * NEAR, LANES), BF16),
            ((2 * NEAR, LANES), BF16),
            ((TILE, row_count), jnp.int32),
        ],
        [SMEM, ANY, ANY, ANY],
        (shard,) + pulled,
        pulled,
    )
    from_back = lax.ppermute(ahead, "ctx", [(i, (i + 1) % shards) for i in range(shards)])
    from_ahead = lax.ppermute(back, "ctx", [(i, (i - 1) % shards) for i in range(shards)])
    (far,) = run_kernel(
        weigh_kernel, shards, [((PIECES * shards, LANES), BF16)], [VMEM, VMEM, VMEM], (importance, peer, far)
    )
    far, importance = lax.optimization_barrier((far, importance))
    far = lax.all_to_all(far.reshape(shards, PIECES, LANES), "ctx", 0, 0, tiled=True)
    pulled = (assignment, cache_keys, cache_values, queries)
    sums, total, bias, padded = run_kernel(
        home_kernel,
        shards,
        [
            ((row_count, 2 * head_dim), F32),
            ((row_count, LANES), F32),
            ((TILE, row_count), F32),
            ((shards * span, head_dim), BF16),
        ],
        [SMEM, VMEM, ANY, ANY, ANY, ANY],
        (shard, importance) + pulled,
        pulled,
    )
    merged, partial = run_kernel(
        attend_kernel,
        shards,
        [((2, row_count, head_dim), BF16), ((shards * span, LANES), BF16)],
        [SMEM] + [VMEM] * 7,
        (shard, sums, total, bias, padded, far.reshape(shards * PIECES, LANES), from_back, from_ahead),
    )
    partial = lax.all_to_all(partial.reshape(shards, span // 2, 2, LANES), "ctx", 0, 0, tiled=True)
    merged_keys = merged[0]
    (finished,) = run_kernel(
        combine_kernel, shards, [((shards, per_peer, LANES), BF16)], [VMEM], (partial.reshape(shards * span, LANES),)
    )
    finished, merged = lax.optimization_barrier((finished, merged))
    finished = lax.all_to_all(finished, "ctx", 0, 0, tiled=True)
    merged_values = merged[1]
    tiles = query_rows // TILE
    attended = finished.reshape(tiles, heads, TILE, head_dim).transpose(0, 2, 1, 3)
    return (merged_keys, merged_values, attended.reshape(query_rows, heads * head_dim))


def solution(mesh):
    placed = (P("ctx", "kv"), P("ctx", "kv"), P("kv", "ctx"), P("ctx"), P(None, "kv"))
    return jax.shard_map(
        per_device,
        mesh=mesh,
        in_specs=placed,
        out_specs=(P("ctx", "kv"), P("ctx", "kv"), P(None, "kv")),
        check_vma=False,
    )
```

time: 120 us -> 111 us (0.925)
  the two profiles are of different devices: /device:TPU:2 before, /device:TPU:4 now
where the time goes in v2:
time: 111 us; the launch traced here: 110 us
  starting transfers between devices  37.5 us (34%)
  blocking collectives  32.9 us (30%)
  waiting for transfers between devices  25.5 us (23%)
  Pallas kernels  8 us (7%)
  local copies, waits for them, and re-layouts  5.14 us (5%)
    all_to_all x1, blocking collectives, per_device(): lax.all_to_all(partial.reshape(shards, span // 2, 2, LANES), 'ctx', 0, 0,...  32.9 us
    all_to_all x1, waiting for transfers between devices, per_device(): finished = lax.all_to_all(finished, 'ctx', 0, 0, tiled=True)  20.4 us
    all_to_all x1, starting transfers between devices, per_device(): lax.all_to_all(far.reshape(shards, PIECES, LANES), 'ctx', 0, 0, tiled=True)  14.4 us
    all_to_all x1, starting transfers between devices, per_device(): importance = lax.all_to_all(copies, 'kv', 0, 0, tiled=True)  9.14 us
    pallas_call x5, Pallas kernels, run_kernel(): pl.pallas_call(functools.partial(body, shards), out_shape=[jax.ShapeDtype...  8 us
    ppermute x1, starting transfers between devices, per_device(): lax.ppermute(back, 'ctx', [(i, (i - 1) % shards) for i in range(shards)])  5.68 us
    all_to_all x1, waiting for transfers between devices, per_device(): lax.all_to_all(far.reshape(shards, PIECES, LANES), 'ctx', 0, 0, tiled=True)  4.83 us
    all_to_all x1, starting transfers between devices, per_device(): finished = lax.all_to_all(finished, 'ctx', 0, 0, tiled=True)  4.8 us
  transfers between devices with their start and end apart: 5, of which 3 were waited for; matrix products, arithmetic and copies ran while one was open for 1% of the time, Pallas kernels for 2%

profile of v2, /device:TPU:4, one launch (start us, length us, event | category | flops | bytes accessed | tf_op | source)
XLA Modules:
  0.0 110.5 jit_solution(7147288832696674006)
XLA Ops:
  0.6 0.7 reduce
  1.3 0.6 broadcast_in_dim.8
  1.9 9.1 %all-to-all-start = ((bf16[8,4,128]{2,1,0:T(4,128)(2,1)}), bf16[8,4,128]{2,1,0:T(4,128)(2,1)S(1)}, u32[]{:S(2)}, u32[]{:S(2)}) async-start(bf16[8,4,128]{2,1,0:T(4,128)(2,1)} %broadcast_in_dim.8), calls=%async_computation | async-start | bytes 16384 | tf_op jit(solution)/shard_map/all_to_all | solution.py:311
  11.1 0.0 copy-start.5
  11.1 0.7 copy-done.5
  11.8 0.0 copy-start
  11.8 0.9 copy-done
  12.7 0.0 copy-start.2
  12.7 0.9 copy-done.2
  13.6 0.8 shard_map.76
  14.4 0.0 all-to-all-done.importance_ref
  14.4 0.0 copy-start.1
  14.4 0.0 copy-start.3
  14.5 0.9 shard_map.77
  15.3 14.4 %all-to-all-start.1 = ((bf16[64,4,128]{2,1,0:T(4,128)(2,1)}), bf16[64,4,128]{2,1,0:T(4,128)(2,1)S(1)}, u32[]{:S(2)}, u32[]{:S(2)}) async-start(bf16[64,4,128]{2,1,0:T(4,128)(2,1)} %bitcast.2), calls=%async_computation.1 | async-start | bytes 131072 | tf_op jit(solution)/shard_map/all_to_all | solution.py:332
  29.7 3.5 %collective-permute-start = (bf16[32,128]{1,0:T(8,128)(2,1)S(1)}, bf16[32,128]{1,0:T(8,128)(2,1)S(1)}, u32[]{:S(2)}, u32[]{:S(2)}) collective-permute-start(bf16[32,128]{1,0:T(8,128)(2,1)S(1)} %get-tuple-element.25), channel_id=1, source_target_pairs={{0,8},{8,16},{16,24},{24,32},{32,40},{40,48},{48,56},{56,64},{64,7... | collective-permute-start | bytes 24584 | tf_op jit(solution)/shard_map/ppermute | solution.py:326
  33.2 5.7 %collective-permute-start.1 = (bf16[32,128]{1,0:T(8,128)(2,1)S(1)}, bf16[32,128]{1,0:T(8,128)(2,1)S(1)}, u32[]{:S(2)}, u32[]{:S(2)}) collective-permute-start(bf16[32,128]{1,0:T(8,128)(2,1)S(1)} %get-tuple-element.26), channel_id=1, source_target_pairs={{0,504},{8,0},{16,8},{24,16},{32,24},{40,32},{48,40},{56,48},{64,5... | collective-permute-start | bytes 24584 | tf_op jit(solution)/shard_map/ppermute | solution.py:327
  38.9 0.0 copy-done.4
  38.9 0.0 copy-done.1
  38.9 0.0 copy-done.3
  38.9 1.1 shard_map.78
  40.0 0.0 collective-permute-done.from_back_ref
  40.0 0.2 collective-permute-done.1.from_ahead_ref
  40.3 4.8 %all-to-all-done.1 = bf16[64,4,128]{2,1,0:T(4,128)(2,1)S(1)} async-done(((bf16[64,4,128]{2,1,0:T(4,128)(2,1)}), bf16[64,4,128]{2,1,0:T(4,128)(2,1)S(1)}, u32[]{:S(2)}, u32[]{:S(2)}) %all-to-all-start.1) | async-done | bytes 65568 | tf_op jit(solution)/shard_map/all_to_all | solution.py:332
  45.1 3.8 %shard_map.79 = (bf16[2,512,128]{2,1,0:T(8,128)(2,1)S(1)}, bf16[1152,128]{1,0:T(8,128)(2,1)S(1)}) custom-call(s32[1]{0:T(128)} %bitcast.shard_ref, f32[512,256]{1,0:T(8,128)S(1)} %get-tuple-element.20.sums_ref, f32[512,128]{1,0:T(8,128)S(1)} %get-tuple-element.21.total_ref, f32[8,512]{1,0:T(8,128)S(1)} %get-tuple-element.22.bias_ref, ...), custom_call_target="tpu_custom_call" | custom-call | tf_op jit(solution)/shard_map/pallas_call | solution.py:289
  48.9 32.9 %all_to_all.20 = bf16[64,9,2,128]{3,2,1,0:T(2,128)(2,1)S(1)} all-to-all(bf16[64,9,2,128]{3,2,1,0:T(2,128)(2,1)S(1)} %bitcast.17), channel_id=1, replica_groups=mesh['ctx'=64,'kv'=8] {'ctx'}, dimensions={0} | all-to-all | bytes 589824 | tf_op jit(solution)/shard_map/all_to_all | solution.py:354
  81.8 1.4 %shard_map.80 = bf16[64,16,128]{2,1,0:T(8,128)(2,1)} custom-call(bf16[1152,128]{1,0:T(8,128)(2,1)S(1)} %bitcast.16), custom_call_target="tpu_custom_call" | custom-call | tf_op jit(solution)/shard_map/pallas_call | solution.py:289
  83.2 4.8 %all-to-all-start.3 = ((bf16[64,16,128]{2,1,0:T(8,128)(2,1)}), bf16[64,16,128]{2,1,0:T(8,128)(2,1)S(1)}, u32[]{:S(2)}, u32[]{:S(2)}) async-start(bf16[64,16,128]{2,1,0:T(8,128)(2,1)} %shard_map.80), calls=%async_computation.3 | async-start | bytes 524288 | tf_op jit(solution)/shard_map/all_to_all | solution.py:360
  88.0 0.7 slice_bitcast_fusion.1
  88.7 0.7 slice_bitcast_fusion
  89.4 20.4 %all-to-all-done.3 = bf16[64,16,128]{2,1,0:T(8,128)(2,1)S(1)} async-done(((bf16[64,16,128]{2,1,0:T(8,128)(2,1)}), bf16[64,16,128]{2,1,0:T(8,128)(2,1)S(1)}, u32[]{:S(2)}, u32[]{:S(2)}) %all-to-all-start.3) | async-done | bytes 262176 | tf_op jit(solution)/shard_map/all_to_all | solution.py:360
  109.8 0.7 copy.9
  (1 shorter events, 0.0 us)
Async XLA Ops:
  1.9 12.5 %all-to-all-start = ((bf16[8,4,128]{2,1,0:T(4,128)(2,1)}), bf16[8,4,128]{2,1,0:T(4,128)(2,1)S(1)}, u32[]{:S(2)}, u32[]{:S(2)}) async-start(bf16[8,4,128]{2,1,0:T(4,128)(2,1)} %broadcast_in_dim.8), calls=%async_computation | async-start | bytes 16384 | tf_op jit(solution)/shard_map/all_to_all | solution.py:311
  11.1 0.7 copy-start.5
  11.8 0.9 copy-start
  12.7 0.9 copy-start.2
  13.6 25.4 %copy-start.4 = (bf16[128,1024]{1,0:T(8,128)(2,1)S(1)}, bf16[128,1024]{1,0:T(8,128)(2,1)}, u32[]{:S(2)}) copy-start(bf16[128,1024]{1,0:T(8,128)(2,1)} %queries_hbm.1) | copy-start | bytes 786436
  14.4 24.5 %copy-start.1 = (bf16[512,128]{1,0:T(8,128)(2,1)S(1)}, bf16[512,128]{1,0:T(8,128)(2,1)}, u32[]{:S(2)}) copy-start(bf16[512,128]{1,0:T(8,128)(2,1)} %keys_hbm.3) | copy-start | bytes 393220
  14.4 24.5 %copy-start.3 = (bf16[512,128]{1,0:T(8,128)(2,1)S(1)}, bf16[512,128]{1,0:T(8,128)(2,1)}, u32[]{:S(2)}) copy-start(bf16[512,128]{1,0:T(8,128)(2,1)} %values_hbm.3) | copy-start | bytes 393220
  15.3 29.8 %all-to-all-start.1 = ((bf16[64,4,128]{2,1,0:T(4,128)(2,1)}), bf16[64,4,128]{2,1,0:T(4,128)(2,1)S(1)}, u32[]{:S(2)}, u32[]{:S(2)}) async-start(bf16[64,4,128]{2,1,0:T(4,128)(2,1)} %bitcast.2), calls=%async_computation.1 | async-start | bytes 131072 | tf_op jit(solution)/shard_map/all_to_all | solution.py:332
  29.7 10.3 %collective-permute-start = (bf16[32,128]{1,0:T(8,128)(2,1)S(1)}, bf16[32,128]{1,0:T(8,128)(2,1)S(1)}, u32[]{:S(2)}, u32[]{:S(2)}) collective-permute-start(bf16[32,128]{1,0:T(8,128)(2,1)S(1)} %get-tuple-element.25), channel_id=1, source_target_pairs={{0,8},{8,16},{16,24},{24,32},{32,40},{40,48},{48,56},{56,64},{64,7... | collective-permute-start | bytes 24584 | tf_op jit(solution)/shard_map/ppermute | solution.py:326
  33.2 7.0 %collective-permute-start.1 = (bf16[32,128]{1,0:T(8,128)(2,1)S(1)}, bf16[32,128]{1,0:T(8,128)(2,1)S(1)}, u32[]{:S(2)}, u32[]{:S(2)}) collective-permute-start(bf16[32,128]{1,0:T(8,128)(2,1)S(1)} %get-tuple-element.26), channel_id=1, source_target_pairs={{0,504},{8,0},{16,8},{24,16},{32,24},{40,32},{48,40},{56,48},{64,5... | collective-permute-start | bytes 24584 | tf_op jit(solution)/shard_map/ppermute | solution.py:327
  83.2 26.6 %all-to-all-start.3 = ((bf16[64,16,128]{2,1,0:T(8,128)(2,1)}), bf16[64,16,128]{2,1,0:T(8,128)(2,1)S(1)}, u32[]{:S(2)}, u32[]{:S(2)}) async-start(bf16[64,16,128]{2,1,0:T(8,128)(2,1)} %shard_map.80), calls=%async_computation.3 | async-start | bytes 524288 | tf_op jit(solution)/shard_map/all_to_all | solution.py:360

commit v3 on v2

--- a/solution.py
+++ b/solution.py
@@ -44,9 +44,20 @@
     return parts
 
 
+def divided(index, size):
+    if size & (size - 1):
+        return (index * (-(-(1 << 16) // size))) >> 16
+    return index >> (size.bit_length() - 1)
+
+
+def remainder(index, size):
+    if size & (size - 1):
+        return index - divided(index, size) * size
+    return index & (size - 1)
+
+
 def peer_place(index, span):
-    peer = index // span
-    return peer, index - peer * span
+    return divided(index, span), remainder(index, span)
 
 
 def pull(sources, targets, semaphore):
@@ -61,7 +72,7 @@
 
 
 def destination(shards, shard, assignment, row_count):
-    owner = assignment // row_count
+    owner = divided(assignment, row_count)
     distance = owner - shard
     distance = jnp.where(distance < 0, distance + shards, distance)
     ahead = distance == 1
@@ -78,7 +89,17 @@
 
 def chosen_rows(shards, peer, far_peer, row_count):
     line = rows_of((PIECES * shards, row_count))
-    return onehot(line // PIECES == jnp.where(line % PIECES == NOTES, peer, far_peer))
+    return onehot(divided(line, PIECES) == jnp.where(remainder(line, PIECES) == NOTES, peer, far_peer))
+
+
+def copy_kernel(shards, importance_ref, copies_ref):
+    importance = importance_ref[...].astype(F32)
+    slices = importance.shape[1] // LANES
+    place = remainder(rows_of(copies_ref.shape), slices)
+    copies = jnp.zeros(copies_ref.shape, F32)
+    for at in range(slices):
+        copies = jnp.where(place == at, importance[:, at * LANES : (at + 1) * LANES], copies)
+    copies_ref[...] = copies.astype(BF16)
 
 
 def rows_kernel(
@@ -96,14 +117,16 @@
     back_ref[...] = jnp.concatenate([near[NEAR:, :LANES], near[NEAR:, LANES:]], axis=0)
     chosen = chosen_rows(shards, peer, far_peer, row_count)
     picked = jnp.dot(chosen, rows, preferred_element_type=F32)
-    target = assignment % row_count
+    target = remainder(assignment, row_count)
     part = rows_of((LANES, row_count))
     place = jnp.where(
-        part // NEAR == 1, (target // LANES).astype(F32), jnp.where(part // NEAR == 2, (target % LANES).astype(F32), 0.0)
-    )
-    notes = jnp.where(part % NEAR == rank, place, 0.0).astype(BF16)
+        divided(part, NEAR) == 1,
+        divided(target, LANES).astype(F32),
+        jnp.where(divided(part, NEAR) == 2, remainder(target, LANES).astype(F32), 0.0),
+    )
+    notes = jnp.where(remainder(part, NEAR) == rank, place, 0.0).astype(BF16)
     noted = lax.dot_general(chosen, notes, (((1,), (1,)), ((), ())), preferred_element_type=F32)
-    piece = rows_of((PIECES * shards, LANES)) % PIECES
+    piece = remainder(rows_of((PIECES * shards, LANES)), PIECES)
     far_ref[...] = jnp.where(
         piece == 0, picked[:, :LANES], jnp.where(piece == 1, picked[:, LANES:], jnp.where(piece == NOTES, noted, 0.0))
     ).astype(BF16)
@@ -118,7 +141,7 @@
     chosen = chosen_rows(shards, peer, far_peer, row_count)
     notes = jnp.where(rows_of((LANES, row_count)) == rank, weight, 0.0).astype(BF16)
     noted = lax.dot_general(chosen, notes, (((1,), (1,)), ((), ())), preferred_element_type=F32)
-    piece = rows_of((PIECES * shards, LANES)) % PIECES
+    piece = remainder(rows_of((PIECES * shards, LANES)), PIECES)
     out_ref[...] = (far_ref[...].astype(F32) + jnp.where(piece == NOTES, noted, 0.0)).astype(BF16)
 
 
@@ -135,7 +158,7 @@
     shard = shard_ref[0]
     assignment = assignment_ref[...]
     weight = row_weight(importance_ref[...])
-    target = jnp.where(assignment // row_count == shard, assignment % row_count, -1)
+    target = jnp.where(divided(assignment, row_count) == shard, remainder(assignment, row_count), -1)
     index = lanes_of((1, row_count))
     kept = target == index
     line = rows_of((row_count, row_count))
@@ -153,8 +176,8 @@
     peers = group // per_peer
     peer, place = peer_place(rows_of((peers * span, group)), span)
     per_tile = heads * TILE // per_peer
-    head = (peer % per_tile) * (per_peer // TILE) + place // TILE
-    source = head * per_peer + (peer // per_tile) * TILE + place % TILE
+    head = remainder(peer, per_tile) * (per_peer // TILE) + divided(place, TILE)
+    source = head * per_peer + divided(peer, per_tile) * TILE + remainder(place, TILE)
     order = onehot((source == lanes_of((peers * span, group))) & (place < per_peer))
     for part in range(query_rows // per_peer):
         block = queries_ref[part * per_peer : (part + 1) * per_peer, :]
@@ -175,8 +198,8 @@
     count = far.shape[0]
     notes = far.astype(F32).T
     lane = lanes_of((1, count))
-    source = lane // PIECES
-    is_far = (lane % PIECES == NOTES) & (source != back) & (source != ahead) & (source != shard)
+    source = divided(lane, PIECES)
+    is_far = (remainder(lane, PIECES) == NOTES) & (source != back) & (source != ahead) & (source != shard)
     far_weight = notes[0:1, :]
     far_target = jnp.where(is_far, notes[NEAR : NEAR + 1, :] * LANES + notes[2 * NEAR : 2 * NEAR + 1, :], -1.0)
 
@@ -225,8 +248,8 @@
     group = TILE * span
     peer, place = peer_place(rows_of((group, LANES)), span)
     lane = lanes_of((group, LANES))
-    part = lane // per_peer
-    diagonal = place == lane % per_peer
+    part = divided(lane, per_peer)
+    diagonal = place == remainder(lane, per_peer)
     from_peer, from_place = peer_place(lanes_of((group, group)), span)
     to_peer, to_place = peer_place(rows_of((group, group)), span)
     gather = onehot((to_place == per_peer) & (from_peer == to_peer) & (from_place < per_peer))
@@ -270,7 +293,7 @@
     spread = onehot((lanes_of(wide) >= start) & (lanes_of(wide) < start + span))
     factor = jnp.dot(factor, spread, preferred_element_type=F32)
     unused, place = peer_place(lanes_of(factor.shape), span)
-    factor = jnp.where(place == rows_of(factor.shape) % per_peer, factor, 0.0).astype(BF16)
+    factor = jnp.where(place == remainder(rows_of(factor.shape), per_peer), factor, 0.0).astype(BF16)
     total = jnp.dot(factor, partial, preferred_element_type=F32)
     finished = (total[:per_peer] + total[per_peer:]).astype(BF16)
     for peer in range(shards):
@@ -307,8 +330,9 @@
     shard = lax.axis_index("ctx").astype(jnp.int32).reshape(1)
     assignment = assignment.reshape(1, row_count)
 
-    copies = jnp.broadcast_to(importance.reshape(1, row_count // LANES, LANES), (groups, row_count // LANES, LANES))
-    importance = lax.all_to_all(copies, "kv", 0, 0, tiled=True)
+    slices = row_count // LANES
+    (copies,) = run_kernel(copy_kernel, shards, [((groups * slices, LANES), BF16)], [VMEM], (importance,))
+    importance = lax.all_to_all(copies.reshape(groups, slices, LANES), "kv", 0, 0, tiled=True)
     pulled = (assignment, cache_keys, cache_values)
     far, ahead, back, peer = run_kernel(
         rows_kernel,
@@ -356,7 +380,7 @@
     (finished,) = run_kernel(
         combine_kernel, shards, [((shards, per_peer, LANES), BF16)], [VMEM], (partial.reshape(shards * span, LANES),)
     )
-    finished, merged = lax.optimization_barrier((finished, merged))
+    finished, merged, merged_keys = lax.optimization_barrier((finished, merged, merged_keys))
     finished = lax.all_to_all(finished, "ctx", 0, 0, tiled=True)
     merged_values = merged[1]
     tiles = query_rows // TILE

time: 111 us -> 112 us (level)
  blocking collectives: 32.9 us -> 0 us
  waiting for transfers between devices: 25.5 us -> 47.9 us
  starting transfers between devices: 37.5 us -> 48.3 us
  Pallas kernels: 8 us -> 9.29 us
    all_to_all x1 -> x0, blocking collectives: 32.9 us -> none  [per_device(): lax.all_to_all(partial.reshape(shards, span // 2, 2, LANES), 'ctx', 0, 0,...]
    all_to_all x1 -> x2, waiting for transfers between devices: 0.01 us -> 21.7 us  [the longest x1 21.7 us: per_device(): lax.all_to_all(partial.reshape(shards, span // 2, 2, LANES), 'ctx', 0, 0,...]
    all_to_all x1 -> x2, starting transfers between devices: 9.14 us -> 19.9 us  [the longest x1 10.8 us: per_device(): lax.all_to_all(partial.reshape(shards, span // 2, 2, LANES), 'ctx', 0, 0,...]
    pallas_call x5 -> x6, Pallas kernels: 8 us -> 9.29 us  [run_kernel(): pl.pallas_call(functools.partial(body, shards), out_shape=[jax.ShapeDtype...]
    unnamed x13 -> x15, local copies, waits for them, and re-layouts: 3.21 us -> 3.88 us
  transfers between devices with their start and end apart: 5 -> 6, of which waited for: 3 -> 4; matrix products, arithmetic and copies ran while one was open for 1% -> 1% of each run, Pallas kernels for 2% -> 2%
where the time goes in v3:
time: 112 us; the launch traced here: 111 us
  starting transfers between devices  48.3 us (43%)
  waiting for transfers between devices  47.9 us (43%)
  Pallas kernels  9.29 us (8%)
  local copies, waits for them, and re-layouts  5.21 us (5%)
    all_to_all x1, waiting for transfers between devices, per_device(): lax.all_to_all(partial.reshape(shards, span // 2, 2, LANES), 'ctx', 0, 0,...  21.7 us
    all_to_all x1, waiting for transfers between devices, per_device(): finished = lax.all_to_all(finished, 'ctx', 0, 0, tiled=True)  21.1 us
    all_to_all x1, starting transfers between devices, per_device(): lax.all_to_all(far.reshape(shards, PIECES, LANES), 'ctx', 0, 0, tiled=True)  14.4 us
    all_to_all x1, starting transfers between devices, per_device(): lax.all_to_all(partial.reshape(shards, span // 2, 2, LANES), 'ctx', 0, 0,...  10.8 us
    pallas_call x6, Pallas kernels, run_kernel(): pl.pallas_call(functools.partial(body, shards), out_shape=[jax.ShapeDtype...  9.29 us
    all_to_all x1, starting transfers between devices, per_device(): lax.all_to_all(copies.reshape(groups, slices, LANES), 'kv', 0, 0, tiled=T...  9.14 us
    ppermute x1, starting transfers between devices, per_device(): lax.ppermute(back, 'ctx', [(i, (i - 1) % shards) for i in range(shards)])  5.68 us
    all_to_all x1, waiting for transfers between devices, per_device(): lax.all_to_all(far.reshape(shards, PIECES, LANES), 'ctx', 0, 0, tiled=True)  4.83 us
  transfers between devices with their start and end apart: 6, of which 4 were waited for; matrix products, arithmetic and copies ran while one was open for 1% of the time, Pallas kernels for 2%

profile of v3, /device:TPU:4, one launch (start us, length us, event | category | flops | bytes accessed | tf_op | source)
XLA Modules:
  0.0 111.4 jit_solution(16650684027718729664)
XLA Ops:
  0.6 0.0 copy-start.6
  0.6 0.7 copy-done.6
  1.3 0.6 shard_map.76
  1.9 9.1 %all-to-all-start = ((bf16[8,4,128]{2,1,0:T(4,128)(2,1)}), bf16[8,4,128]{2,1,0:T(4,128)(2,1)S(1)}, u32[]{:S(2)}, u32[]{:S(2)}) async-start(bf16[8,4,128]{2,1,0:T(4,128)(2,1)} %bitcast.1), calls=%async_computation | async-start | bytes 16384 | tf_op jit(solution)/shard_map/all_to_all | solution.py:335
  11.1 0.0 copy-start.5
  11.1 0.7 copy-done.5
  11.7 0.9 copy-done
  12.6 0.9 copy-done.2
  13.6 0.9 shard_map.77
  14.4 0.0 all-to-all-done.importance_ref
  14.5 0.0 copy-start.1
  14.5 0.0 copy-start.3
  14.5 0.9 shard_map.78
  15.4 14.4 %all-to-all-start.1 = ((bf16[64,4,128]{2,1,0:T(4,128)(2,1)}), bf16[64,4,128]{2,1,0:T(4,128)(2,1)S(1)}, u32[]{:S(2)}, u32[]{:S(2)}) async-start(bf16[64,4,128]{2,1,0:T(4,128)(2,1)} %bitcast.3), calls=%async_computation.1 | async-start | bytes 131072 | tf_op jit(solution)/shard_map/all_to_all | solution.py:356
  29.8 3.5 %collective-permute-start = (bf16[32,128]{1,0:T(8,128)(2,1)S(1)}, bf16[32,128]{1,0:T(8,128)(2,1)S(1)}, u32[]{:S(2)}, u32[]{:S(2)}) collective-permute-start(bf16[32,128]{1,0:T(8,128)(2,1)S(1)} %get-tuple-element.26), channel_id=1, source_target_pairs={{0,8},{8,16},{16,24},{24,32},{32,40},{40,48},{48,56},{56,64},{64,7... | collective-permute-start | bytes 24584 | tf_op jit(solution)/shard_map/ppermute | solution.py:350
  33.3 5.7 %collective-permute-start.1 = (bf16[32,128]{1,0:T(8,128)(2,1)S(1)}, bf16[32,128]{1,0:T(8,128)(2,1)S(1)}, u32[]{:S(2)}, u32[]{:S(2)}) collective-permute-start(bf16[32,128]{1,0:T(8,128)(2,1)S(1)} %get-tuple-element.27), channel_id=1, source_target_pairs={{0,504},{8,0},{16,8},{24,16},{32,24},{40,32},{48,40},{56,48},{64,5... | collective-permute-start | bytes 24584 | tf_op jit(solution)/shard_map/ppermute | solution.py:351
  38.9 0.0 copy-done.4
  39.0 0.0 copy-done.1
  39.0 0.0 copy-done.3
  39.0 1.0 shard_map.79
  40.0 0.0 collective-permute-done.from_back_ref
  40.0 0.3 collective-permute-done.1.from_ahead_ref
  40.3 4.8 %all-to-all-done.1 = bf16[64,4,128]{2,1,0:T(4,128)(2,1)S(1)} async-done(((bf16[64,4,128]{2,1,0:T(4,128)(2,1)}), bf16[64,4,128]{2,1,0:T(4,128)(2,1)S(1)}, u32[]{:S(2)}, u32[]{:S(2)}) %all-to-all-start.1) | async-done | bytes 65568 | tf_op jit(solution)/shard_map/all_to_all | solution.py:356
  45.1 4.5 %shard_map.80 = (bf16[2,512,128]{2,1,0:T(8,128)(2,1)S(1)}, bf16[1152,128]{1,0:T(8,128)(2,1)}) custom-call(s32[1]{0:T(128)} %bitcast.shard_ref, f32[512,256]{1,0:T(8,128)S(1)} %get-tuple-element.21.sums_ref, f32[512,128]{1,0:T(8,128)S(1)} %get-tuple-element.22.total_ref, f32[8,512]{1,0:T(8,128)S(1)} %get-tuple-element.23.bias_ref, ...), custom_call_target="tpu_custom_call" | custom-call | tf_op jit(solution)/shard_map/pallas_call | solution.py:312
  49.6 10.8 %all-to-all-start.2 = ((bf16[64,9,2,128]{3,2,1,0:T(2,128)(2,1)}), bf16[64,9,2,128]{3,2,1,0:T(2,128)(2,1)S(1)}, u32[]{:S(2)}, u32[]{:S(2)}) async-start(bf16[64,9,2,128]{3,2,1,0:T(2,128)(2,1)} %bitcast.5), calls=%async_computation.2 | async-start | bytes 589824 | tf_op jit(solution)/shard_map/all_to_all | solution.py:378
  60.4 0.7 slice_bitcast_fusion.1
  61.1 21.7 %all-to-all-done.2 = bf16[64,9,2,128]{3,2,1,0:T(2,128)(2,1)S(1)} async-done(((bf16[64,9,2,128]{3,2,1,0:T(2,128)(2,1)}), bf16[64,9,2,128]{3,2,1,0:T(2,128)(2,1)S(1)}, u32[]{:S(2)}, u32[]{:S(2)}) %all-to-all-start.2) | async-done | bytes 294944 | tf_op jit(solution)/shard_map/all_to_all | solution.py:378
  82.8 1.4 %shard_map.81 = bf16[64,16,128]{2,1,0:T(8,128)(2,1)} custom-call(bf16[1152,128]{1,0:T(8,128)(2,1)S(1)} %bitcast.16), custom_call_target="tpu_custom_call" | custom-call | tf_op jit(solution)/shard_map/pallas_call | solution.py:312
  84.2 4.8 %all-to-all-start.3 = ((bf16[64,16,128]{2,1,0:T(8,128)(2,1)}), bf16[64,16,128]{2,1,0:T(8,128)(2,1)S(1)}, u32[]{:S(2)}, u32[]{:S(2)}) async-start(bf16[64,16,128]{2,1,0:T(8,128)(2,1)} %shard_map.81), calls=%async_computation.3 | async-start | bytes 524288 | tf_op jit(solution)/shard_map/all_to_all | solution.py:384
  89.0 0.7 slice_bitcast_fusion
  89.6 21.1 %all-to-all-done.3 = bf16[64,16,128]{2,1,0:T(8,128)(2,1)S(1)} async-done(((bf16[64,16,128]{2,1,0:T(8,128)(2,1)}), bf16[64,16,128]{2,1,0:T(8,128)(2,1)S(1)}, u32[]{:S(2)}, u32[]{:S(2)}) %all-to-all-start.3) | async-done | bytes 262176 | tf_op jit(solution)/shard_map/all_to_all | solution.py:384
  110.7 0.7 copy.9
  (3 shorter events, 0.0 us)
Async XLA Ops:
  0.6 0.7 copy-start.6
  1.9 12.5 %all-to-all-start = ((bf16[8,4,128]{2,1,0:T(4,128)(2,1)}), bf16[8,4,128]{2,1,0:T(4,128)(2,1)S(1)}, u32[]{:S(2)}, u32[]{:S(2)}) async-start(bf16[8,4,128]{2,1,0:T(4,128)(2,1)} %bitcast.1), calls=%async_computation | async-start | bytes 16384 | tf_op jit(solution)/shard_map/all_to_all | solution.py:335
  11.1 0.7 copy-start.5
  11.7 0.9 copy-start
  12.6 0.9 copy-start.2
  13.5 25.4 %copy-start.4 = (bf16[128,1024]{1,0:T(8,128)(2,1)S(1)}, bf16[128,1024]{1,0:T(8,128)(2,1)}, u32[]{:S(2)}) copy-start(bf16[128,1024]{1,0:T(8,128)(2,1)} %queries_hbm.1) | copy-start | bytes 786436
  14.5 24.5 %copy-start.1 = (bf16[512,128]{1,0:T(8,128)(2,1)S(1)}, bf16[512,128]{1,0:T(8,128)(2,1)}, u32[]{:S(2)}) copy-start(bf16[512,128]{1,0:T(8,128)(2,1)} %keys_hbm.3) | copy-start | bytes 393220
  14.5 24.5 %copy-start.3 = (bf16[512,128]{1,0:T(8,128)(2,1)S(1)}, bf16[512,128]{1,0:T(8,128)(2,1)}, u32[]{:S(2)}) copy-start(bf16[512,128]{1,0:T(8,128)(2,1)} %values_hbm.3) | copy-start | bytes 393220
  15.4 29.8 %all-to-all-start.1 = ((bf16[64,4,128]{2,1,0:T(4,128)(2,1)}), bf16[64,4,128]{2,1,0:T(4,128)(2,1)S(1)}, u32[]{:S(2)}, u32[]{:S(2)}) async-start(bf16[64,4,128]{2,1,0:T(4,128)(2,1)} %bitcast.3), calls=%async_computation.1 | async-start | bytes 131072 | tf_op jit(solution)/shard_map/all_to_all | solution.py:356
  29.8 10.2 %collective-permute-start = (bf16[32,128]{1,0:T(8,128)(2,1)S(1)}, bf16[32,128]{1,0:T(8,128)(2,1)S(1)}, u32[]{:S(2)}, u32[]{:S(2)}) collective-permute-start(bf16[32,128]{1,0:T(8,128)(2,1)S(1)} %get-tuple-element.26), channel_id=1, source_target_pairs={{0,8},{8,16},{16,24},{24,32},{32,40},{40,48},{48,56},{56,64},{64,7... | collective-permute-start | bytes 24584 | tf_op jit(solution)/shard_map/ppermute | solution.py:350
  33.3 7.0 %collective-permute-start.1 = (bf16[32,128]{1,0:T(8,128)(2,1)S(1)}, bf16[32,128]{1,0:T(8,128)(2,1)S(1)}, u32[]{:S(2)}, u32[]{:S(2)}) collective-permute-start(bf16[32,128]{1,0:T(8,128)(2,1)S(1)} %get-tuple-element.27), channel_id=1, source_target_pairs={{0,504},{8,0},{16,8},{24,16},{32,24},{40,32},{48,40},{56,48},{64,5... | collective-permute-start | bytes 24584 | tf_op jit(solution)/shard_map/ppermute | solution.py:351
  49.6 33.1 %all-to-all-start.2 = ((bf16[64,9,2,128]{3,2,1,0:T(2,128)(2,1)}), bf16[64,9,2,128]{3,2,1,0:T(2,128)(2,1)S(1)}, u32[]{:S(2)}, u32[]{:S(2)}) async-start(bf16[64,9,2,128]{3,2,1,0:T(2,128)(2,1)} %bitcast.5), calls=%async_computation.2 | async-start | bytes 589824 | tf_op jit(solution)/shard_map/all_to_all | solution.py:378
  84.2 26.6 %all-to-all-start.3 = ((bf16[64,16,128]{2,1,0:T(8,128)(2,1)}), bf16[64,16,128]{2,1,0:T(8,128)(2,1)S(1)}, u32[]{:S(2)}, u32[]{:S(2)}) async-start(bf16[64,16,128]{2,1,0:T(8,128)(2,1)} %shard_map.81), calls=%async_computation.3 | async-start | bytes 524288 | tf_op jit(solution)/shard_map/all_to_all | solution.py:384

commit v4 on v3

--- a/solution.py
+++ b/solution.py
@@ -1,4 +1,5 @@
 import functools
+import math
 
 import jax
 import jax.numpy as jnp
@@ -12,10 +13,22 @@
 TILE = 8
 PIECES = 4
 NOTES = 2
+FIRST_NUMBER = 32
 PEAK_PARTS = 3
 SIZE_PARTS = 2
+SCORE_SCALE = LANES ** (-0.5) * math.log2(math.e)
 F32 = jnp.float32
 BF16 = jnp.bfloat16
+
+
+def first_member(shards):
+    return shards * FIRST_NUMBER // 64
+
+
+def exchange(array, shards):
+    first = first_member(shards)
+    members = [(first + at) % shards for at in range(shards)]
+    return lax.all_to_all(array, "ctx", 0, 0, tiled=True, axis_index_groups=[members])
 
 
 def rows_of(shape):
@@ -69,6 +82,11 @@
         copy.start()
     for copy in copies:
         copy.wait()
+
+
+def position(shard, shards):
+    moved = shard - first_member(shards)
+    return jnp.where(moved < 0, moved + shards, moved)
 
 
 def destination(shards, shard, assignment, row_count):
@@ -82,7 +100,7 @@
     earlier = onehot(rows_of((row_count, row_count)) < lanes_of((row_count, row_count)))
     ranks = jnp.dot(flags, earlier, preferred_element_type=F32).astype(jnp.int32)
     rank = jnp.where(ahead, ranks[0:1, :], jnp.where(back, ranks[1:2, :], 0))
-    peer = jnp.where(distance == 0, -1, owner)
+    peer = jnp.where(distance == 0, -1, position(owner, shards))
     far_peer = jnp.where(ahead | back, -1, peer)
     return peer, far_peer, ahead, back, rank
 
@@ -103,7 +121,7 @@
 
 
 def rows_kernel(
-    shards, shard_ref, assignment_hbm, keys_hbm, values_hbm, far_ref, ahead_ref, back_ref, peer_ref,
+    shards, shard_ref, assignment_hbm, keys_hbm, values_hbm, far_ref, first_ref, second_ref, peer_ref,
     assignment_ref, keys_ref, values_ref, semaphore,
 ):
     pull((assignment_hbm, keys_hbm, values_hbm), (assignment_ref, keys_ref, values_ref), semaphore)
@@ -111,10 +129,11 @@
     assignment = assignment_ref[...]
     peer, far_peer, ahead, back, rank = destination(shards, shard_ref[0], assignment, row_count)
     rows = jnp.concatenate([keys_ref[...], values_ref[...]], axis=1)
-    slot = jnp.where(ahead, rank, jnp.where(back, NEAR + rank, -1))
+    is_odd = remainder(shard_ref[0], 2)
+    slot = jnp.where(ahead, is_odd * NEAR + rank, jnp.where(back, (1 - is_odd) * NEAR + rank, -1))
     near = jnp.dot(onehot(rows_of((2 * NEAR, row_count)) == slot), rows, preferred_element_type=F32).astype(BF16)
-    ahead_ref[...] = jnp.concatenate([near[:NEAR, :LANES], near[:NEAR, LANES:]], axis=0)
-    back_ref[...] = jnp.concatenate([near[NEAR:, :LANES], near[NEAR:, LANES:]], axis=0)
+    first_ref[...] = jnp.concatenate([near[:NEAR, :LANES], near[:NEAR, LANES:]], axis=0)
+    second_ref[...] = jnp.concatenate([near[NEAR:, :LANES], near[NEAR:, LANES:]], axis=0)
     chosen = chosen_rows(shards, peer, far_peer, row_count)
     picked = jnp.dot(chosen, rows, preferred_element_type=F32)
     target = remainder(assignment, row_count)
@@ -187,87 +206,100 @@
 
 
 def attend_kernel(
-    shards, shard_ref, sums_ref, total_ref, bias_ref, padded_ref, far_ref, from_back_ref, from_ahead_ref,
+    shards, shard_ref, sums_ref, total_ref, bias_ref, padded_ref, far_ref, first_ref, second_ref,
     merged_ref, partial_ref,
 ):
     row_count = sums_ref.shape[0]
     shard = shard_ref[0]
     back = jnp.where(shard == 0, shards - 1, shard - 1)
     ahead = jnp.where(shard == shards - 1, 0, shard + 1)
+    is_odd = remainder(shard, 2) == 1
+    shard = position(shard, shards)
+    first_source = position(jnp.where(is_odd, back, ahead), shards)
+    second_source = position(jnp.where(is_odd, ahead, back), shards)
+
     far = far_ref[...]
-    count = far.shape[0]
-    notes = far.astype(F32).T
-    lane = lanes_of((1, count))
-    source = divided(lane, PIECES)
-    is_far = (remainder(lane, PIECES) == NOTES) & (source != back) & (source != ahead) & (source != shard)
-    far_weight = notes[0:1, :]
-    far_target = jnp.where(is_far, notes[NEAR : NEAR + 1, :] * LANES + notes[2 * NEAR : 2 * NEAR + 1, :], -1.0)
-
-    line = rows_of((TILE, count))
-    wanted = jnp.where(line == 0, back, ahead) * PIECES + NOTES
-    picked = onehot((lanes_of((TILE, count)) == wanted) & (line < 2))
-    near_notes = jnp.dot(picked, far, preferred_element_type=F32)
+    lines = PIECES * shards
+    line = rows_of((lines, lines))
+    piece = divided(line, shards)
+    wanted = remainder(line, shards) * PIECES + piece
+    neighbour = jnp.where(line == 3 * shards, first_source, second_source) * PIECES + NOTES
+    wanted = jnp.where(piece < 3, wanted, jnp.where(line < 3 * shards + 2, neighbour, -1))
+    pieces = jnp.dot(onehot(lanes_of((lines, lines)) == wanted), far, preferred_element_type=F32)
+    notes = pieces[2 * shards : 3 * shards]
+    if shards < LANES:
+        notes = jnp.concatenate([notes, jnp.zeros((LANES - shards, LANES), F32)], axis=0)
+    notes = notes.T
+    near_notes = pieces[3 * shards : 3 * shards + TILE]
     near_target = (
         pltpu.roll(near_notes, LANES - NEAR, 1) * LANES + pltpu.roll(near_notes, LANES - 2 * NEAR, 1)
     )
+    far_target = notes[NEAR : NEAR + 1, :] * LANES + notes[2 * NEAR : 2 * NEAR + 1, :]
     lane = lanes_of((1, LANES))
-    second = (lane >= 2 * NEAR) & (lane < 3 * NEAR)
-    shifted_notes = pltpu.roll(near_notes, 2 * NEAR, 1)
-    shifted_target = pltpu.roll(near_target, 2 * NEAR, 1)
-    near_weight = jnp.where(lane < NEAR, near_notes[0:1, :], shifted_notes[1:2, :])
-    near_place = jnp.where(lane < NEAR, near_target[0:1, :], jnp.where(second, shifted_target[1:2, :], -1.0))
-
-    line = rows_of((row_count, count + LANES))
-
-    def mixing(far_shift, near_shift):
-        def moved(value, shift):
-            value = jnp.broadcast_to(value, (TILE, value.shape[1]))
-            return pltpu.roll(value, shift, 1)[0:1, :] if shift else value[0:1, :]
-
-        target = jnp.concatenate([moved(far_target, far_shift), moved(near_place, near_shift)], axis=1)
-        weight = jnp.concatenate([moved(far_weight, far_shift), moved(near_weight, near_shift)], axis=1)
-        return jnp.where(target.astype(jnp.int32) == line, weight, 0.0).astype(BF16)
-
-    key_mix = mixing(count - NOTES, 0)
-    value_mix = mixing(count - NOTES + 1, NEAR)
+    near_start = [shards, shards + NEAR]
+    is_far = (lane < shards) & (lane != first_source) & (lane != second_source) & (lane != shard)
+    target = jnp.where(is_far, far_target, -1.0)
+    weight = notes[0:1, :]
+    for at, start in enumerate(near_start):
+        inside = (lane >= start) & (lane < start + NEAR)
+        target = jnp.where(inside, pltpu.roll(near_target, start, 1)[at : at + 1, :], target)
+        weight = jnp.where(inside, pltpu.roll(near_notes, start, 1)[at : at + 1, :], weight)
+    target = target.astype(jnp.int32)
+    mix = jnp.where(target == rows_of((row_count, LANES)), weight, 0.0).astype(BF16)
+    unused = jnp.zeros((LANES - shards - 2 * NEAR, 2 * LANES), BF16)
     arrived = jnp.concatenate(
-        [far, from_back_ref[...], from_ahead_ref[...], jnp.zeros((LANES - 4 * NEAR, LANES), BF16)], axis=0
-    )
-    total = total_ref[...] + jnp.dot(key_mix, jnp.ones(arrived.shape, BF16), preferred_element_type=F32)
-    merged_keys = (sums_ref[:, :LANES] + jnp.dot(key_mix, arrived, preferred_element_type=F32)) / total
-    merged_values = (sums_ref[:, LANES:] + jnp.dot(value_mix, arrived, preferred_element_type=F32)) / total
-    merged_keys = merged_keys.astype(BF16)
-    merged_values = merged_values.astype(BF16)
+        [jnp.concatenate([pieces[:shards], pieces[shards : 2 * shards]], axis=1).astype(BF16)]
+        + [jnp.concatenate([near[:NEAR], near[NEAR:]], axis=1) for near in (first_ref[...], second_ref[...])]
+        + [unused],
+        axis=0,
+    )
+    total = total_ref[...] + jnp.dot(mix, jnp.ones((LANES, LANES), BF16), preferred_element_type=F32)
+    sums = sums_ref[...] + jnp.dot(mix, arrived, preferred_element_type=F32)
+    share = 1.0 / total
+    merged_keys = (sums[:, :LANES] * share).astype(BF16)
+    merged_values = (sums[:, LANES:] * share).astype(BF16)
     merged_ref[0] = merged_keys
     merged_ref[1] = merged_values
 
     span = padded_ref.shape[0] // shards
     per_peer = span - 2
-    scale = LANES ** (-0.5)
     bias = bias_ref[0:1, :]
     group = TILE * span
     peer, place = peer_place(rows_of((group, LANES)), span)
     lane = lanes_of((group, LANES))
-    part = divided(lane, per_peer)
-    diagonal = place == remainder(lane, per_peer)
-    from_peer, from_place = peer_place(lanes_of((group, group)), span)
-    to_peer, to_place = peer_place(rows_of((group, group)), span)
-    gather = onehot((to_place == per_peer) & (from_peer == to_peer) & (from_place < per_peer))
-    for at in range(0, padded_ref.shape[0], group):
+    diagonal = (place < per_peer) & (lane == peer * per_peer + place)
+    inside = place < per_peer
+    row = rows_of((TILE, LANES))
+    peaks = jnp.zeros((TILE, LANES), F32)
+    sizes = jnp.zeros((TILE, LANES), F32)
+    starts = range(0, padded_ref.shape[0], group)
+    for which, at in enumerate(starts):
         scores = lax.dot_general(
             padded_ref[at : at + group, :], merged_keys, (((1,), (1,)), ((), ())), preferred_element_type=F32
         )
-        scores = scores * scale + bias
+        scores = scores + bias
         peak = jnp.max(scores, axis=1, keepdims=True)
-        prob = jnp.exp(scores - peak)
+        prob = jnp.exp2((scores - peak) * SCORE_SCALE)
         size = jnp.sum(prob, axis=1, keepdims=True)
         sums = jnp.dot(prob.astype(BF16), merged_values, preferred_element_type=F32)
-        stats = jnp.zeros((group, LANES), F32)
-        for which, member in enumerate(split_parts(peak, PEAK_PARTS) + split_parts(size, SIZE_PARTS)):
-            stats = jnp.where(part == which, member, stats)
-        stats = jnp.where(diagonal, stats, 0.0).astype(BF16)
-        stats = jnp.dot(gather, stats, preferred_element_type=F32)
-        partial_ref[at : at + group, :] = jnp.where(place < per_peer, sums, stats).astype(BF16)
+        peaks = jnp.where(row == which, jnp.sum(jnp.where(diagonal, peak, 0.0), axis=0, keepdims=True), peaks)
+        sizes = jnp.where(row == which, jnp.sum(jnp.where(diagonal, size, 0.0), axis=0, keepdims=True), sizes)
+        partial_ref[at : at + group, :] = jnp.where(inside, sums, 0.0).astype(BF16)
+    part = divided(lanes_of((TILE, LANES)), per_peer)
+    members = split_parts(peaks, PEAK_PARTS) + split_parts(sizes, SIZE_PARTS)
+    stats = []
+    for turn in range(TILE):
+        mine = jnp.zeros((TILE, LANES), F32)
+        for which, member in enumerate(members):
+            shift = (which - turn) * per_peer % LANES
+            mine = jnp.where(part == which, pltpu.roll(member, shift, 1) if shift else member, mine)
+        stats.append(mine)
+    stats = jnp.concatenate(stats, axis=0).astype(BF16)
+    peer, place = peer_place(rows_of((group, TILE * TILE)), span)
+    source = lanes_of((group, TILE * TILE)) - jnp.where(place == per_peer, peer * TILE, -LANES)
+    for which, at in enumerate(starts):
+        spread = jnp.dot(onehot(source == which), stats, preferred_element_type=F32)
+        partial_ref[at : at + group, :] = (partial_ref[at : at + group, :].astype(F32) + spread).astype(BF16)
 
 
 def combine_kernel(shards, partial_ref, finished_ref):
@@ -285,7 +317,7 @@
     valid = lanes_of((shards, LANES)) < per_peer
     peak = jnp.where(valid, (part(0) + part(1)) + part(2), 0.0)
     size = jnp.where(valid, part(3) + part(4), 1.0)
-    rescale = jnp.exp(peak - jnp.max(peak, axis=0, keepdims=True))
+    rescale = jnp.exp2((peak - jnp.max(peak, axis=0, keepdims=True)) * SCORE_SCALE)
     factor = rescale / jnp.sum(rescale * size, axis=0, keepdims=True)
     factor = jnp.concatenate([factor, jnp.zeros((LANES - shards, LANES), F32)], axis=0).T[:per_peer, :shards]
     factor = jnp.concatenate(split_parts(factor, 2), axis=0).astype(BF16)
@@ -334,7 +366,7 @@
     (copies,) = run_kernel(copy_kernel, shards, [((groups * slices, LANES), BF16)], [VMEM], (importance,))
     importance = lax.all_to_all(copies.reshape(groups, slices, LANES), "kv", 0, 0, tiled=True)
     pulled = (assignment, cache_keys, cache_values)
-    far, ahead, back, peer = run_kernel(
+    far, first, second, peer = run_kernel(
         rows_kernel,
         shards,
         [
@@ -347,13 +379,13 @@
         (shard,) + pulled,
         pulled,
     )
-    from_back = lax.ppermute(ahead, "ctx", [(i, (i + 1) % shards) for i in range(shards)])
-    from_ahead = lax.ppermute(back, "ctx", [(i, (i - 1) % shards) for i in range(shards)])
+    first = lax.ppermute(first, "ctx", [(i, (i + 1 - 2 * (i % 2)) % shards) for i in range(shards)])
+    second = lax.ppermute(second, "ctx", [(i, (i - 1 + 2 * (i % 2)) % shards) for i in range(shards)])
     (far,) = run_kernel(
         weigh_kernel, shards, [((PIECES * shards, LANES), BF16)], [VMEM, VMEM, VMEM], (importance, peer, far)
     )
     far, importance = lax.optimization_barrier((far, importance))
-    far = lax.all_to_all(far.reshape(shards, PIECES, LANES), "ctx", 0, 0, tiled=True)
+    far = exchange(far.reshape(shards, PIECES, LANES), shards)
     pulled = (assignment, cache_keys, cache_values, queries)
     sums, total, bias, padded = run_kernel(
         home_kernel,
@@ -373,15 +405,15 @@
         shards,
         [((2, row_count, head_dim), BF16), ((shards * span, LANES), BF16)],
         [SMEM] + [VMEM] * 7,
-        (shard, sums, total, bias, padded, far.reshape(shards * PIECES, LANES), from_back, from_ahead),
-    )
-    partial = lax.all_to_all(partial.reshape(shards, span // 2, 2, LANES), "ctx", 0, 0, tiled=True)
+        (shard, sums, total, bias, padded, far.reshape(shards * PIECES, LANES), first, second),
+    )
+    partial = exchange(partial.reshape(shards, span // 2, 2, LANES), shards)
     merged_keys = merged[0]
     (finished,) = run_kernel(
         combine_kernel, shards, [((shards, per_peer, LANES), BF16)], [VMEM], (partial.reshape(shards * span, LANES),)
     )
     finished, merged, merged_keys = lax.optimization_barrier((finished, merged, merged_keys))
-    finished = lax.all_to_all(finished, "ctx", 0, 0, tiled=True)
+    finished = exchange(finished, shards)
     merged_values = merged[1]
     tiles = query_rows // TILE
     attended = finished.reshape(tiles, heads, TILE, head_dim).transpose(0, 2, 1, 3)

time: 112 us -> 105 us (0.938)
  waiting for transfers between devices: 47.9 us -> 29.4 us
  starting transfers between devices: 48.3 us -> 60.6 us
    all_to_all x3, waiting for transfers between devices: 47.6 us -> 25.5 us  [exchange(): lax.all_to_all(array, 'ctx', 0, 0, tiled=True, axis_index_groups=[members])]
    all_to_all x3, starting transfers between devices: 30 us -> 44.1 us  [exchange(): lax.all_to_all(array, 'ctx', 0, 0, tiled=True, axis_index_groups=[members])]
    ppermute x2, waiting for transfers between devices: 0.3 us -> 3.85 us  [the longest x1 3.85 us: per_device(): lax.ppermute(second, 'ctx', [(i, (i - 1 + 2 * (i % 2)) % shards) for i in...]
    ppermute x2, starting transfers between devices: 9.16 us -> 7.33 us  [the longest x1 3.95 us: per_device(): lax.ppermute(second, 'ctx', [(i, (i - 1 + 2 * (i % 2)) % shards) for i in...]
  transfers between devices with their start and end apart: 6 -> 6, of which waited for: 4 -> 3; matrix products, arithmetic and copies ran while one was open for 1% -> 1% of each run, Pallas kernels for 2% -> 2%
where the time goes in v4:
time: 105 us
  starting transfers between devices  60.6 us (58%)
  waiting for transfers between devices  29.4 us (28%)
  Pallas kernels  8.72 us (8%)
  local copies, waits for them, and re-layouts  5.21 us (5%)
    all_to_all x3, starting transfers between devices, exchange(): lax.all_to_all(array, 'ctx', 0, 0, tiled=True, axis_index_groups=[members])  44.1 us
    all_to_all x3, waiting for transfers between devices, exchange(): lax.all_to_all(array, 'ctx', 0, 0, tiled=True, axis_index_groups=[members])  25.5 us
    all_to_all x1, starting transfers between devices, per_device(): lax.all_to_all(copies.reshape(groups, slices, LANES), 'kv', 0, 0, tiled=T...  9.14 us
    pallas_call x6, Pallas kernels, run_kernel(): pl.pallas_call(functools.partial(body, shards), out_shape=[jax.ShapeDtype...  8.72 us
    ppermute x1, starting transfers between devices, per_device(): lax.ppermute(second, 'ctx', [(i, (i - 1 + 2 * (i % 2)) % shards) for i in...  3.95 us
    unnamed x15, local copies, waits for them, and re-layouts  3.88 us
    ppermute x1, waiting for transfers between devices, per_device(): lax.ppermute(second, 'ctx', [(i, (i - 1 + 2 * (i % 2)) % shards) for i in...  3.85 us
    ppermute x1, starting transfers between devices, per_device(): lax.ppermute(first, 'ctx', [(i, (i + 1 - 2 * (i % 2)) % shards) for i in...  3.38 us
  transfers between devices with their start and end apart: 6, of which 3 were waited for; matrix products, arithmetic and copies ran while one was open for 1% of the time, Pallas kernels for 2%

profile of v4, /device:TPU:4, one launch (start us, length us, event | category | flops | bytes accessed | tf_op | source)
XLA Modules:
  0.0 104.7 jit_solution(422142069232869306)
XLA Ops:
  0.6 0.0 copy-start.6
  0.6 0.7 copy-done.6
  1.3 0.6 shard_map.76
  1.9 9.1 %all-to-all-start = ((bf16[8,4,128]{2,1,0:T(4,128)(2,1)}), bf16[8,4,128]{2,1,0:T(4,128)(2,1)S(1)}, u32[]{:S(2)}, u32[]{:S(2)}) async-start(bf16[8,4,128]{2,1,0:T(4,128)(2,1)} %bitcast.1), calls=%async_computation | async-start | bytes 16384 | tf_op jit(solution)/shard_map/all_to_all | solution.py:367
  11.1 0.0 copy-start.5
  11.1 0.7 copy-done.5
  11.7 0.9 copy-done
  12.6 0.9 copy-done.2
  13.6 0.9 shard_map.77
  14.4 0.0 all-to-all-done.importance_ref
  14.5 0.0 copy-start.1
  14.5 0.0 copy-start.3
  14.5 0.9 shard_map.78
  15.4 17.8 %all-to-all-start.1 = ((bf16[64,4,128]{2,1,0:T(4,128)(2,1)}), bf16[64,4,128]{2,1,0:T(4,128)(2,1)S(1)}, u32[]{:S(2)}, u32[]{:S(2)}) async-start(bf16[64,4,128]{2,1,0:T(4,128)(2,1)} %bitcast.3), calls=%async_computation.1 | async-start | bytes 131072 | tf_op jit(solution)/shard_map/all_to_all | solution.py:31
  33.2 3.4 %collective-permute-start = (bf16[32,128]{1,0:T(8,128)(2,1)S(1)}, bf16[32,128]{1,0:T(8,128)(2,1)S(1)}, u32[]{:S(2)}, u32[]{:S(2)}) collective-permute-start(bf16[32,128]{1,0:T(8,128)(2,1)S(1)} %get-tuple-element.26), channel_id=1, source_target_pairs={{0,8},{8,0},{16,24},{24,16},{32,40},{40,32},{48,56},{56,48},{64,72... | collective-permute-start | bytes 24584 | tf_op jit(solution)/shard_map/ppermute | solution.py:382
  36.6 4.0 %collective-permute-start.1 = (bf16[32,128]{1,0:T(8,128)(2,1)S(1)}, bf16[32,128]{1,0:T(8,128)(2,1)S(1)}, u32[]{:S(2)}, u32[]{:S(2)}) collective-permute-start(bf16[32,128]{1,0:T(8,128)(2,1)S(1)} %get-tuple-element.27), channel_id=1, source_target_pairs={{0,504},{8,16},{16,8},{24,32},{32,24},{40,48},{48,40},{56,64},{64,... | collective-permute-start | bytes 24584 | tf_op jit(solution)/shard_map/ppermute | solution.py:383
  40.5 0.0 copy-done.4
  40.5 0.0 copy-done.1
  40.5 0.0 copy-done.3
  40.5 1.0 shard_map.79
  41.6 0.0 collective-permute-done.first_ref
  41.6 3.9 %collective-permute-done.1.second_ref = bf16[32,128]{1,0:T(8,128)(2,1)S(1)} collective-permute-done((bf16[32,128]{1,0:T(8,128)(2,1)S(1)}, bf16[32,128]{1,0:T(8,128)(2,1)S(1)}, u32[]{:S(2)}, u32[]{:S(2)}) %collective-permute-start.1) | collective-permute-done | bytes 8224 | tf_op jit(solution)/shard_map/ppermute | solution.py:383
  45.4 0.0 all-to-all-done.1
  45.4 4.0 %shard_map.80 = (bf16[2,512,128]{2,1,0:T(8,128)(2,1)S(1)}, bf16[1152,128]{1,0:T(8,128)(2,1)}) custom-call(s32[1]{0:T(128)} %bitcast.shard_ref, f32[512,256]{1,0:T(8,128)S(1)} %get-tuple-element.21.sums_ref, f32[512,128]{1,0:T(8,128)S(1)} %get-tuple-element.22.total_ref, f32[8,512]{1,0:T(8,128)S(1)} %get-tuple-element.23.bias_ref, ...), custom_call_target="tpu_custom_call" | custom-call | tf_op jit(solution)/shard_map/pallas_call | solution.py:344
  49.4 13.0 %all-to-all-start.2 = ((bf16[64,9,2,128]{3,2,1,0:T(2,128)(2,1)}), bf16[64,9,2,128]{3,2,1,0:T(2,128)(2,1)S(1)}, u32[]{:S(2)}, u32[]{:S(2)}) async-start(bf16[64,9,2,128]{3,2,1,0:T(2,128)(2,1)} %bitcast.5), calls=%async_computation.2 | async-start | bytes 589824 | tf_op jit(solution)/shard_map/all_to_all | solution.py:31
  62.4 0.7 slice_bitcast_fusion.1
  63.0 13.1 %all-to-all-done.2 = bf16[64,9,2,128]{3,2,1,0:T(2,128)(2,1)S(1)} async-done(((bf16[64,9,2,128]{3,2,1,0:T(2,128)(2,1)}), bf16[64,9,2,128]{3,2,1,0:T(2,128)(2,1)S(1)}, u32[]{:S(2)}, u32[]{:S(2)}) %all-to-all-start.2) | async-done | bytes 294944 | tf_op jit(solution)/shard_map/all_to_all | solution.py:31
  76.1 1.4 %shard_map.81 = bf16[64,16,128]{2,1,0:T(8,128)(2,1)} custom-call(bf16[1152,128]{1,0:T(8,128)(2,1)S(1)} %bitcast.16), custom_call_target="tpu_custom_call" | custom-call | tf_op jit(solution)/shard_map/pallas_call | solution.py:344
  77.5 13.4 %all-to-all-start.3 = ((bf16[64,16,128]{2,1,0:T(8,128)(2,1)}), bf16[64,16,128]{2,1,0:T(8,128)(2,1)S(1)}, u32[]{:S(2)}, u32[]{:S(2)}) async-start(bf16[64,16,128]{2,1,0:T(8,128)(2,1)} %shard_map.81), calls=%async_computation.3 | async-start | bytes 524288 | tf_op jit(solution)/shard_map/all_to_all | solution.py:31
  90.9 0.7 slice_bitcast_fusion
  91.5 12.4 %all-to-all-done.3 = bf16[64,16,128]{2,1,0:T(8,128)(2,1)S(1)} async-done(((bf16[64,16,128]{2,1,0:T(8,128)(2,1)}), bf16[64,16,128]{2,1,0:T(8,128)(2,1)S(1)}, u32[]{:S(2)}, u32[]{:S(2)}) %all-to-all-start.3) | async-done | bytes 262176 | tf_op jit(solution)/shard_map/all_to_all | solution.py:31
  104.0 0.7 copy.9
  (3 shorter events, 0.0 us)
Async XLA Ops:
  0.6 0.7 copy-start.6
  1.9 12.5 %all-to-all-start = ((bf16[8,4,128]{2,1,0:T(4,128)(2,1)}), bf16[8,4,128]{2,1,0:T(4,128)(2,1)S(1)}, u32[]{:S(2)}, u32[]{:S(2)}) async-start(bf16[8,4,128]{2,1,0:T(4,128)(2,1)} %bitcast.1), calls=%async_computation | async-start | bytes 16384 | tf_op jit(solution)/shard_map/all_to_all | solution.py:367
  11.1 0.7 copy-start.5
  11.7 0.9 copy-start
  12.6 0.9 copy-start.2
  13.5 27.0 %copy-start.4 = (bf16[128,1024]{1,0:T(8,128)(2,1)S(1)}, bf16[128,1024]{1,0:T(8,128)(2,1)}, u32[]{:S(2)}) copy-start(bf16[128,1024]{1,0:T(8,128)(2,1)} %queries_hbm.1) | copy-start | bytes 786436
  14.5 26.1 %copy-start.1 = (bf16[512,128]{1,0:T(8,128)(2,1)S(1)}, bf16[512,128]{1,0:T(8,128)(2,1)}, u32[]{:S(2)}) copy-start(bf16[512,128]{1,0:T(8,128)(2,1)} %keys_hbm.3) | copy-start | bytes 393220
  14.5 26.1 %copy-start.3 = (bf16[512,128]{1,0:T(8,128)(2,1)S(1)}, bf16[512,128]{1,0:T(8,128)(2,1)}, u32[]{:S(2)}) copy-start(bf16[512,128]{1,0:T(8,128)(2,1)} %values_hbm.3) | copy-start | bytes 393220
  15.4 30.1 %all-to-all-start.1 = ((bf16[64,4,128]{2,1,0:T(4,128)(2,1)}), bf16[64,4,128]{2,1,0:T(4,128)(2,1)S(1)}, u32[]{:S(2)}, u32[]{:S(2)}) async-start(bf16[64,4,128]{2,1,0:T(4,128)(2,1)} %bitcast.3), calls=%async_computation.1 | async-start | bytes 131072 | tf_op jit(solution)/shard_map/all_to_all | solution.py:31
  33.2 8.4 %collective-permute-start = (bf16[32,128]{1,0:T(8,128)(2,1)S(1)}, bf16[32,128]{1,0:T(8,128)(2,1)S(1)}, u32[]{:S(2)}, u32[]{:S(2)}) collective-permute-start(bf16[32,128]{1,0:T(8,128)(2,1)S(1)} %get-tuple-element.26), channel_id=1, source_target_pairs={{0,8},{8,0},{16,24},{24,16},{32,40},{40,32},{48,56},{56,48},{64,72... | collective-permute-start | bytes 24584 | tf_op jit(solution)/shard_map/ppermute | solution.py:382
  36.6 8.9 %collective-permute-start.1 = (bf16[32,128]{1,0:T(8,128)(2,1)S(1)}, bf16[32,128]{1,0:T(8,128)(2,1)S(1)}, u32[]{:S(2)}, u32[]{:S(2)}) collective-permute-start(bf16[32,128]{1,0:T(8,128)(2,1)S(1)} %get-tuple-element.27), channel_id=1, source_target_pairs={{0,504},{8,16},{16,8},{24,32},{32,24},{40,48},{48,40},{56,64},{64,... | collective-permute-start | bytes 24584 | tf_op jit(solution)/shard_map/ppermute | solution.py:383
  49.4 26.7 %all-to-all-start.2 = ((bf16[64,9,2,128]{3,2,1,0:T(2,128)(2,1)}), bf16[64,9,2,128]{3,2,1,0:T(2,128)(2,1)S(1)}, u32[]{:S(2)}, u32[]{:S(2)}) async-start(bf16[64,9,2,128]{3,2,1,0:T(2,128)(2,1)} %bitcast.5), calls=%async_computation.2 | async-start | bytes 589824 | tf_op jit(solution)/shard_map/all_to_all | solution.py:31
  77.5 26.5 %all-to-all-start.3 = ((bf16[64,16,128]{2,1,0:T(8,128)(2,1)}), bf16[64,16,128]{2,1,0:T(8,128)(2,1)S(1)}, u32[]{:S(2)}, u32[]{:S(2)}) async-start(bf16[64,16,128]{2,1,0:T(8,128)(2,1)} %shard_map.81), calls=%async_computation.3 | async-start | bytes 524288 | tf_op jit(solution)/shard_map/all_to_all | solution.py:31

commit v5 on v4

--- a/solution.py
+++ b/solution.py
@@ -13,7 +13,7 @@
 TILE = 8
 PIECES = 4
 NOTES = 2
-FIRST_NUMBER = 32
+FIRST_NUMBER = 43
 PEAK_PARTS = 3
 SIZE_PARTS = 2
 SCORE_SCALE = LANES ** (-0.5) * math.log2(math.e)
@@ -110,7 +110,8 @@
     return onehot(divided(line, PIECES) == jnp.where(remainder(line, PIECES) == NOTES, peer, far_peer))
 
 
-def copy_kernel(shards, importance_ref, copies_ref):
+def copy_kernel(shards, importance_hbm, copies_ref, importance_ref, semaphore):
+    pull((importance_hbm,), (importance_ref,), semaphore)
     importance = importance_ref[...].astype(F32)
     slices = importance.shape[1] // LANES
     place = remainder(rows_of(copies_ref.shape), slices)
@@ -129,8 +130,8 @@
     assignment = assignment_ref[...]
     peer, far_peer, ahead, back, rank = destination(shards, shard_ref[0], assignment, row_count)
     rows = jnp.concatenate([keys_ref[...], values_ref[...]], axis=1)
-    is_odd = remainder(shard_ref[0], 2)
-    slot = jnp.where(ahead, is_odd * NEAR + rank, jnp.where(back, (1 - is_odd) * NEAR + rank, -1))
+    is_even = 1 - remainder(shard_ref[0], 2)
+    slot = jnp.where(ahead, is_even * NEAR + rank, jnp.where(back, (1 - is_even) * NEAR + rank, -1))
     near = jnp.dot(onehot(rows_of((2 * NEAR, row_count)) == slot), rows, preferred_element_type=F32).astype(BF16)
     first_ref[...] = jnp.concatenate([near[:NEAR, :LANES], near[:NEAR, LANES:]], axis=0)
     second_ref[...] = jnp.concatenate([near[NEAR:, :LANES], near[NEAR:, LANES:]], axis=0)
@@ -207,7 +208,7 @@
 
 def attend_kernel(
     shards, shard_ref, sums_ref, total_ref, bias_ref, padded_ref, far_ref, first_ref, second_ref,
-    merged_ref, partial_ref,
+    merged_keys_ref, merged_values_ref, partial_ref,
 ):
     row_count = sums_ref.shape[0]
     shard = shard_ref[0]
@@ -215,8 +216,8 @@
     ahead = jnp.where(shard == shards - 1, 0, shard + 1)
     is_odd = remainder(shard, 2) == 1
     shard = position(shard, shards)
-    first_source = position(jnp.where(is_odd, back, ahead), shards)
-    second_source = position(jnp.where(is_odd, ahead, back), shards)
+    first_source = position(jnp.where(is_odd, ahead, back), shards)
+    second_source = position(jnp.where(is_odd, back, ahead), shards)
 
     far = far_ref[...]
     lines = PIECES * shards
@@ -258,8 +259,8 @@
     share = 1.0 / total
     merged_keys = (sums[:, :LANES] * share).astype(BF16)
     merged_values = (sums[:, LANES:] * share).astype(BF16)
-    merged_ref[0] = merged_keys
-    merged_ref[1] = merged_values
+    merged_keys_ref[...] = merged_keys
+    merged_values_ref[...] = merged_values
 
     span = padded_ref.shape[0] // shards
     per_peer = span - 2
@@ -334,7 +335,7 @@
 
 SMEM = pl.BlockSpec(memory_space=pltpu.SMEM)
 VMEM = pl.BlockSpec(memory_space=pltpu.VMEM)
-ANY = pl.BlockSpec(memory_space=pl.ANY)
+HBM = pl.BlockSpec(memory_space=pltpu.HBM)
 
 
 def run_kernel(body, shards, shapes, specs, operands, pulled=()):
@@ -363,7 +364,8 @@
     assignment = assignment.reshape(1, row_count)
 
     slices = row_count // LANES
-    (copies,) = run_kernel(copy_kernel, shards, [((groups * slices, LANES), BF16)], [VMEM], (importance,))
+    pulled = (importance,)
+    (copies,) = run_kernel(copy_kernel, shards, [((groups * slices, LANES), BF16)], [HBM], pulled, pulled)
     importance = lax.all_to_all(copies.reshape(groups, slices, LANES), "kv", 0, 0, tiled=True)
     pulled = (assignment, cache_keys, cache_values)
     far, first, second, peer = run_kernel(
@@ -375,12 +377,12 @@
             ((2 * NEAR, LANES), BF16),
             ((TILE, row_count), jnp.int32),
         ],
-        [SMEM, ANY, ANY, ANY],
+        [SMEM, HBM, HBM, HBM],
         (shard,) + pulled,
         pulled,
     )
-    first = lax.ppermute(first, "ctx", [(i, (i + 1 - 2 * (i % 2)) % shards) for i in range(shards)])
-    second = lax.ppermute(second, "ctx", [(i, (i - 1 + 2 * (i % 2)) % shards) for i in range(shards)])
+    first = lax.ppermute(first, "ctx", [(i, (i - 1 + 2 * (i % 2)) % shards) for i in range(shards)])
+    second = lax.ppermute(second, "ctx", [(i, (i + 1 - 2 * (i % 2)) % shards) for i in range(shards)])
     (far,) = run_kernel(
         weigh_kernel, shards, [((PIECES * shards, LANES), BF16)], [VMEM, VMEM, VMEM], (importance, peer, far)
     )
@@ -396,25 +398,22 @@
             ((TILE, row_count), F32),
             ((shards * span, head_dim), BF16),
         ],
-        [SMEM, VMEM, ANY, ANY, ANY, ANY],
+        [SMEM, VMEM, HBM, HBM, HBM, HBM],
         (shard, importance) + pulled,
         pulled,
     )
-    merged, partial = run_kernel(
+    merged_keys, merged_values, partial = run_kernel(
         attend_kernel,
         shards,
-        [((2, row_count, head_dim), BF16), ((shards * span, LANES), BF16)],
+        [(cache_keys.shape, BF16), (cache_keys.shape, BF16), ((shards * span, LANES), BF16)],
         [SMEM] + [VMEM] * 7,
         (shard, sums, total, bias, padded, far.reshape(shards * PIECES, LANES), first, second),
     )
     partial = exchange(partial.reshape(shards, span // 2, 2, LANES), shards)
-    merged_keys = merged[0]
     (finished,) = run_kernel(
         combine_kernel, shards, [((shards, per_peer, LANES), BF16)], [VMEM], (partial.reshape(shards * span, LANES),)
     )
-    finished, merged, merged_keys = lax.optimization_barrier((finished, merged, merged_keys))
     finished = exchange(finished, shards)
-    merged_values = merged[1]
     tiles = query_rows // TILE
     attended = finished.reshape(tiles, heads, TILE, head_dim).transpose(0, 2, 1, 3)
     return (merged_keys, merged_values, attended.reshape(query_rows, heads * head_dim))

time: 105 us -> 99.6 us (0.949)
  the two profiles are of different devices: /device:TPU:4 before, /device:TPU:8 now
where the time goes in v5:
time: 99.6 us; the launch traced here: 99.2 us
  blocking collectives  53.7 us (54%)
  starting transfers between devices  29.9 us (30%)
  Pallas kernels  7.65 us (8%)
  local copies, waits for them, and re-layouts  3.87 us (4%)
  waiting for transfers between devices  3.35 us (3%)
    all_to_all x2, blocking collectives, exchange(): lax.all_to_all(array, 'ctx', 0, 0, tiled=True, axis_index_groups=[members])  53.7 us
    all_to_all x1, starting transfers between devices, exchange(): lax.all_to_all(array, 'ctx', 0, 0, tiled=True, axis_index_groups=[members])  20 us
    pallas_call x6, Pallas kernels, run_kernel(): pl.pallas_call(functools.partial(body, shards), out_shape=[jax.ShapeDtype...  7.65 us
    all_to_all x1, starting transfers between devices, per_device(): lax.all_to_all(copies.reshape(groups, slices, LANES), 'kv', 0, 0, tiled=T...  4.31 us
    unnamed x15, local copies, waits for them, and re-layouts  3.87 us
    ppermute x1, starting transfers between devices, per_device(): lax.ppermute(second, 'ctx', [(i, (i + 1 - 2 * (i % 2)) % shards) for i in...  3.06 us
    ppermute x1, starting transfers between devices, per_device(): lax.ppermute(first, 'ctx', [(i, (i - 1 + 2 * (i % 2)) % shards) for i in...  2.48 us
  transfers between devices with their start and end apart: 4, of which 2 were waited for; matrix products, arithmetic and copies ran while one was open for 0% of the time, Pallas kernels for 2%

profile of v5, /device:TPU:8, one launch (start us, length us, event | category | flops | bytes accessed | tf_op | source)
XLA Modules:
  0.0 99.2 jit_solution(7105397069844454578)
XLA Ops:
  0.6 0.0 copy-start.6
  0.6 0.7 copy-done.6
  1.3 0.6 shard_map.76
  1.9 4.3 %all-to-all-start = ((bf16[8,4,128]{2,1,0:T(4,128)(2,1)}), bf16[8,4,128]{2,1,0:T(4,128)(2,1)S(1)}, u32[]{:S(2)}, u32[]{:S(2)}) async-start(bf16[8,4,128]{2,1,0:T(4,128)(2,1)} %bitcast.1), calls=%async_computation | async-start | bytes 16384 | tf_op jit(solution)/shard_map/all_to_all | solution.py:369
  6.3 0.0 copy-start.5
  6.3 0.7 copy-done.5
  6.9 0.0 copy-start
  6.9 0.9 copy-done
  7.8 0.0 copy-start.2
  7.8 0.9 copy-done.2
  8.7 0.0 copy-start.4
  8.7 0.9 shard_map.77
  9.6 1.9 %all-to-all-done.importance_ref = bf16[8,4,128]{2,1,0:T(4,128)(2,1)S(1)} async-done(((bf16[8,4,128]{2,1,0:T(4,128)(2,1)}), bf16[8,4,128]{2,1,0:T(4,128)(2,1)S(1)}, u32[]{:S(2)}, u32[]{:S(2)}) %all-to-all-start) | async-done | bytes 8224 | tf_op jit(solution)/shard_map/all_to_all | solution.py:369
  11.6 0.0 copy-start.1
  11.6 0.0 copy-start.3
  11.6 0.9 shard_map.78
  12.4 20.0 %all-to-all-start.1 = ((bf16[64,4,128]{2,1,0:T(4,128)(2,1)}), bf16[64,4,128]{2,1,0:T(4,128)(2,1)S(1)}, u32[]{:S(2)}, u32[]{:S(2)}) async-start(bf16[64,4,128]{2,1,0:T(4,128)(2,1)} %bitcast.3), calls=%async_computation.1 | async-start | bytes 131072 | tf_op jit(solution)/shard_map/all_to_all | solution.py:31
  32.5 2.5 %collective-permute-start = (bf16[32,128]{1,0:T(8,128)(2,1)S(1)}, bf16[32,128]{1,0:T(8,128)(2,1)S(1)}, u32[]{:S(2)}, u32[]{:S(2)}) collective-permute-start(bf16[32,128]{1,0:T(8,128)(2,1)S(1)} %get-tuple-element.24), channel_id=1, source_target_pairs={{0,504},{8,16},{16,8},{24,32},{32,24},{40,48},{48,40},{56,64},{64,... | collective-permute-start | bytes 24584 | tf_op jit(solution)/shard_map/ppermute | solution.py:384
  35.0 3.1 %collective-permute-start.1 = (bf16[32,128]{1,0:T(8,128)(2,1)S(1)}, bf16[32,128]{1,0:T(8,128)(2,1)S(1)}, u32[]{:S(2)}, u32[]{:S(2)}) collective-permute-start(bf16[32,128]{1,0:T(8,128)(2,1)S(1)} %get-tuple-element.25), channel_id=1, source_target_pairs={{0,8},{8,0},{16,24},{24,16},{32,40},{40,32},{48,56},{56,48},{64,72... | collective-permute-start | bytes 24584 | tf_op jit(solution)/shard_map/ppermute | solution.py:385
  38.0 0.0 copy-done.4
  38.0 0.0 copy-done.1
  38.1 0.0 copy-done.3
  38.1 1.0 %shard_map.79 = (f32[512,256]{1,0:T(8,128)S(1)}, f32[512,128]{1,0:T(8,128)S(1)}, f32[8,512]{1,0:T(8,128)S(1)}, bf16[1152,128]{1,0:T(8,128)(2,1)S(1)}) custom-call(s32[1]{0:T(128)} %bitcast.shard_ref, bf16[8,4,128]{2,1,0:T(4,128)(2,1)S(1)} %all-to-all-done.importance_ref, s32[1,512]{1,0:T(1,128)S(1)} %bitcast.16, bf16[512,128]{1,0:T(8,128)(2,1)S(1)} %copy-done.1, ...), custom_call_target="tpu_custom_call" | custom-call | tf_op jit(solution)/shard_map/pallas_call | solution.py:345
  39.1 0.0 collective-permute-done.first_ref
  39.1 1.4 %collective-permute-done.1.second_ref = bf16[32,128]{1,0:T(8,128)(2,1)S(1)} collective-permute-done((bf16[32,128]{1,0:T(8,128)(2,1)S(1)}, bf16[32,128]{1,0:T(8,128)(2,1)S(1)}, u32[]{:S(2)}, u32[]{:S(2)}) %collective-permute-start.1) | collective-permute-done | bytes 8224 | tf_op jit(solution)/shard_map/ppermute | solution.py:385
  40.5 0.0 all-to-all-done.1
  40.5 3.6 %shard_map.80 = (bf16[512,128]{1,0:T(8,128)(2,1)}, bf16[512,128]{1,0:T(8,128)(2,1)}, bf16[1152,128]{1,0:T(8,128)(2,1)S(1)}) custom-call(s32[1]{0:T(128)} %bitcast.shard_ref, f32[512,256]{1,0:T(8,128)S(1)} %get-tuple-element.19.sums_ref, f32[512,128]{1,0:T(8,128)S(1)} %get-tuple-element.20.total_ref, f32[8,512]{1,0:T(8,128)S(1)} %get-tuple-element.21.bias_ref, ...), custom_call_target="tpu_custom_call" | custom-call | tf_op jit(solution)/shard_map/pallas_call | solution.py:345
  44.1 28.3 %all_to_all.20 = bf16[64,9,2,128]{3,2,1,0:T(2,128)(2,1)S(1)} all-to-all(bf16[64,9,2,128]{3,2,1,0:T(2,128)(2,1)S(1)} %bitcast.13), channel_id=1, replica_groups={{344,352,360,368,376,384,392,400,408,416,424,432,440,448,456,464,472,48..., dimensions={0} | all-to-all | bytes 589824 | tf_op jit(solution)/shard_map/all_to_all | solution.py:31
  72.4 0.7 shard_map.81
  73.1 25.4 %all_to_all.21 = bf16[64,16,128]{2,1,0:T(8,128)(2,1)S(1)} all-to-all(bf16[64,16,128]{2,1,0:T(8,128)(2,1)S(1)} %shard_map.81), channel_id=1, replica_groups={{344,352,360,368,376,384,392,400,408,416,424,432,440,448,456,464,472,48..., dimensions={0} | all-to-all | bytes 524288 | tf_op jit(solution)/shard_map/all_to_all | solution.py:31
  98.5 0.7 copy.9
Async XLA Ops:
  0.6 0.7 copy-start.6
  1.9 9.6 %all-to-all-start = ((bf16[8,4,128]{2,1,0:T(4,128)(2,1)}), bf16[8,4,128]{2,1,0:T(4,128)(2,1)S(1)}, u32[]{:S(2)}, u32[]{:S(2)}) async-start(bf16[8,4,128]{2,1,0:T(4,128)(2,1)} %bitcast.1), calls=%async_computation | async-start | bytes 16384 | tf_op jit(solution)/shard_map/all_to_all | solution.py:369
  6.3 0.7 copy-start.5
  6.9 0.9 copy-start
  7.8 0.9 copy-start.2
  8.7 29.3 %copy-start.4 = (bf16[128,1024]{1,0:T(8,128)(2,1)S(1)}, bf16[128,1024]{1,0:T(8,128)(2,1)}, u32[]{:S(2)}) copy-start(bf16[128,1024]{1,0:T(8,128)(2,1)} %queries_hbm.1) | copy-start | bytes 786436
  11.6 26.5 %copy-start.1 = (bf16[512,128]{1,0:T(8,128)(2,1)S(1)}, bf16[512,128]{1,0:T(8,128)(2,1)}, u32[]{:S(2)}) copy-start(bf16[512,128]{1,0:T(8,128)(2,1)} %keys_hbm.3) | copy-start | bytes 393220
  11.6 26.5 %copy-start.3 = (bf16[512,128]{1,0:T(8,128)(2,1)S(1)}, bf16[512,128]{1,0:T(8,128)(2,1)}, u32[]{:S(2)}) copy-start(bf16[512,128]{1,0:T(8,128)(2,1)} %values_hbm.3) | copy-start | bytes 393220
  12.4 28.1 %all-to-all-start.1 = ((bf16[64,4,128]{2,1,0:T(4,128)(2,1)}), bf16[64,4,128]{2,1,0:T(4,128)(2,1)S(1)}, u32[]{:S(2)}, u32[]{:S(2)}) async-start(bf16[64,4,128]{2,1,0:T(4,128)(2,1)} %bitcast.3), calls=%async_computation.1 | async-start | bytes 131072 | tf_op jit(solution)/shard_map/all_to_all | solution.py:31
  32.5 6.6 %collective-permute-start = (bf16[32,128]{1,0:T(8,128)(2,1)S(1)}, bf16[32,128]{1,0:T(8,128)(2,1)S(1)}, u32[]{:S(2)}, u32[]{:S(2)}) collective-permute-start(bf16[32,128]{1,0:T(8,128)(2,1)S(1)} %get-tuple-element.24), channel_id=1, source_target_pairs={{0,504},{8,16},{16,8},{24,32},{32,24},{40,48},{48,40},{56,64},{64,... | collective-permute-start | bytes 24584 | tf_op jit(solution)/shard_map/ppermute | solution.py:384
  35.0 5.5 %collective-permute-start.1 = (bf16[32,128]{1,0:T(8,128)(2,1)S(1)}, bf16[32,128]{1,0:T(8,128)(2,1)S(1)}, u32[]{:S(2)}, u32[]{:S(2)}) collective-permute-start(bf16[32,128]{1,0:T(8,128)(2,1)S(1)} %get-tuple-element.25), channel_id=1, source_target_pairs={{0,8},{8,0},{16,24},{24,16},{32,40},{40,32},{48,56},{56,48},{64,72... | collective-permute-start | bytes 24584 | tf_op jit(solution)/shard_map/ppermute | solution.py:385

commit v6 on v5

--- a/solution.py
+++ b/solution.py
@@ -13,7 +13,8 @@
 TILE = 8
 PIECES = 4
 NOTES = 2
-FIRST_NUMBER = 43
+ROWS_FIRST = (11, 43)
+SUMS_FIRST = (43, 43)
 PEAK_PARTS = 3
 SIZE_PARTS = 2
 SCORE_SCALE = LANES ** (-0.5) * math.log2(math.e)
@@ -21,14 +22,12 @@
 BF16 = jnp.bfloat16
 
 
-def first_member(shards):
-    return shards * FIRST_NUMBER // 64
-
-
-def exchange(array, shards):
-    first = first_member(shards)
-    members = [(first + at) % shards for at in range(shards)]
-    return lax.all_to_all(array, "ctx", 0, 0, tiled=True, axis_index_groups=[members])
+def exchange(array, shards, groups, firsts):
+    members = []
+    for group in range(groups):
+        first = shards * firsts[group % 2] // 64
+        members.append([(first + at) % shards * groups + group for at in range(shards)])
+    return lax.all_to_all(array, ("ctx", "kv"), 0, 0, tiled=True, axis_index_groups=members)
 
 
 def rows_of(shape):
@@ -84,12 +83,12 @@
         copy.wait()
 
 
-def position(shard, shards):
-    moved = shard - first_member(shards)
+def position(shard, first, shards):
+    moved = shard - first
     return jnp.where(moved < 0, moved + shards, moved)
 
 
-def destination(shards, shard, assignment, row_count):
+def destination(shards, shard, first, assignment, row_count):
     owner = divided(assignment, row_count)
     distance = owner - shard
     distance = jnp.where(distance < 0, distance + shards, distance)
@@ -100,7 +99,7 @@
     earlier = onehot(rows_of((row_count, row_count)) < lanes_of((row_count, row_count)))
     ranks = jnp.dot(flags, earlier, preferred_element_type=F32).astype(jnp.int32)
     rank = jnp.where(ahead, ranks[0:1, :], jnp.where(back, ranks[1:2, :], 0))
-    peer = jnp.where(distance == 0, -1, position(owner, shards))
+    peer = jnp.where(distance == 0, -1, position(owner, first, shards))
     far_peer = jnp.where(ahead | back, -1, peer)
     return peer, far_peer, ahead, back, rank
 
@@ -122,13 +121,13 @@
 
 
 def rows_kernel(
-    shards, shard_ref, assignment_hbm, keys_hbm, values_hbm, far_ref, first_ref, second_ref, peer_ref,
+    shards, shard_ref, begin_ref, assignment_hbm, keys_hbm, values_hbm, far_ref, first_ref, second_ref, peer_ref,
     assignment_ref, keys_ref, values_ref, semaphore,
 ):
     pull((assignment_hbm, keys_hbm, values_hbm), (assignment_ref, keys_ref, values_ref), semaphore)
     row_count = keys_ref.shape[0]
     assignment = assignment_ref[...]
-    peer, far_peer, ahead, back, rank = destination(shards, shard_ref[0], assignment, row_count)
+    peer, far_peer, ahead, back, rank = destination(shards, shard_ref[0], begin_ref[0], assignment, row_count)
     rows = jnp.concatenate([keys_ref[...], values_ref[...]], axis=1)
     is_even = 1 - remainder(shard_ref[0], 2)
     slot = jnp.where(ahead, is_even * NEAR + rank, jnp.where(back, (1 - is_even) * NEAR + rank, -1))
@@ -207,7 +206,7 @@
 
 
 def attend_kernel(
-    shards, shard_ref, sums_ref, total_ref, bias_ref, padded_ref, far_ref, first_ref, second_ref,
+    shards, shard_ref, begin_ref, sums_ref, total_ref, bias_ref, padded_ref, far_ref, first_ref, second_ref,
     merged_keys_ref, merged_values_ref, partial_ref,
 ):
     row_count = sums_ref.shape[0]
@@ -215,9 +214,10 @@
     back = jnp.where(shard == 0, shards - 1, shard - 1)
     ahead = jnp.where(shard == shards - 1, 0, shard + 1)
     is_odd = remainder(shard, 2) == 1
-    shard = position(shard, shards)
-    first_source = position(jnp.where(is_odd, ahead, back), shards)
-    second_source = position(jnp.where(is_odd, back, ahead), shards)
+    first = begin_ref[0]
+    shard = position(shard, first, shards)
+    first_source = position(jnp.where(is_odd, ahead, back), first, shards)
+    second_source = position(jnp.where(is_odd, back, ahead), first, shards)
 
     far = far_ref[...]
     lines = PIECES * shards
@@ -361,6 +361,9 @@
     per_peer = query_rows * heads // shards
     span = per_peer + 2
     shard = lax.axis_index("ctx").astype(jnp.int32).reshape(1)
+    core = lax.axis_index("kv").astype(jnp.int32) % 2
+    begins = [shards * number // 64 for number in ROWS_FIRST]
+    begin = (begins[0] + core * (begins[1] - begins[0])).reshape(1)
     assignment = assignment.reshape(1, row_count)
 
     slices = row_count // LANES
@@ -377,8 +380,8 @@
             ((2 * NEAR, LANES), BF16),
             ((TILE, row_count), jnp.int32),
         ],
-        [SMEM, HBM, HBM, HBM],
-        (shard,) + pulled,
+        [SMEM, SMEM, HBM, HBM, HBM],
+        (shard, begin) + pulled,
         pulled,
     )
     first = lax.ppermute(first, "ctx", [(i, (i - 1 + 2 * (i % 2)) % shards) for i in range(shards)])
@@ -387,7 +390,7 @@
         weigh_kernel, shards, [((PIECES * shards, LANES), BF16)], [VMEM, VMEM, VMEM], (importance, peer, far)
     )
     far, importance = lax.optimization_barrier((far, importance))
-    far = exchange(far.reshape(shards, PIECES, LANES), shards)
+    far = exchange(far.reshape(shards, PIECES, LANES), shards, groups, ROWS_FIRST)
     pulled = (assignment, cache_keys, cache_values, queries)
     sums, total, bias, padded = run_kernel(
         home_kernel,
@@ -406,14 +409,14 @@
         attend_kernel,
         shards,
         [(cache_keys.shape, BF16), (cache_keys.shape, BF16), ((shards * span, LANES), BF16)],
-        [SMEM] + [VMEM] * 7,
-        (shard, sums, total, bias, padded, far.reshape(shards * PIECES, LANES), first, second),
-    )
-    partial = exchange(partial.reshape(shards, span // 2, 2, LANES), shards)
+        [SMEM] * 2 + [VMEM] * 7,
+        (shard, begin, sums, total, bias, padded, far.reshape(shards * PIECES, LANES), first, second),
+    )
+    partial = exchange(partial.reshape(shards, span // 2, 2, LANES), shards, groups, SUMS_FIRST)
     (finished,) = run_kernel(
         combine_kernel, shards, [((shards, per_peer, LANES), BF16)], [VMEM], (partial.reshape(shards * span, LANES),)
     )
-    finished = exchange(finished, shards)
+    finished = exchange(finished, shards, groups, SUMS_FIRST)
     tiles = query_rows // TILE
     attended = finished.reshape(tiles, heads, TILE, head_dim).transpose(0, 2, 1, 3)
     return (merged_keys, merged_values, attended.reshape(query_rows, heads * head_dim))

time: 99.6 us -> 97.7 us (0.981)
  blocking collectives: 53.7 us -> 49.2 us
  starting transfers between devices: 29.9 us -> 31.7 us
    all_to_all x2, blocking collectives: 53.7 us -> 49.2 us  [exchange(): lax.all_to_all(array, ('ctx', 'kv'), 0, 0, tiled=True, axis_index_groups=...]
    ppermute x1, starting transfers between devices: 3.06 us -> 5.17 us  [per_device(): lax.ppermute(second, 'ctx', [(i, (i + 1 - 2 * (i % 2)) % shards) for i in...]
    all_to_all x1, waiting for transfers between devices: 0.01 us -> 1.63 us  [exchange(): lax.all_to_all(array, ('ctx', 'kv'), 0, 0, tiled=True, axis_index_groups=...]
  transfers between devices with their start and end apart: 4 -> 4, of which waited for: 2 -> 3; matrix products, arithmetic and copies ran while one was open for 0% -> 0% of each run, Pallas kernels for 2% -> 2%
where the time goes in v6:
time: 97.7 us; the launch traced here: 97.3 us
  blocking collectives  49.2 us (50%)
  starting transfers between devices  31.7 us (32%)
  Pallas kernels  7.64 us (8%)
  waiting for transfers between devices  4.12 us (4%)
  local copies, waits for them, and re-layouts  3.87 us (4%)
    all_to_all x2, blocking collectives, exchange(): lax.all_to_all(array, ('ctx', 'kv'), 0, 0, tiled=True, axis_index_groups=...  49.2 us
    all_to_all x1, starting transfers between devices, exchange(): lax.all_to_all(array, ('ctx', 'kv'), 0, 0, tiled=True, axis_index_groups=...  19.8 us
    pallas_call x6, Pallas kernels, run_kernel(): pl.pallas_call(functools.partial(body, shards), out_shape=[jax.ShapeDtype...  7.64 us
    ppermute x1, starting transfers between devices, per_device(): lax.ppermute(second, 'ctx', [(i, (i + 1 - 2 * (i % 2)) % shards) for i in...  5.17 us
    all_to_all x1, starting transfers between devices, per_device(): lax.all_to_all(copies.reshape(groups, slices, LANES), 'kv', 0, 0, tiled=T...  4.31 us
    unnamed x15, local copies, waits for them, and re-layouts  3.87 us
    ppermute x1, starting transfers between devices, per_device(): lax.ppermute(first, 'ctx', [(i, (i - 1 + 2 * (i % 2)) % shards) for i in...  2.48 us
  transfers between devices with their start and end apart: 4, of which 3 were waited for; matrix products, arithmetic and copies ran while one was open for 0% of the time, Pallas kernels for 2%

profile of v6, /device:TPU:8, one launch (start us, length us, event | category | flops | bytes accessed | tf_op | source)
XLA Modules:
  0.0 97.3 jit_solution(1433925778084758335)
XLA Ops:
  0.6 0.0 copy-start.6
  0.6 0.7 copy-done.6
  1.3 0.6 shard_map.76
  1.9 4.3 %all-to-all-start = ((bf16[8,4,128]{2,1,0:T(4,128)(2,1)}), bf16[8,4,128]{2,1,0:T(4,128)(2,1)S(1)}, u32[]{:S(2)}, u32[]{:S(2)}) async-start(bf16[8,4,128]{2,1,0:T(4,128)(2,1)} %bitcast.2), calls=%async_computation | async-start | bytes 16384 | tf_op jit(solution)/shard_map/all_to_all | solution.py:372
  6.3 0.0 copy-start.5
  6.3 0.7 copy-done.5
  6.9 0.0 copy-start
  6.9 0.9 copy-done
  7.8 0.0 copy-start.2
  7.8 0.9 copy-done.2
  8.7 0.0 copy-start.4
  8.7 0.9 shard_map.77
  9.6 1.9 %all-to-all-done.importance_ref = bf16[8,4,128]{2,1,0:T(4,128)(2,1)S(1)} async-done(((bf16[8,4,128]{2,1,0:T(4,128)(2,1)}), bf16[8,4,128]{2,1,0:T(4,128)(2,1)S(1)}, u32[]{:S(2)}, u32[]{:S(2)}) %all-to-all-start) | async-done | bytes 8224 | tf_op jit(solution)/shard_map/all_to_all | solution.py:372
  11.6 0.0 copy-start.1
  11.6 0.0 copy-start.3
  11.6 0.9 shard_map.78
  12.4 19.8 %all-to-all-start.1 = ((bf16[64,4,128]{2,1,0:T(4,128)(2,1)}), bf16[64,4,128]{2,1,0:T(4,128)(2,1)S(1)}, u32[]{:S(2)}, u32[]{:S(2)}) async-start(bf16[64,4,128]{2,1,0:T(4,128)(2,1)} %bitcast.4), calls=%async_computation.1 | async-start | bytes 131072 | tf_op jit(solution)/shard_map/all_to_all | solution.py:30
  32.2 2.5 %collective-permute-start = (bf16[32,128]{1,0:T(8,128)(2,1)S(1)}, bf16[32,128]{1,0:T(8,128)(2,1)S(1)}, u32[]{:S(2)}, u32[]{:S(2)}) collective-permute-start(bf16[32,128]{1,0:T(8,128)(2,1)S(1)} %get-tuple-element.24), channel_id=1, source_target_pairs={{0,504},{8,16},{16,8},{24,32},{32,24},{40,48},{48,40},{56,64},{64,... | collective-permute-start | bytes 24584 | tf_op jit(solution)/shard_map/ppermute | solution.py:387
  34.7 5.2 %collective-permute-start.1 = (bf16[32,128]{1,0:T(8,128)(2,1)S(1)}, bf16[32,128]{1,0:T(8,128)(2,1)S(1)}, u32[]{:S(2)}, u32[]{:S(2)}) collective-permute-start(bf16[32,128]{1,0:T(8,128)(2,1)S(1)} %get-tuple-element.25), channel_id=1, source_target_pairs={{0,8},{8,0},{16,24},{24,16},{32,40},{40,32},{48,56},{56,48},{64,72... | collective-permute-start | bytes 24584 | tf_op jit(solution)/shard_map/ppermute | solution.py:388
  39.9 0.0 copy-done.4
  39.9 0.0 copy-done.1
  39.9 0.0 copy-done.3
  39.9 1.0 %shard_map.79 = (f32[512,256]{1,0:T(8,128)S(1)}, f32[512,128]{1,0:T(8,128)S(1)}, f32[8,512]{1,0:T(8,128)S(1)}, bf16[1152,128]{1,0:T(8,128)(2,1)S(1)}) custom-call(s32[1]{0:T(128)} %bitcast.shard_ref, bf16[8,4,128]{2,1,0:T(4,128)(2,1)S(1)} %all-to-all-done.importance_ref, s32[1,512]{1,0:T(1,128)S(1)} %bitcast.17, bf16[512,128]{1,0:T(8,128)(2,1)S(1)} %copy-done.1, ...), custom_call_target="tpu_custom_call" | custom-call | tf_op jit(solution)/shard_map/pallas_call | solution.py:345
  40.9 0.0 collective-permute-done.first_ref
  40.9 0.6 collective-permute-done.1.second_ref
  41.5 1.6 %all-to-all-done.1 = bf16[64,4,128]{2,1,0:T(4,128)(2,1)S(1)} async-done(((bf16[64,4,128]{2,1,0:T(4,128)(2,1)}), bf16[64,4,128]{2,1,0:T(4,128)(2,1)S(1)}, u32[]{:S(2)}, u32[]{:S(2)}) %all-to-all-start.1) | async-done | bytes 65568 | tf_op jit(solution)/shard_map/all_to_all | solution.py:30
  43.1 3.6 %shard_map.80 = (bf16[512,128]{1,0:T(8,128)(2,1)}, bf16[512,128]{1,0:T(8,128)(2,1)}, bf16[1152,128]{1,0:T(8,128)(2,1)S(1)}) custom-call(s32[1]{0:T(128)} %bitcast.shard_ref, s32[1]{0:T(128)} %bitcast.1.begin_ref, f32[512,256]{1,0:T(8,128)S(1)} %get-tuple-element.19.sums_ref, f32[512,128]{1,0:T(8,128)S(1)} %get-tuple-element.20.total_ref, ...), custom_call_target="tpu_custom_call" | custom-call | tf_op jit(solution)/shard_map/pallas_call | solution.py:345
  46.7 26.1 %all_to_all.20 = bf16[64,9,2,128]{3,2,1,0:T(2,128)(2,1)S(1)} all-to-all(bf16[64,9,2,128]{3,2,1,0:T(2,128)(2,1)S(1)} %bitcast.14), channel_id=1, replica_groups={{344,352,360,368,376,384,392,400,408,416,424,432,440,448,456,464,472,48..., dimensions={0} | all-to-all | bytes 589824 | tf_op jit(solution)/shard_map/all_to_all | solution.py:30
  72.8 0.7 shard_map.81
  73.5 23.1 %all_to_all.21 = bf16[64,16,128]{2,1,0:T(8,128)(2,1)S(1)} all-to-all(bf16[64,16,128]{2,1,0:T(8,128)(2,1)S(1)} %shard_map.81), channel_id=1, replica_groups={{344,352,360,368,376,384,392,400,408,416,424,432,440,448,456,464,472,48..., dimensions={0} | all-to-all | bytes 524288 | tf_op jit(solution)/shard_map/all_to_all | solution.py:30
  96.6 0.7 copy.9
Async XLA Ops:
  0.6 0.7 copy-start.6
  1.9 9.6 %all-to-all-start = ((bf16[8,4,128]{2,1,0:T(4,128)(2,1)}), bf16[8,4,128]{2,1,0:T(4,128)(2,1)S(1)}, u32[]{:S(2)}, u32[]{:S(2)}) async-start(bf16[8,4,128]{2,1,0:T(4,128)(2,1)} %bitcast.2), calls=%async_computation | async-start | bytes 16384 | tf_op jit(solution)/shard_map/all_to_all | solution.py:372
  6.3 0.7 copy-start.5
  6.9 0.9 copy-start
  7.8 0.9 copy-start.2
  8.7 31.1 %copy-start.4 = (bf16[128,1024]{1,0:T(8,128)(2,1)S(1)}, bf16[128,1024]{1,0:T(8,128)(2,1)}, u32[]{:S(2)}) copy-start(bf16[128,1024]{1,0:T(8,128)(2,1)} %queries_hbm.1) | copy-start | bytes 786436
  11.6 28.3 %copy-start.1 = (bf16[512,128]{1,0:T(8,128)(2,1)S(1)}, bf16[512,128]{1,0:T(8,128)(2,1)}, u32[]{:S(2)}) copy-start(bf16[512,128]{1,0:T(8,128)(2,1)} %keys_hbm.3) | copy-start | bytes 393220
  11.6 28.3 %copy-start.3 = (bf16[512,128]{1,0:T(8,128)(2,1)S(1)}, bf16[512,128]{1,0:T(8,128)(2,1)}, u32[]{:S(2)}) copy-start(bf16[512,128]{1,0:T(8,128)(2,1)} %values_hbm.3) | copy-start | bytes 393220
  12.4 30.7 %all-to-all-start.1 = ((bf16[64,4,128]{2,1,0:T(4,128)(2,1)}), bf16[64,4,128]{2,1,0:T(4,128)(2,1)S(1)}, u32[]{:S(2)}, u32[]{:S(2)}) async-start(bf16[64,4,128]{2,1,0:T(4,128)(2,1)} %bitcast.4), calls=%async_computation.1 | async-start | bytes 131072 | tf_op jit(solution)/shard_map/all_to_all | solution.py:30
  32.2 8.7 %collective-permute-start = (bf16[32,128]{1,0:T(8,128)(2,1)S(1)}, bf16[32,128]{1,0:T(8,128)(2,1)S(1)}, u32[]{:S(2)}, u32[]{:S(2)}) collective-permute-start(bf16[32,128]{1,0:T(8,128)(2,1)S(1)} %get-tuple-element.24), channel_id=1, source_target_pairs={{0,504},{8,16},{16,8},{24,32},{32,24},{40,48},{48,40},{56,64},{64,... | collective-permute-start | bytes 24584 | tf_op jit(solution)/shard_map/ppermute | solution.py:387
  34.7 6.8 %collective-permute-start.1 = (bf16[32,128]{1,0:T(8,128)(2,1)S(1)}, bf16[32,128]{1,0:T(8,128)(2,1)S(1)}, u32[]{:S(2)}, u32[]{:S(2)}) collective-permute-start(bf16[32,128]{1,0:T(8,128)(2,1)S(1)} %get-tuple-element.25), channel_id=1, source_target_pairs={{0,8},{8,0},{16,24},{24,16},{32,40},{40,32},{48,56},{56,48},{64,72... | collective-permute-start | bytes 24584 | tf_op jit(solution)/shard_map/ppermute | solution.py:388

commit v7 on v6

--- a/solution.py
+++ b/solution.py
@@ -13,8 +13,8 @@
 TILE = 8
 PIECES = 4
 NOTES = 2
-ROWS_FIRST = (11, 43)
-SUMS_FIRST = (43, 43)
+ROWS_FIRST = (11, 47)
+SUMS_FIRST = (47, 47)
 PEAK_PARTS = 3
 SIZE_PARTS = 2
 SCORE_SCALE = LANES ** (-0.5) * math.log2(math.e)
@@ -166,7 +166,7 @@
 
 def home_kernel(
     shards, shard_ref, importance_ref, assignment_hbm, keys_hbm, values_hbm, queries_hbm,
-    sums_ref, total_ref, bias_ref, padded_ref, assignment_ref, keys_ref, values_ref, queries_ref, semaphore,
+    sums_ref, total_ref, bias_ref, padded_ref, kept_rows_ref, assignment_ref, keys_ref, values_ref, queries_ref, semaphore,
 ):
     pull(
         (assignment_hbm, keys_hbm, values_hbm, queries_hbm),
@@ -185,7 +185,14 @@
     rows = jnp.concatenate([keys_ref[...], values_ref[...]], axis=1)
     sums_ref[...] = jnp.dot(mix, rows, preferred_element_type=F32)
     total_ref[...] = jnp.dot(mix, jnp.ones((row_count, LANES), BF16), preferred_element_type=F32)
-    bias_ref[...] = jnp.broadcast_to(jnp.where(kept, 0.0, -jnp.inf), bias_ref.shape)
+    room = kept_rows_ref.shape[0]
+    earlier = onehot(line < lanes_of((row_count, row_count)))
+    kept = kept.astype(F32)
+    rank = jnp.dot(jnp.broadcast_to(kept, (TILE, row_count)).astype(BF16), earlier, preferred_element_type=F32)[0:1, :]
+    rank = jnp.where(kept > 0.0, rank, -1.0).astype(jnp.int32)
+    kept_rows_ref[...] = onehot(rows_of((room, row_count)) == rank)
+    kept_count = jnp.sum(kept, axis=1, keepdims=True)
+    bias_ref[...] = jnp.where(lanes_of(bias_ref.shape).astype(F32) < kept_count, 0.0, -jnp.inf)
 
     query_rows = queries_ref.shape[0]
     heads = queries_ref.shape[1] // head_dim
@@ -206,7 +213,7 @@
 
 
 def attend_kernel(
-    shards, shard_ref, begin_ref, sums_ref, total_ref, bias_ref, padded_ref, far_ref, first_ref, second_ref,
+    shards, shard_ref, begin_ref, sums_ref, total_ref, bias_ref, padded_ref, kept_rows_ref, far_ref, first_ref, second_ref,
     merged_keys_ref, merged_values_ref, partial_ref,
 ):
     row_count = sums_ref.shape[0]
@@ -261,6 +268,10 @@
     merged_values = (sums[:, LANES:] * share).astype(BF16)
     merged_keys_ref[...] = merged_keys
     merged_values_ref[...] = merged_values
+    kept = jnp.dot(
+        kept_rows_ref[...], jnp.concatenate([merged_keys, merged_values], axis=1), preferred_element_type=F32
+    ).astype(BF16)
+    kept_keys, kept_values = kept[:, :LANES], kept[:, LANES:]
 
     span = padded_ref.shape[0] // shards
     per_peer = span - 2
@@ -276,13 +287,13 @@
     starts = range(0, padded_ref.shape[0], group)
     for which, at in enumerate(starts):
         scores = lax.dot_general(
-            padded_ref[at : at + group, :], merged_keys, (((1,), (1,)), ((), ())), preferred_element_type=F32
+            padded_ref[at : at + group, :], kept_keys, (((1,), (1,)), ((), ())), preferred_element_type=F32
         )
         scores = scores + bias
         peak = jnp.max(scores, axis=1, keepdims=True)
         prob = jnp.exp2((scores - peak) * SCORE_SCALE)
         size = jnp.sum(prob, axis=1, keepdims=True)
-        sums = jnp.dot(prob.astype(BF16), merged_values, preferred_element_type=F32)
+        sums = jnp.dot(prob.astype(BF16), kept_values, preferred_element_type=F32)
         peaks = jnp.where(row == which, jnp.sum(jnp.where(diagonal, peak, 0.0), axis=0, keepdims=True), peaks)
         sizes = jnp.where(row == which, jnp.sum(jnp.where(diagonal, size, 0.0), axis=0, keepdims=True), sizes)
         partial_ref[at : at + group, :] = jnp.where(inside, sums, 0.0).astype(BF16)
@@ -392,14 +403,15 @@
     far, importance = lax.optimization_barrier((far, importance))
     far = exchange(far.reshape(shards, PIECES, LANES), shards, groups, ROWS_FIRST)
     pulled = (assignment, cache_keys, cache_values, queries)
-    sums, total, bias, padded = run_kernel(
+    sums, total, bias, padded, kept_rows = run_kernel(
         home_kernel,
         shards,
         [
             ((row_count, 2 * head_dim), F32),
             ((row_count, LANES), F32),
-            ((TILE, row_count), F32),
+            ((TILE, row_count * 3 // 4), F32),
             ((shards * span, head_dim), BF16),
+            ((row_count * 3 // 4, row_count), BF16),
         ],
         [SMEM, VMEM, HBM, HBM, HBM, HBM],
         (shard, importance) + pulled,
@@ -409,8 +421,8 @@
         attend_kernel,
         shards,
         [(cache_keys.shape, BF16), (cache_keys.shape, BF16), ((shards * span, LANES), BF16)],
-        [SMEM] * 2 + [VMEM] * 7,
-        (shard, begin, sums, total, bias, padded, far.reshape(shards * PIECES, LANES), first, second),
+        [SMEM] * 2 + [VMEM] * 8,
+        (shard, begin, sums, total, bias, padded, kept_rows, far.reshape(shards * PIECES, LANES), first, second),
     )
     partial = exchange(partial.reshape(shards, span // 2, 2, LANES), shards, groups, SUMS_FIRST)
     (finished,) = run_kernel(

time: 97.7 us -> 96.8 us (level)
  blocking collectives: 49.2 us -> 48.1 us
    all_to_all x2, blocking collectives: 49.2 us -> 48.1 us  [exchange(): lax.all_to_all(array, ('ctx', 'kv'), 0, 0, tiled=True, axis_index_groups=...]
where the time goes in v7:
time: 96.8 us; the launch traced here: 96.4 us
  blocking collectives  48.1 us (50%)
  starting transfers between devices  31.7 us (33%)
  Pallas kernels  7.68 us (8%)
  waiting for transfers between devices  4.28 us (4%)
  local copies, waits for them, and re-layouts  3.87 us (4%)
    all_to_all x2, blocking collectives, exchange(): lax.all_to_all(array, ('ctx', 'kv'), 0, 0, tiled=True, axis_index_groups=...  48.1 us
    all_to_all x1, starting transfers between devices, exchange(): lax.all_to_all(array, ('ctx', 'kv'), 0, 0, tiled=True, axis_index_groups=...  19.8 us
    pallas_call x6, Pallas kernels, run_kernel(): pl.pallas_call(functools.partial(body, shards), out_shape=[jax.ShapeDtype...  7.68 us
    ppermute x1, starting transfers between devices, per_device(): lax.ppermute(second, 'ctx', [(i, (i + 1 - 2 * (i % 2)) % shards) for i in...  5.17 us
    all_to_all x1, starting transfers between devices, per_device(): lax.all_to_all(copies.reshape(groups, slices, LANES), 'kv', 0, 0, tiled=T...  4.31 us
    unnamed x15, local copies, waits for them, and re-layouts  3.87 us
    ppermute x1, starting transfers between devices, per_device(): lax.ppermute(first, 'ctx', [(i, (i - 1 + 2 * (i % 2)) % shards) for i in...  2.48 us
    all_to_all x1, waiting for transfers between devices, exchange(): lax.all_to_all(array, ('ctx', 'kv'), 0, 0, tiled=True, axis_index_groups=...  1.98 us
  transfers between devices with their start and end apart: 4, of which 3 were waited for; matrix products, arithmetic and copies ran while one was open for 0% of the time, Pallas kernels for 2%

profile of v7, /device:TPU:8, one launch (start us, length us, event | category | flops | bytes accessed | tf_op | source)
XLA Modules:
  0.0 96.4 jit_solution(219950122652871241)
XLA Ops:
  0.6 0.0 copy-start.6
  0.6 0.7 copy-done.6
  1.3 0.6 shard_map.76
  1.9 4.3 %all-to-all-start = ((bf16[8,4,128]{2,1,0:T(4,128)(2,1)}), bf16[8,4,128]{2,1,0:T(4,128)(2,1)S(1)}, u32[]{:S(2)}, u32[]{:S(2)}) async-start(bf16[8,4,128]{2,1,0:T(4,128)(2,1)} %bitcast.2), calls=%async_computation | async-start | bytes 16384 | tf_op jit(solution)/shard_map/all_to_all | solution.py:383
  6.3 0.0 copy-start.5
  6.3 0.7 copy-done.5
  6.9 0.0 copy-start
  6.9 0.9 copy-done
  7.8 0.0 copy-start.2
  7.8 0.9 copy-done.2
  8.7 0.0 copy-start.4
  8.7 0.9 shard_map.77
  9.6 1.9 %all-to-all-done.importance_ref = bf16[8,4,128]{2,1,0:T(4,128)(2,1)S(1)} async-done(((bf16[8,4,128]{2,1,0:T(4,128)(2,1)}), bf16[8,4,128]{2,1,0:T(4,128)(2,1)S(1)}, u32[]{:S(2)}, u32[]{:S(2)}) %all-to-all-start) | async-done | bytes 8224 | tf_op jit(solution)/shard_map/all_to_all | solution.py:383
  11.6 0.0 copy-start.1
  11.6 0.0 copy-start.3
  11.6 0.9 shard_map.78
  12.4 19.8 %all-to-all-start.1 = ((bf16[64,4,128]{2,1,0:T(4,128)(2,1)}), bf16[64,4,128]{2,1,0:T(4,128)(2,1)S(1)}, u32[]{:S(2)}, u32[]{:S(2)}) async-start(bf16[64,4,128]{2,1,0:T(4,128)(2,1)} %bitcast.4), calls=%async_computation.1 | async-start | bytes 131072 | tf_op jit(solution)/shard_map/all_to_all | solution.py:30
  32.2 2.5 %collective-permute-start = (bf16[32,128]{1,0:T(8,128)(2,1)S(1)}, bf16[32,128]{1,0:T(8,128)(2,1)S(1)}, u32[]{:S(2)}, u32[]{:S(2)}) collective-permute-start(bf16[32,128]{1,0:T(8,128)(2,1)S(1)} %get-tuple-element.26), channel_id=1, source_target_pairs={{0,504},{8,16},{16,8},{24,32},{32,24},{40,48},{48,40},{56,64},{64,... | collective-permute-start | bytes 24584 | tf_op jit(solution)/shard_map/ppermute | solution.py:398
  34.7 5.2 %collective-permute-start.1 = (bf16[32,128]{1,0:T(8,128)(2,1)S(1)}, bf16[32,128]{1,0:T(8,128)(2,1)S(1)}, u32[]{:S(2)}, u32[]{:S(2)}) collective-permute-start(bf16[32,128]{1,0:T(8,128)(2,1)S(1)} %get-tuple-element.27), channel_id=1, source_target_pairs={{0,8},{8,0},{16,24},{24,16},{32,40},{40,32},{48,56},{56,48},{64,72... | collective-permute-start | bytes 24584 | tf_op jit(solution)/shard_map/ppermute | solution.py:399
  39.9 0.0 copy-done.4
  39.9 0.0 copy-done.1
  39.9 0.0 copy-done.3
  39.9 1.2 %shard_map.79 = (f32[512,256]{1,0:T(8,128)S(1)}, f32[512,128]{1,0:T(8,128)S(1)}, f32[8,384]{1,0:T(8,128)S(1)}, bf16[1152,128]{1,0:T(8,128)(2,1)S(1)}, bf16[384,512]{1,0:T(8,128)(2,1)S(1)}) custom-call(s32[1]{0:T(128)} %bitcast.shard_ref, bf16[8,4,128]{2,1,0:T(4,128)(2,1)S(1)} %all-to-all-done.importance_ref, s32[1,512]{1,0:T(1,128)S(1)} %bitcast.17, ...), custom_call_target="tpu_custom_call" | custom-call | tf_op jit(solution)/shard_map/pallas_call | solution.py:356
  41.1 0.0 collective-permute-done.first_ref
  41.1 0.4 collective-permute-done.1.second_ref
  41.5 2.0 %all-to-all-done.1 = bf16[64,4,128]{2,1,0:T(4,128)(2,1)S(1)} async-done(((bf16[64,4,128]{2,1,0:T(4,128)(2,1)}), bf16[64,4,128]{2,1,0:T(4,128)(2,1)S(1)}, u32[]{:S(2)}, u32[]{:S(2)}) %all-to-all-start.1) | async-done | bytes 65568 | tf_op jit(solution)/shard_map/all_to_all | solution.py:30
  43.5 3.4 %shard_map.80 = (bf16[512,128]{1,0:T(8,128)(2,1)}, bf16[512,128]{1,0:T(8,128)(2,1)}, bf16[1152,128]{1,0:T(8,128)(2,1)S(1)}) custom-call(s32[1]{0:T(128)} %bitcast.shard_ref, s32[1]{0:T(128)} %bitcast.1.begin_ref, f32[512,256]{1,0:T(8,128)S(1)} %get-tuple-element.20.sums_ref, f32[512,128]{1,0:T(8,128)S(1)} %get-tuple-element.21.total_ref, ...), custom_call_target="tpu_custom_call" | custom-call | tf_op jit(solution)/shard_map/pallas_call | solution.py:356
  46.9 25.0 %all_to_all.20 = bf16[64,9,2,128]{3,2,1,0:T(2,128)(2,1)S(1)} all-to-all(bf16[64,9,2,128]{3,2,1,0:T(2,128)(2,1)S(1)} %bitcast.14), channel_id=1, replica_groups={{376,384,392,400,408,416,424,432,440,448,456,464,472,480,488,496,504,0,..., dimensions={0} | all-to-all | bytes 589824 | tf_op jit(solution)/shard_map/all_to_all | solution.py:30
  71.9 0.7 shard_map.81
  72.6 23.1 %all_to_all.21 = bf16[64,16,128]{2,1,0:T(8,128)(2,1)S(1)} all-to-all(bf16[64,16,128]{2,1,0:T(8,128)(2,1)S(1)} %shard_map.81), channel_id=1, replica_groups={{376,384,392,400,408,416,424,432,440,448,456,464,472,480,488,496,504,0,..., dimensions={0} | all-to-all | bytes 524288 | tf_op jit(solution)/shard_map/all_to_all | solution.py:30
  95.7 0.7 copy.9
Async XLA Ops:
  0.6 0.7 copy-start.6
  1.9 9.6 %all-to-all-start = ((bf16[8,4,128]{2,1,0:T(4,128)(2,1)}), bf16[8,4,128]{2,1,0:T(4,128)(2,1)S(1)}, u32[]{:S(2)}, u32[]{:S(2)}) async-start(bf16[8,4,128]{2,1,0:T(4,128)(2,1)} %bitcast.2), calls=%async_computation | async-start | bytes 16384 | tf_op jit(solution)/shard_map/all_to_all | solution.py:383
  6.3 0.7 copy-start.5
  6.9 0.9 copy-start
  7.8 0.9 copy-start.2
  8.7 31.1 %copy-start.4 = (bf16[128,1024]{1,0:T(8,128)(2,1)S(1)}, bf16[128,1024]{1,0:T(8,128)(2,1)}, u32[]{:S(2)}) copy-start(bf16[128,1024]{1,0:T(8,128)(2,1)} %queries_hbm.1) | copy-start | bytes 786436
  11.6 28.3 %copy-start.1 = (bf16[512,128]{1,0:T(8,128)(2,1)S(1)}, bf16[512,128]{1,0:T(8,128)(2,1)}, u32[]{:S(2)}) copy-start(bf16[512,128]{1,0:T(8,128)(2,1)} %keys_hbm.3) | copy-start | bytes 393220
  11.6 28.3 %copy-start.3 = (bf16[512,128]{1,0:T(8,128)(2,1)S(1)}, bf16[512,128]{1,0:T(8,128)(2,1)}, u32[]{:S(2)}) copy-start(bf16[512,128]{1,0:T(8,128)(2,1)} %values_hbm.3) | copy-start | bytes 393220
  12.4 31.0 %all-to-all-start.1 = ((bf16[64,4,128]{2,1,0:T(4,128)(2,1)}), bf16[64,4,128]{2,1,0:T(4,128)(2,1)S(1)}, u32[]{:S(2)}, u32[]{:S(2)}) async-start(bf16[64,4,128]{2,1,0:T(4,128)(2,1)} %bitcast.4), calls=%async_computation.1 | async-start | bytes 131072 | tf_op jit(solution)/shard_map/all_to_all | solution.py:30
  32.2 8.9 %collective-permute-start = (bf16[32,128]{1,0:T(8,128)(2,1)S(1)}, bf16[32,128]{1,0:T(8,128)(2,1)S(1)}, u32[]{:S(2)}, u32[]{:S(2)}) collective-permute-start(bf16[32,128]{1,0:T(8,128)(2,1)S(1)} %get-tuple-element.26), channel_id=1, source_target_pairs={{0,504},{8,16},{16,8},{24,32},{32,24},{40,48},{48,40},{56,64},{64,... | collective-permute-start | bytes 24584 | tf_op jit(solution)/shard_map/ppermute | solution.py:398
  34.7 6.8 %collective-permute-start.1 = (bf16[32,128]{1,0:T(8,128)(2,1)S(1)}, bf16[32,128]{1,0:T(8,128)(2,1)S(1)}, u32[]{:S(2)}, u32[]{:S(2)}) collective-permute-start(bf16[32,128]{1,0:T(8,128)(2,1)S(1)} %get-tuple-element.27), channel_id=1, source_target_pairs={{0,8},{8,0},{16,24},{24,16},{32,40},{40,32},{48,56},{56,48},{64,72... | collective-permute-start | bytes 24584 | tf_op jit(solution)/shard_map/ppermute | solution.py:399

commit v8 on v7

--- a/solution.py
+++ b/solution.py
@@ -121,7 +121,7 @@
 
 
 def rows_kernel(
-    shards, shard_ref, begin_ref, assignment_hbm, keys_hbm, values_hbm, far_ref, first_ref, second_ref, peer_ref,
+    shards, shard_ref, begin_ref, assignment_hbm, keys_hbm, values_hbm, far_ref, first_ref, second_ref, rank_ref, chosen_ref,
     assignment_ref, keys_ref, values_ref, semaphore,
 ):
     pull((assignment_hbm, keys_hbm, values_hbm), (assignment_ref, keys_ref, values_ref), semaphore)
@@ -149,17 +149,15 @@
     far_ref[...] = jnp.where(
         piece == 0, picked[:, :LANES], jnp.where(piece == 1, picked[:, LANES:], jnp.where(piece == NOTES, noted, 0.0))
     ).astype(BF16)
-    at = rows_of((TILE, row_count))
-    peer_ref[...] = jnp.where(at == 0, peer, jnp.where(at == 1, far_peer, rank))
-
-
-def weigh_kernel(shards, importance_ref, peer_ref, far_ref, out_ref):
-    row_count = peer_ref.shape[1]
+    rank_ref[...] = jnp.broadcast_to(rank, rank_ref.shape)
+    chosen_ref[...] = chosen
+
+
+def weigh_kernel(shards, importance_ref, rank_ref, chosen_ref, far_ref, out_ref):
+    row_count = rank_ref.shape[1]
     weight = row_weight(importance_ref[...])
-    peer, far_peer, rank = peer_ref[0:1, :], peer_ref[1:2, :], peer_ref[2:3, :]
-    chosen = chosen_rows(shards, peer, far_peer, row_count)
-    notes = jnp.where(rows_of((LANES, row_count)) == rank, weight, 0.0).astype(BF16)
-    noted = lax.dot_general(chosen, notes, (((1,), (1,)), ((), ())), preferred_element_type=F32)
+    notes = jnp.where(rows_of((LANES, row_count)) == rank_ref[0:1, :], weight, 0.0).astype(BF16)
+    noted = lax.dot_general(chosen_ref[...], notes, (((1,), (1,)), ((), ())), preferred_element_type=F32)
     piece = remainder(rows_of((PIECES * shards, LANES)), PIECES)
     out_ref[...] = (far_ref[...].astype(F32) + jnp.where(piece == NOTES, noted, 0.0)).astype(BF16)
 
@@ -382,7 +380,7 @@
     (copies,) = run_kernel(copy_kernel, shards, [((groups * slices, LANES), BF16)], [HBM], pulled, pulled)
     importance = lax.all_to_all(copies.reshape(groups, slices, LANES), "kv", 0, 0, tiled=True)
     pulled = (assignment, cache_keys, cache_values)
-    far, first, second, peer = run_kernel(
+    far, first, second, rank, chosen = run_kernel(
         rows_kernel,
         shards,
         [
@@ -390,6 +388,7 @@
             ((2 * NEAR, LANES), BF16),
             ((2 * NEAR, LANES), BF16),
             ((TILE, row_count), jnp.int32),
+            ((PIECES * shards, row_count), BF16),
         ],
         [SMEM, SMEM, HBM, HBM, HBM],
         (shard, begin) + pulled,
@@ -398,7 +397,7 @@
     first = lax.ppermute(first, "ctx", [(i, (i - 1 + 2 * (i % 2)) % shards) for i in range(shards)])
     second = lax.ppermute(second, "ctx", [(i, (i + 1 - 2 * (i % 2)) % shards) for i in range(shards)])
     (far,) = run_kernel(
-        weigh_kernel, shards, [((PIECES * shards, LANES), BF16)], [VMEM, VMEM, VMEM], (importance, peer, far)
+        weigh_kernel, shards, [((PIECES * shards, LANES), BF16)], [VMEM] * 4, (importance, rank, chosen, far)
     )
     far, importance = lax.optimization_barrier((far, importance))
     far = exchange(far.reshape(shards, PIECES, LANES), shards, groups, ROWS_FIRST)

time: 96.8 us -> 96.9 us (level)
  no operation moved by 1% of the time
where the time goes in v8:
time: 96.9 us; the launch traced here: 96.5 us
  blocking collectives  48 us (50%)
  starting transfers between devices  31.9 us (33%)
  Pallas kernels  7.69 us (8%)
  waiting for transfers between devices  4.28 us (4%)
  local copies, waits for them, and re-layouts  3.87 us (4%)
    all_to_all x2, blocking collectives, exchange(): lax.all_to_all(array, ('ctx', 'kv'), 0, 0, tiled=True, axis_index_groups=...  48 us
    all_to_all x1, starting transfers between devices, exchange(): lax.all_to_all(array, ('ctx', 'kv'), 0, 0, tiled=True, axis_index_groups=...  19.9 us
    pallas_call x6, Pallas kernels, run_kernel(): pl.pallas_call(functools.partial(body, shards), out_shape=[jax.ShapeDtype...  7.69 us
    ppermute x1, starting transfers between devices, per_device(): lax.ppermute(second, 'ctx', [(i, (i + 1 - 2 * (i % 2)) % shards) for i in...  5.17 us
    all_to_all x1, starting transfers between devices, per_device(): lax.all_to_all(copies.reshape(groups, slices, LANES), 'kv', 0, 0, tiled=T...  4.31 us
    unnamed x15, local copies, waits for them, and re-layouts  3.87 us
    ppermute x1, starting transfers between devices, per_device(): lax.ppermute(first, 'ctx', [(i, (i - 1 + 2 * (i % 2)) % shards) for i in...  2.48 us
    all_to_all x1, waiting for transfers between devices, exchange(): lax.all_to_all(array, ('ctx', 'kv'), 0, 0, tiled=True, axis_index_groups=...  1.98 us
  transfers between devices with their start and end apart: 4, of which 3 were waited for; matrix products, arithmetic and copies ran while one was open for 0% of the time, Pallas kernels for 2%

profile of v8, /device:TPU:8, one launch (start us, length us, event | category | flops | bytes accessed | tf_op | source)
XLA Modules:
  0.0 96.5 jit_solution(17532083283027092413)
XLA Ops:
  0.6 0.0 copy-start.6
  0.6 0.7 copy-done.6
  1.3 0.6 shard_map.76
  1.9 4.3 %all-to-all-start = ((bf16[8,4,128]{2,1,0:T(4,128)(2,1)}), bf16[8,4,128]{2,1,0:T(4,128)(2,1)S(1)}, u32[]{:S(2)}, u32[]{:S(2)}) async-start(bf16[8,4,128]{2,1,0:T(4,128)(2,1)} %bitcast.2), calls=%async_computation | async-start | bytes 16384 | tf_op jit(solution)/shard_map/all_to_all | solution.py:381
  6.3 0.0 copy-start.5
  6.3 0.7 copy-done.5
  6.9 0.0 copy-start
  6.9 0.9 copy-done
  7.8 0.0 copy-start.2
  7.8 0.9 copy-done.2
  8.7 0.9 shard_map.77
  9.6 1.9 %all-to-all-done.importance_ref = bf16[8,4,128]{2,1,0:T(4,128)(2,1)S(1)} async-done(((bf16[8,4,128]{2,1,0:T(4,128)(2,1)}), bf16[8,4,128]{2,1,0:T(4,128)(2,1)S(1)}, u32[]{:S(2)}, u32[]{:S(2)}) %all-to-all-start) | async-done | bytes 8224 | tf_op jit(solution)/shard_map/all_to_all | solution.py:381
  11.6 0.0 copy-start.3
  11.6 0.0 copy-start.4
  11.6 0.9 shard_map.78
  12.4 0.0 copy-start.1
  12.5 19.9 %all-to-all-start.1 = ((bf16[64,4,128]{2,1,0:T(4,128)(2,1)}), bf16[64,4,128]{2,1,0:T(4,128)(2,1)S(1)}, u32[]{:S(2)}, u32[]{:S(2)}) async-start(bf16[64,4,128]{2,1,0:T(4,128)(2,1)} %bitcast.4), calls=%async_computation.1 | async-start | bytes 131072 | tf_op jit(solution)/shard_map/all_to_all | solution.py:30
  32.4 2.5 %collective-permute-start = (bf16[32,128]{1,0:T(8,128)(2,1)S(1)}, bf16[32,128]{1,0:T(8,128)(2,1)S(1)}, u32[]{:S(2)}, u32[]{:S(2)}) collective-permute-start(bf16[32,128]{1,0:T(8,128)(2,1)S(1)} %get-tuple-element.28), channel_id=1, source_target_pairs={{0,504},{8,16},{16,8},{24,32},{32,24},{40,48},{48,40},{56,64},{64,... | collective-permute-start | bytes 24584 | tf_op jit(solution)/shard_map/ppermute | solution.py:397
  34.9 5.2 %collective-permute-start.1 = (bf16[32,128]{1,0:T(8,128)(2,1)S(1)}, bf16[32,128]{1,0:T(8,128)(2,1)S(1)}, u32[]{:S(2)}, u32[]{:S(2)}) collective-permute-start(bf16[32,128]{1,0:T(8,128)(2,1)S(1)} %get-tuple-element.29), channel_id=1, source_target_pairs={{0,8},{8,0},{16,24},{24,16},{32,40},{40,32},{48,56},{56,48},{64,72... | collective-permute-start | bytes 24584 | tf_op jit(solution)/shard_map/ppermute | solution.py:398
  40.0 0.0 copy-done.3
  40.0 0.0 copy-done.4
  40.0 0.0 copy-done.1
  40.1 1.2 %shard_map.79 = (f32[512,256]{1,0:T(8,128)S(1)}, f32[512,128]{1,0:T(8,128)S(1)}, f32[8,384]{1,0:T(8,128)S(1)}, bf16[1152,128]{1,0:T(8,128)(2,1)S(1)}, bf16[384,512]{1,0:T(8,128)(2,1)S(1)}) custom-call(s32[1]{0:T(128)} %bitcast.shard_ref, bf16[8,4,128]{2,1,0:T(4,128)(2,1)S(1)} %all-to-all-done.importance_ref, s32[1,512]{1,0:T(1,128)S(1)} %bitcast.17, ...), custom_call_target="tpu_custom_call" | custom-call | tf_op jit(solution)/shard_map/pallas_call | solution.py:354
  41.2 0.0 collective-permute-done.first_ref
  41.3 0.4 collective-permute-done.1.second_ref
  41.6 2.0 %all-to-all-done.1 = bf16[64,4,128]{2,1,0:T(4,128)(2,1)S(1)} async-done(((bf16[64,4,128]{2,1,0:T(4,128)(2,1)}), bf16[64,4,128]{2,1,0:T(4,128)(2,1)S(1)}, u32[]{:S(2)}, u32[]{:S(2)}) %all-to-all-start.1) | async-done | bytes 65568 | tf_op jit(solution)/shard_map/all_to_all | solution.py:30
  43.6 3.4 %shard_map.80 = (bf16[512,128]{1,0:T(8,128)(2,1)}, bf16[512,128]{1,0:T(8,128)(2,1)}, bf16[1152,128]{1,0:T(8,128)(2,1)S(1)}) custom-call(s32[1]{0:T(128)} %bitcast.shard_ref, s32[1]{0:T(128)} %bitcast.1.begin_ref, f32[512,256]{1,0:T(8,128)S(1)} %get-tuple-element.22.sums_ref, f32[512,128]{1,0:T(8,128)S(1)} %get-tuple-element.23.total_ref, ...), custom_call_target="tpu_custom_call" | custom-call | tf_op jit(solution)/shard_map/pallas_call | solution.py:354
  47.0 25.0 %all_to_all.20 = bf16[64,9,2,128]{3,2,1,0:T(2,128)(2,1)S(1)} all-to-all(bf16[64,9,2,128]{3,2,1,0:T(2,128)(2,1)S(1)} %bitcast.14), channel_id=1, replica_groups={{376,384,392,400,408,416,424,432,440,448,456,464,472,480,488,496,504,0,..., dimensions={0} | all-to-all | bytes 589824 | tf_op jit(solution)/shard_map/all_to_all | solution.py:30
  72.1 0.7 shard_map.81
  72.7 23.0 %all_to_all.21 = bf16[64,16,128]{2,1,0:T(8,128)(2,1)S(1)} all-to-all(bf16[64,16,128]{2,1,0:T(8,128)(2,1)S(1)} %shard_map.81), channel_id=1, replica_groups={{376,384,392,400,408,416,424,432,440,448,456,464,472,480,488,496,504,0,..., dimensions={0} | all-to-all | bytes 524288 | tf_op jit(solution)/shard_map/all_to_all | solution.py:30
  95.8 0.7 copy.9
Async XLA Ops:
  0.6 0.7 copy-start.6
  1.9 9.6 %all-to-all-start = ((bf16[8,4,128]{2,1,0:T(4,128)(2,1)}), bf16[8,4,128]{2,1,0:T(4,128)(2,1)S(1)}, u32[]{:S(2)}, u32[]{:S(2)}) async-start(bf16[8,4,128]{2,1,0:T(4,128)(2,1)} %bitcast.2), calls=%async_computation | async-start | bytes 16384 | tf_op jit(solution)/shard_map/all_to_all | solution.py:381
  6.3 0.7 copy-start.5
  6.9 0.9 copy-start
  7.8 0.9 copy-start.2
  11.6 28.5 %copy-start.3 = (bf16[512,128]{1,0:T(8,128)(2,1)S(1)}, bf16[512,128]{1,0:T(8,128)(2,1)}, u32[]{:S(2)}) copy-start(bf16[512,128]{1,0:T(8,128)(2,1)} %values_hbm.3) | copy-start | bytes 393220
  11.6 28.5 %copy-start.4 = (bf16[128,1024]{1,0:T(8,128)(2,1)S(1)}, bf16[128,1024]{1,0:T(8,128)(2,1)}, u32[]{:S(2)}) copy-start(bf16[128,1024]{1,0:T(8,128)(2,1)} %queries_hbm.1) | copy-start | bytes 786436
  12.4 27.6 %copy-start.1 = (bf16[512,128]{1,0:T(8,128)(2,1)S(1)}, bf16[512,128]{1,0:T(8,128)(2,1)}, u32[]{:S(2)}) copy-start(bf16[512,128]{1,0:T(8,128)(2,1)} %keys_hbm.3) | copy-start | bytes 393220
  12.5 31.2 %all-to-all-start.1 = ((bf16[64,4,128]{2,1,0:T(4,128)(2,1)}), bf16[64,4,128]{2,1,0:T(4,128)(2,1)S(1)}, u32[]{:S(2)}, u32[]{:S(2)}) async-start(bf16[64,4,128]{2,1,0:T(4,128)(2,1)} %bitcast.4), calls=%async_computation.1 | async-start | bytes 131072 | tf_op jit(solution)/shard_map/all_to_all | solution.py:30
  32.4 8.9 %collective-permute-start = (bf16[32,128]{1,0:T(8,128)(2,1)S(1)}, bf16[32,128]{1,0:T(8,128)(2,1)S(1)}, u32[]{:S(2)}, u32[]{:S(2)}) collective-permute-start(bf16[32,128]{1,0:T(8,128)(2,1)S(1)} %get-tuple-element.28), channel_id=1, source_target_pairs={{0,504},{8,16},{16,8},{24,32},{32,24},{40,48},{48,40},{56,64},{64,... | collective-permute-start | bytes 24584 | tf_op jit(solution)/shard_map/ppermute | solution.py:397
  34.9 6.8 %collective-permute-start.1 = (bf16[32,128]{1,0:T(8,128)(2,1)S(1)}, bf16[32,128]{1,0:T(8,128)(2,1)S(1)}, u32[]{:S(2)}, u32[]{:S(2)}) collective-permute-start(bf16[32,128]{1,0:T(8,128)(2,1)S(1)} %get-tuple-element.29), channel_id=1, source_target_pairs={{0,8},{8,0},{16,24},{24,16},{32,40},{40,32},{48,56},{56,48},{64,72... | collective-permute-start | bytes 24584 | tf_op jit(solution)/shard_map/ppermute | solution.py:398
